TPU v7x, 32 devices: a whole 2x2x4 slice. The times are simulated.
32 devices in a mesh: pb: 4 (over z), kv: 8 (over y, x, core).
Axes of the slice: x: 2, y: 2, z: 4, core: 2. Of those that a mesh axis runs over, the one named last changes fastest.
Arguments:
- queries: bfloat16 [4096, 1024], P(('pb', 'kv')), may hold values from -6 to 6
- key_rows: bfloat16 [4096, 128], P(('pb', 'kv')), may hold values from -6 to 6
- value_rows: bfloat16 [4096, 128], P(('pb', 'kv')), may hold values from -6 to 6
- out_grad: bfloat16 [4096, 1024], P(('pb', 'kv')), may hold values from -6 to 6
- doc_ids: int32 [32], replicated, may hold values from 0 to 15, never falling along the last dimension, each value on 1 to 8 neighbouring positions
Outputs:
- attended: bfloat16 [4096, 1024], P(('pb', 'kv'))
- query_grad: bfloat16 [4096, 1024], P(('pb', 'kv'))
- key_grad: bfloat16 [4096, 128], P(('pb', 'kv'))
- value_grad: bfloat16 [4096, 128], P(('pb', 'kv'))
Inputs may be any that keep to these rules, and one draw needn't show every extreme that they name: `doc_ids`: ids never fall along the sequence; each document covers 1 to 8 consecutive blocks, and one covers exactly 8.
All inputs are finite; a program needn't handle non-finite values.
Results may differ from a plain program's by a relative error of at most 0.03.
Values may be sent and summed in bfloat16 or wider, within the bound.
No kernel may reach another device: no remote copies, remote signals or barrier semaphores. Data moves between devices by JAX's collectives and lax.ppermute only.
A program may use at most 64 MiB of HBM per device.

v0:
```python
import jax
import jax.numpy as jnp
from jax import lax
from jax.sharding import PartitionSpec as P

HEADS = 8
HEAD_DIM = 128
BLOCK = 128


NEG_FILL = -1e30


def passed_along(block, axis, distance):
    devices = range(lax.axis_size(axis))
    route = [(i - distance, i) for i in devices if i - distance in devices]
    return lax.ppermute(block, axis, route)


def shifted(shard, axis, by):
    length = lax.axis_size(axis)
    return lax.ppermute(shard, axis, [(i, (i + by) % length) for i in range(length)])


def contract_last(left, right):
    return lax.dot_general(
        left, right, (((1,), (1,)), ((), ())), preferred_element_type=jnp.float32
    )


def contract_first(left, right):
    return lax.dot_general(
        left, right, (((0,), (0,)), ((), ())), preferred_element_type=jnp.float32
    )


def tile_mask(doc_ids, query_dev, key_dev, row_count):
    per_dev = row_count // BLOCK
    query_docs = jnp.repeat(
        lax.dynamic_slice_in_dim(doc_ids, query_dev * per_dev, per_dev, 0), BLOCK
    )
    key_docs = jnp.repeat(
        lax.dynamic_slice_in_dim(doc_ids, jnp.maximum(key_dev, 0) * per_dev, per_dev, 0), BLOCK
    )
    local_pos = jnp.arange(row_count, dtype=jnp.int32)
    query_pos = query_dev * row_count + local_pos
    key_pos = key_dev * row_count + local_pos
    allowed = (
        (query_docs[:, None] == key_docs[None, :])
        & (key_pos[None, :] <= query_pos[:, None])
        & (key_dev >= 0)
    )
    return jnp.repeat(allowed, HEADS, axis=0)


def local(queries, key_rows, value_rows, out_grad, doc_ids):
    row_count = queries.shape[0]
    flat_rows = row_count * HEADS
    cycle_len = lax.axis_size("kv")
    column = lax.axis_index("kv")
    query_dev = lax.axis_index("pb") * cycle_len + column
    score_scale = HEAD_DIM ** (-0.5)
    query_flat = queries.reshape(flat_rows, HEAD_DIM)
    grad_flat = out_grad.reshape(flat_rows, HEAD_DIM)
    kv_pair = jnp.stack([key_rows, value_rows])
    offsets = jnp.arange(cycle_len, dtype=jnp.int32)

    def cycle_column(offset):
        return (column - offset) % cycle_len

    def tile_scores(kv_shard, allowed):
        return jnp.where(allowed, contract_last(query_flat, kv_shard[0]) * score_scale, NEG_FILL)

    def absorb(softmax_stats, offset, kv_shard):
        allowed = tile_mask(doc_ids, query_dev, query_dev - offset, row_count)
        running_max, running_sum = softmax_stats
        scores = tile_scores(kv_shard, allowed)
        new_max = jnp.maximum(running_max, jnp.max(scores, axis=1))
        fresh = jnp.sum(jnp.where(allowed, jnp.exp(scores - new_max[:, None]), 0.0), axis=1)
        return (new_max, running_sum * jnp.exp(running_max - new_max) + fresh)

    start_stats = (
        jnp.full((flat_rows,), NEG_FILL, jnp.float32),
        jnp.zeros((flat_rows,), jnp.float32),
    )
    behind = passed_along(kv_pair, "pb", 1)

    def pick_shard(bundles, offset):
        return jnp.where(cycle_column(offset) <= column, bundles[0], bundles[1])

    def forward_turn(running, offset):
        bundles, softmax_stats = running
        kv_shard = pick_shard(bundles, offset)
        softmax_stats = absorb(softmax_stats, offset, kv_shard)
        bundles = shifted(bundles, "kv", 1)
        return ((bundles, softmax_stats), kv_shard)

    final_run, stored = lax.scan(
        forward_turn, (jnp.stack([kv_pair, behind]), start_stats), offsets[:-1]
    )
    bundles, softmax_stats = final_run
    last_shard = pick_shard(bundles, cycle_len - 1)
    softmax_stats = absorb(softmax_stats, cycle_len - 1, last_shard)
    stored = jnp.concatenate([stored, last_shard[None]], axis=0)
    row_max, row_sum = softmax_stats
    log_total = row_max + jnp.log(row_sum)

    def weights_for(scores, allowed):
        return jnp.where(allowed, jnp.exp(scores - log_total[:, None]), 0.0)

    def emit(mixed_rows, inputs):
        offset, kv_shard = inputs
        allowed = tile_mask(doc_ids, query_dev, query_dev - offset, row_count)
        weights = weights_for(tile_scores(kv_shard, allowed), allowed)
        return (
            mixed_rows
            + jnp.dot(
                weights.astype(jnp.bfloat16), kv_shard[1], preferred_element_type=jnp.float32
            ),
            None,
        )

    mixed_rows = lax.scan(emit, jnp.zeros((flat_rows, HEAD_DIM), jnp.float32), (offsets, stored))[0]
    attended = mixed_rows.reshape(row_count, HEADS * HEAD_DIM).astype(jnp.bfloat16)
    delta_rows = jnp.sum(
        grad_flat.astype(jnp.float32) * attended.reshape(flat_rows, HEAD_DIM).astype(jnp.float32),
        axis=1,
    )
    query_zero = jnp.zeros((flat_rows, HEAD_DIM), jnp.float32)

    def contribution(offset, kv_shard):
        allowed = tile_mask(doc_ids, query_dev, query_dev - offset, row_count)
        weights = weights_for(tile_scores(kv_shard, allowed), allowed)
        weights_b = weights.astype(jnp.bfloat16)
        grad_probs = contract_last(grad_flat, kv_shard[1])
        score_grad = (score_scale * weights * (grad_probs - delta_rows[:, None])).astype(
            jnp.bfloat16
        )
        query_part = jnp.dot(score_grad, kv_shard[0], preferred_element_type=jnp.float32)
        pair_part = jnp.stack(
            [contract_first(score_grad, query_flat), contract_first(weights_b, grad_flat)]
        )
        return (query_part, pair_part)

    def backward_turn(running, inputs):
        carried, query_acc = running
        query_part, pair_part = contribution(inputs[0], inputs[1])
        own_side = cycle_column(inputs[0]) <= column
        carried = carried + jnp.stack(
            [jnp.where(own_side, pair_part, 0.0), jnp.where(own_side, 0.0, pair_part)]
        )
        carried = shifted(carried, "kv", 1)
        return ((carried, query_acc + query_part), None)

    start_carry = jnp.zeros((2, 2, row_count, HEAD_DIM), jnp.float32)
    carried, query_acc = lax.scan(backward_turn, (start_carry, query_zero), (offsets, stored))[0]
    ahead = passed_along(carried[1], "pb", -1)
    pair_grad = carried[0] + ahead
    query_grad = query_acc.reshape(row_count, HEADS * HEAD_DIM).astype(jnp.bfloat16)
    return (
        attended,
        query_grad,
        pair_grad[0].astype(jnp.bfloat16),
        pair_grad[1].astype(jnp.bfloat16),
    )


def solution(mesh):
    in_specs = (
        P(("pb", "kv"), None),
        P(("pb", "kv"), None),
        P(("pb", "kv"), None),
        P(("pb", "kv"), None),
        P(),
    )
    out_specs = (
        P(("pb", "kv"), None),
        P(("pb", "kv"), None),
        P(("pb", "kv"), None),
        P(("pb", "kv"), None),
    )
    return jax.shard_map(local, mesh=mesh, in_specs=in_specs, out_specs=out_specs, check_vma=False)
```

profile of v0, /device:TPU:0, one launch (start us, length us, event | category | flops | bytes accessed | tf_op | source)
XLA Modules:
  0.0 186.0 jit_solution(8434555674416037715)
XLA Ops:
  0.6 0.8 fusion.37
  1.5 4.9 %collective-permute-start.2 = (bf16[2,128,128]{2,1,0:T(8,128)(2,1)S(1)}, bf16[2,128,128]{2,1,0:T(8,128)(2,1)S(1)}, u32[]{:S(2)}, u32[]{:S(2)}) collective-permute-start(bf16[2,128,128]{2,1,0:T(8,128)(2,1)S(1)} %get-tuple-element.632), channel_id=1, source_target_pairs={{0,8},{8,16},{16,24},{1,9},{9,17},{17,25},{2,10},{10,18},{18,26},{... | collective-permute-start | bytes 196616 | tf_op jit(solution)/shard_map/ppermute | solution.py:17
  6.4 1.4 fusion.39
  9.6 0.8 copy-done.1
  10.8 0.6 copy-done.2
  11.4 39.3 %while.47 = (s32[]{:T(128)}, bf16[2,2,128,128]{3,2,1,0:T(8,128)(2,1)S(1)}, f32[1024]{0:T(1024)S(1)}, f32[1024]{0:T(1024)S(1)}, bf16[7,2,128,128]{3,2,1,0:T(8,128...) while((s32[]{:T(128)}, ...), condition=%wide.region_3.4_spmd.clone, body=%wide.region_0.3_spmd.clone.sunk | while | flops 34428180 | bytes 3135927 | solution.py:98
  13.4 0.6 dynamic_slice.82
  16.8 1.2 collective-permute-start
  28.1 1.2 collective-permute-start
  39.4 1.2 collective-permute-start
  51.3 30.4 %while.48 = (s32[]{:T(128)}, f32[1024,128]{1,0:T(8,128)S(1)}, s32[8]{0:T(128)S(1)}, s32[]{:T(128)}, s32[32]{0:T(128)S(1)}, /*index=5*/s32[1]{0:T(128)}, s32[]{:T...) while((s32[]{:T(128)}, f32[1024,128]{1,0:T(8,128)S(1)}, ...), condition=%wide.region_7.8_spmd.clone, body=%wide.region_6.7_spmd.clone.sunk | while | flops 68075784 | bytes 1417466 | solution.py:123
  81.9 96.6 %while.49 = (s32[]{:T(128)}, f32[2,2,128,128]{3,2,1,0:T(8,128)S(1)}, f32[1024,128]{1,0:T(8,128)S(1)}, s32[8]{0:T(128)S(1)}, s32[]{:T(128)}, /*index=5*/s32[]{:T(...) while((s32[]{:T(128)}, ...), condition=%wide.region_10.11_spmd.clone, body=%wide.region_9.10_spmd.clone.sunk | while | flops 169492736 | bytes 7481830 | solution.py:156
  88.1 5.9 %collective-permute-done.1 = f32[2,2,128,128]{3,2,1,0:T(8,128)S(1)} collective-permute-done((f32[2,2,128,128]{3,2,1,0:T(8,128)S(1)}, f32[2,2,128,128]{3,2,1,0:T(8,128)S(1)}, u32[]{:S(2)}, u32[]{:S(2)}) %collective-permute-start.1) | collective-permute-done | bytes 262176 | tf_op jit(solution)/shard_map/while/body/eval_jaxpr/ppermute | solution.py:22
  99.7 6.4 %collective-permute-done.1 = f32[2,2,128,128]{3,2,1,0:T(8,128)S(1)} collective-permute-done((f32[2,2,128,128]{3,2,1,0:T(8,128)S(1)}, f32[2,2,128,128]{3,2,1,0:T(8,128)S(1)}, u32[]{:S(2)}, u32[]{:S(2)}) %collective-permute-start.1) | collective-permute-done | bytes 262176 | tf_op jit(solution)/shard_map/while/body/eval_jaxpr/ppermute | solution.py:22
  111.7 6.4 %collective-permute-done.1 = f32[2,2,128,128]{3,2,1,0:T(8,128)S(1)} collective-permute-done((f32[2,2,128,128]{3,2,1,0:T(8,128)S(1)}, f32[2,2,128,128]{3,2,1,0:T(8,128)S(1)}, u32[]{:S(2)}, u32[]{:S(2)}) %collective-permute-start.1) | collective-permute-done | bytes 262176 | tf_op jit(solution)/shard_map/while/body/eval_jaxpr/ppermute | solution.py:22
  123.8 6.4 %collective-permute-done.1 = f32[2,2,128,128]{3,2,1,0:T(8,128)S(1)} collective-permute-done((f32[2,2,128,128]{3,2,1,0:T(8,128)S(1)}, f32[2,2,128,128]{3,2,1,0:T(8,128)S(1)}, u32[]{:S(2)}, u32[]{:S(2)}) %collective-permute-start.1) | collective-permute-done | bytes 262176 | tf_op jit(solution)/shard_map/while/body/eval_jaxpr/ppermute | solution.py:22
  135.9 6.4 %collective-permute-done.1 = f32[2,2,128,128]{3,2,1,0:T(8,128)S(1)} collective-permute-done((f32[2,2,128,128]{3,2,1,0:T(8,128)S(1)}, f32[2,2,128,128]{3,2,1,0:T(8,128)S(1)}, u32[]{:S(2)}, u32[]{:S(2)}) %collective-permute-start.1) | collective-permute-done | bytes 262176 | tf_op jit(solution)/shard_map/while/body/eval_jaxpr/ppermute | solution.py:22
  147.9 6.4 %collective-permute-done.1 = f32[2,2,128,128]{3,2,1,0:T(8,128)S(1)} collective-permute-done((f32[2,2,128,128]{3,2,1,0:T(8,128)S(1)}, f32[2,2,128,128]{3,2,1,0:T(8,128)S(1)}, u32[]{:S(2)}, u32[]{:S(2)}) %collective-permute-start.1) | collective-permute-done | bytes 262176 | tf_op jit(solution)/shard_map/while/body/eval_jaxpr/ppermute | solution.py:22
  160.0 6.4 %collective-permute-done.1 = f32[2,2,128,128]{3,2,1,0:T(8,128)S(1)} collective-permute-done((f32[2,2,128,128]{3,2,1,0:T(8,128)S(1)}, f32[2,2,128,128]{3,2,1,0:T(8,128)S(1)}, u32[]{:S(2)}, u32[]{:S(2)}) %collective-permute-start.1) | collective-permute-done | bytes 262176 | tf_op jit(solution)/shard_map/while/body/eval_jaxpr/ppermute | solution.py:22
  172.1 6.4 %collective-permute-done.1 = f32[2,2,128,128]{3,2,1,0:T(8,128)S(1)} collective-permute-done((f32[2,2,128,128]{3,2,1,0:T(8,128)S(1)}, f32[2,2,128,128]{3,2,1,0:T(8,128)S(1)}, u32[]{:S(2)}, u32[]{:S(2)}) %collective-permute-start.1) | collective-permute-done | bytes 262176 | tf_op jit(solution)/shard_map/while/body/eval_jaxpr/ppermute | solution.py:22
  178.5 1.3 collective-permute-start.3
  179.8 0.8 convert_element_type.45
  180.6 0.8 convert_element_type.49
  181.4 3.9 %collective-permute-done.3 = f32[2,128,128]{2,1,0:T(8,128)S(1)} collective-permute-done((f32[2,128,128]{2,1,0:T(8,128)S(1)}, f32[2,128,128]{2,1,0:T(8,128)S(1)}, u32[]{:S(2)}, u32[]{:S(2)}) %collective-permute-start.3) | collective-permute-done | bytes 131104 | tf_op jit(solution)/shard_map/ppermute | solution.py:17
  (292 shorter events, 56.1 us)
Async XLA Ops:
  0.6 8.8 %copy-start = (bf16[128,1024]{1,0:T(8,128)(2,1)S(1)}, bf16[128,1024]{1,0:T(8,128)(2,1)}, u32[]{:S(2)}) copy-start(bf16[128,1024]{1,0:T(8,128)(2,1)} %param.14) | copy-start | bytes 786436
  1.5 9.3 %collective-permute-start.2 = (bf16[2,128,128]{2,1,0:T(8,128)(2,1)S(1)}, bf16[2,128,128]{2,1,0:T(8,128)(2,1)S(1)}, u32[]{:S(2)}, u32[]{:S(2)}) collective-permute-start(bf16[2,128,128]{2,1,0:T(8,128)(2,1)S(1)} %get-tuple-element.632), channel_id=1, source_target_pairs={{0,8},{8,16},{16,24},{1,9},{9,17},{17,25},{2,10},{10,18},{18,26},{... | collective-permute-start | bytes 196616 | tf_op jit(solution)/shard_map/ppermute | solution.py:17
  9.4 1.0 copy-start.1
  10.8 0.7 copy-start.2
  11.4 5.3 %collective-permute-start = (bf16[2,2,128,128]{3,2,1,0:T(8,128)(2,1)S(1)}, bf16[2,2,128,128]{3,2,1,0:T(8,128)(2,1)S(1)}, u32[]{:S(2)}, u32[]{:S(2)}) collective-permute-start(bf16[2,2,128,128]{3,2,1,0:T(8,128)(2,1)S(1)} %copy.26), channel_id=1, source_target_pairs={{0,1},{1,2},{2,3},{3,4},{4,5},{5,6},{6,7},{7,0},{8,9},{9,10},{10,1... | collective-permute-start | bytes 393224 | tf_op jit(solution)/shard_map/while/body/eval_jaxpr/ppermute | solution.py:22
  16.8 5.9 %collective-permute-start = (bf16[2,2,128,128]{3,2,1,0:T(8,128)(2,1)S(1)}, bf16[2,2,128,128]{3,2,1,0:T(8,128)(2,1)S(1)}, u32[]{:S(2)}, u32[]{:S(2)}) collective-permute-start(bf16[2,2,128,128]{3,2,1,0:T(8,128)(2,1)S(1)} %copy.26), channel_id=1, source_target_pairs={{0,1},{1,2},{2,3},{3,4},{4,5},{5,6},{6,7},{7,0},{8,9},{9,10},{10,1... | collective-permute-start | bytes 393224 | tf_op jit(solution)/shard_map/while/body/eval_jaxpr/ppermute | solution.py:22
  22.8 5.3 %collective-permute-start = (bf16[2,2,128,128]{3,2,1,0:T(8,128)(2,1)S(1)}, bf16[2,2,128,128]{3,2,1,0:T(8,128)(2,1)S(1)}, u32[]{:S(2)}, u32[]{:S(2)}) collective-permute-start(bf16[2,2,128,128]{3,2,1,0:T(8,128)(2,1)S(1)} %copy.26), channel_id=1, source_target_pairs={{0,1},{1,2},{2,3},{3,4},{4,5},{5,6},{6,7},{7,0},{8,9},{9,10},{10,1... | collective-permute-start | bytes 393224 | tf_op jit(solution)/shard_map/while/body/eval_jaxpr/ppermute | solution.py:22
  28.1 5.9 %collective-permute-start = (bf16[2,2,128,128]{3,2,1,0:T(8,128)(2,1)S(1)}, bf16[2,2,128,128]{3,2,1,0:T(8,128)(2,1)S(1)}, u32[]{:S(2)}, u32[]{:S(2)}) collective-permute-start(bf16[2,2,128,128]{3,2,1,0:T(8,128)(2,1)S(1)} %copy.26), channel_id=1, source_target_pairs={{0,1},{1,2},{2,3},{3,4},{4,5},{5,6},{6,7},{7,0},{8,9},{9,10},{10,1... | collective-permute-start | bytes 393224 | tf_op jit(solution)/shard_map/while/body/eval_jaxpr/ppermute | solution.py:22
  34.1 5.3 %collective-permute-start = (bf16[2,2,128,128]{3,2,1,0:T(8,128)(2,1)S(1)}, bf16[2,2,128,128]{3,2,1,0:T(8,128)(2,1)S(1)}, u32[]{:S(2)}, u32[]{:S(2)}) collective-permute-start(bf16[2,2,128,128]{3,2,1,0:T(8,128)(2,1)S(1)} %copy.26), channel_id=1, source_target_pairs={{0,1},{1,2},{2,3},{3,4},{4,5},{5,6},{6,7},{7,0},{8,9},{9,10},{10,1... | collective-permute-start | bytes 393224 | tf_op jit(solution)/shard_map/while/body/eval_jaxpr/ppermute | solution.py:22
  39.4 5.9 %collective-permute-start = (bf16[2,2,128,128]{3,2,1,0:T(8,128)(2,1)S(1)}, bf16[2,2,128,128]{3,2,1,0:T(8,128)(2,1)S(1)}, u32[]{:S(2)}, u32[]{:S(2)}) collective-permute-start(bf16[2,2,128,128]{3,2,1,0:T(8,128)(2,1)S(1)} %copy.26), channel_id=1, source_target_pairs={{0,1},{1,2},{2,3},{3,4},{4,5},{5,6},{6,7},{7,0},{8,9},{9,10},{10,1... | collective-permute-start | bytes 393224 | tf_op jit(solution)/shard_map/while/body/eval_jaxpr/ppermute | solution.py:22
  45.4 5.3 %collective-permute-start = (bf16[2,2,128,128]{3,2,1,0:T(8,128)(2,1)S(1)}, bf16[2,2,128,128]{3,2,1,0:T(8,128)(2,1)S(1)}, u32[]{:S(2)}, u32[]{:S(2)}) collective-permute-start(bf16[2,2,128,128]{3,2,1,0:T(8,128)(2,1)S(1)} %copy.26), channel_id=1, source_target_pairs={{0,1},{1,2},{2,3},{3,4},{4,5},{5,6},{6,7},{7,0},{8,9},{9,10},{10,1... | collective-permute-start | bytes 393224 | tf_op jit(solution)/shard_map/while/body/eval_jaxpr/ppermute | solution.py:22
  87.2 6.7 %collective-permute-start.1 = (f32[2,2,128,128]{3,2,1,0:T(8,128)S(1)}, f32[2,2,128,128]{3,2,1,0:T(8,128)S(1)}, u32[]{:S(2)}, u32[]{:S(2)}) collective-permute-start(f32[2,2,128,128]{3,2,1,0:T(8,128)S(1)} %maximum_add_fusion.2), channel_id=1, source_target_pairs={{0,1},{1,2},{2,3},{3,4},{4,5},{5,6},{6,7},{7,0},{8,9},{9,10},{10,1... | collective-permute-start | bytes 786440 | tf_op jit(solution)/shard_map/while/body/eval_jaxpr/ppermute | solution.py:22
  99.3 6.7 %collective-permute-start.1 = (f32[2,2,128,128]{3,2,1,0:T(8,128)S(1)}, f32[2,2,128,128]{3,2,1,0:T(8,128)S(1)}, u32[]{:S(2)}, u32[]{:S(2)}) collective-permute-start(f32[2,2,128,128]{3,2,1,0:T(8,128)S(1)} %maximum_add_fusion.2), channel_id=1, source_target_pairs={{0,1},{1,2},{2,3},{3,4},{4,5},{5,6},{6,7},{7,0},{8,9},{9,10},{10,1... | collective-permute-start | bytes 786440 | tf_op jit(solution)/shard_map/while/body/eval_jaxpr/ppermute | solution.py:22
  111.4 6.7 %collective-permute-start.1 = (f32[2,2,128,128]{3,2,1,0:T(8,128)S(1)}, f32[2,2,128,128]{3,2,1,0:T(8,128)S(1)}, u32[]{:S(2)}, u32[]{:S(2)}) collective-permute-start(f32[2,2,128,128]{3,2,1,0:T(8,128)S(1)} %maximum_add_fusion.2), channel_id=1, source_target_pairs={{0,1},{1,2},{2,3},{3,4},{4,5},{5,6},{6,7},{7,0},{8,9},{9,10},{10,1... | collective-permute-start | bytes 786440 | tf_op jit(solution)/shard_map/while/body/eval_jaxpr/ppermute | solution.py:22
  123.4 6.7 %collective-permute-start.1 = (f32[2,2,128,128]{3,2,1,0:T(8,128)S(1)}, f32[2,2,128,128]{3,2,1,0:T(8,128)S(1)}, u32[]{:S(2)}, u32[]{:S(2)}) collective-permute-start(f32[2,2,128,128]{3,2,1,0:T(8,128)S(1)} %maximum_add_fusion.2), channel_id=1, source_target_pairs={{0,1},{1,2},{2,3},{3,4},{4,5},{5,6},{6,7},{7,0},{8,9},{9,10},{10,1... | collective-permute-start | bytes 786440 | tf_op jit(solution)/shard_map/while/body/eval_jaxpr/ppermute | solution.py:22
  135.5 6.7 %collective-permute-start.1 = (f32[2,2,128,128]{3,2,1,0:T(8,128)S(1)}, f32[2,2,128,128]{3,2,1,0:T(8,128)S(1)}, u32[]{:S(2)}, u32[]{:S(2)}) collective-permute-start(f32[2,2,128,128]{3,2,1,0:T(8,128)S(1)} %maximum_add_fusion.2), channel_id=1, source_target_pairs={{0,1},{1,2},{2,3},{3,4},{4,5},{5,6},{6,7},{7,0},{8,9},{9,10},{10,1... | collective-permute-start | bytes 786440 | tf_op jit(solution)/shard_map/while/body/eval_jaxpr/ppermute | solution.py:22
  147.6 6.7 %collective-permute-start.1 = (f32[2,2,128,128]{3,2,1,0:T(8,128)S(1)}, f32[2,2,128,128]{3,2,1,0:T(8,128)S(1)}, u32[]{:S(2)}, u32[]{:S(2)}) collective-permute-start(f32[2,2,128,128]{3,2,1,0:T(8,128)S(1)} %maximum_add_fusion.2), channel_id=1, source_target_pairs={{0,1},{1,2},{2,3},{3,4},{4,5},{5,6},{6,7},{7,0},{8,9},{9,10},{10,1... | collective-permute-start | bytes 786440 | tf_op jit(solution)/shard_map/while/body/eval_jaxpr/ppermute | solution.py:22
  159.6 6.7 %collective-permute-start.1 = (f32[2,2,128,128]{3,2,1,0:T(8,128)S(1)}, f32[2,2,128,128]{3,2,1,0:T(8,128)S(1)}, u32[]{:S(2)}, u32[]{:S(2)}) collective-permute-start(f32[2,2,128,128]{3,2,1,0:T(8,128)S(1)} %maximum_add_fusion.2), channel_id=1, source_target_pairs={{0,1},{1,2},{2,3},{3,4},{4,5},{5,6},{6,7},{7,0},{8,9},{9,10},{10,1... | collective-permute-start | bytes 786440 | tf_op jit(solution)/shard_map/while/body/eval_jaxpr/ppermute | solution.py:22
  171.7 6.7 %collective-permute-start.1 = (f32[2,2,128,128]{3,2,1,0:T(8,128)S(1)}, f32[2,2,128,128]{3,2,1,0:T(8,128)S(1)}, u32[]{:S(2)}, u32[]{:S(2)}) collective-permute-start(f32[2,2,128,128]{3,2,1,0:T(8,128)S(1)} %maximum_add_fusion.2), channel_id=1, source_target_pairs={{0,1},{1,2},{2,3},{3,4},{4,5},{5,6},{6,7},{7,0},{8,9},{9,10},{10,1... | collective-permute-start | bytes 786440 | tf_op jit(solution)/shard_map/while/body/eval_jaxpr/ppermute | solution.py:22
  178.5 6.9 %collective-permute-start.3 = (f32[2,128,128]{2,1,0:T(8,128)S(1)}, f32[2,128,128]{2,1,0:T(8,128)S(1)}, u32[]{:S(2)}, u32[]{:S(2)}) collective-permute-start(f32[2,128,128]{2,1,0:T(8,128)S(1)} %slice_bitcast_fusion.2), channel_id=1, source_target_pairs={{8,0},{16,8},{24,16},{9,1},{17,9},{25,17},{10,2},{18,10},{26,18},{... | collective-permute-start | bytes 393224 | tf_op jit(solution)/shard_map/ppermute | solution.py:17
where the time goes:
time: 187 us; the launch traced here: 186 us
  loops' own time  57.7 us (31%)
  waiting for transfers between devices  55.4 us (30%)
  local copies, waits for them, and re-layouts  37.2 us (20%)
  matrix products  16.2 us (9%)
  starting transfers between devices  11.9 us (6%)
  other arithmetic  5.38 us (3%)
  between operations  2.25 us (1%)
    ppermute x15, waiting for transfers between devices, shifted(): lax.ppermute(shard, axis, [(i, (i + by) % length) for i in range(length)])  51.5 us
    another operation x1, loops' own time, local(): lax.scan(backward_turn, (start_carry, query_zero), (offsets, stored))[0]  22.1 us
    another operation x1, loops' own time, local(): lax.scan(forward_turn, (jnp.stack([kv_pair, behind]), start_stats), offse...  19.2 us
    another operation x1, loops' own time, local(): lax.scan(emit, jnp.zeros((flat_rows, HEAD_DIM), jnp.float32), (offsets, s...  16.3 us
    dynamic_slice x24, local copies, waits for them, and re-layouts, tile_mask(): lax.dynamic_slice_in_dim(doc_ids, jnp.maximum(key_dev, 0) * per_dev, per_...  15.3 us
    dynamic_slice x16, local copies, waits for them, and re-layouts, local(): lax.scan(emit, jnp.zeros((flat_rows, HEAD_DIM), jnp.float32), (offsets, s...  9.36 us
    dot_general x24, matrix products, contract_last(): lax.dot_general(left, right, (((1,), (1,)), ((), ())), preferred_element_...  6.31 us
    ppermute x2, starting transfers between devices, passed_along(): return lax.ppermute(block, axis, route)  6.22 us
  transfers between devices with their start and end apart: 17, of which 11 were waited for; matrix products, arithmetic and copies ran while one was open for 11% of the time, Pallas kernels for 0%

commit v1 on v0

v1 whole, which is shorter than its diff:
```python
import functools
import math

import jax
import jax.numpy as jnp
from jax import lax
from jax.experimental import pallas as pl
from jax.experimental.pallas import tpu as pltpu
from jax.sharding import PartitionSpec as P

HEADS = 8
HEAD_DIM = 128
BLOCK = 128
AXES = ("pb", "kv")
SCALE = HEAD_DIM ** (-0.5)
SCALE_LOG2 = SCALE / math.log(2.0)
FAR = 1e30
COLS = 256


def dot(left, right, left_dim, right_dim):
    return lax.dot_general(
        left, right, (((left_dim,), (right_dim,)), ((), ())), preferred_element_type=jnp.float32
    )


def attention_kernel(window, refs):
    half = window // 2
    doc_ref, query_ref, grad_ref, own_ref = refs[:4]
    lin_refs = refs[4 : 4 + half - 1]
    sib_refs = refs[4 + half - 1 : 4 + 2 * half - 1]
    sib_own_ref = refs[4 + 2 * half - 1]
    attended_ref, query_grad_ref, kept_ref, lin_out_ref, sib_out_ref = refs[5 + 2 * half - 1 : 10 + 2 * half - 1]
    keys, values, query_rows, grad_rows, weights_s, score_grad_s = refs[10 + 2 * half - 1 :]

    me = lax.axis_index("pb") * lax.axis_size("kv") + lax.axis_index("kv")
    core = lax.rem(me, 2)

    def place(slot, ref):
        keys[slot * BLOCK : (slot + 1) * BLOCK, :] = ref[:BLOCK, :]
        values[slot * BLOCK : (slot + 1) * BLOCK, :] = ref[BLOCK:, :]

    place(0, own_ref)
    for k in range(1, half):
        place(k, lin_refs[k - 1])
        place(half - 1 + k, sib_refs[k - 1])

    @pl.when(core == 0)
    def _():
        place(window - 1, sib_refs[half - 1])

    @pl.when(core == 1)
    def _():
        place(window - 1, sib_own_ref)

    my_doc = doc_ref[me]

    def reach(distance):
        at = me - distance
        return (at >= 0) & (doc_ref[jnp.maximum(at, 0)] == my_doc)

    allowed = [None]
    allowed += [reach(2 * k) for k in range(1, half)]
    allowed += [reach(2 * k - 1 + 2 * core) for k in range(1, half)]
    allowed += [reach(jnp.where(core == 0, window - 1, 1))]

    for h in range(HEADS):
        rows = slice(h * BLOCK, (h + 1) * BLOCK)
        query_rows[rows, :] = query_ref[:, rows]
        grad_rows[rows, :] = grad_ref[:, rows]

    key_row = lax.broadcasted_iota(jnp.int32, (BLOCK, COLS), 0)
    token = lax.broadcasted_iota(jnp.int32, (BLOCK, COLS), 1) % BLOCK
    causal = key_row <= token

    key_all, value_all = keys[...], values[...]
    for tile in range(HEADS * BLOCK // COLS):
        cols = slice(tile * COLS, (tile + 1) * COLS)
        scores = dot(key_all, query_rows[cols, :], 1, 1)
        probs_grad = dot(value_all, grad_rows[cols, :], 1, 1)
        parts = [scores[s * BLOCK : (s + 1) * BLOCK, :] for s in range(window)]
        parts[0] = jnp.where(causal, parts[0], -FAR)
        top = jnp.max(parts[0], axis=0, keepdims=True)
        for s in range(1, window):
            top = jnp.maximum(top, jnp.where(allowed[s], jnp.max(parts[s], axis=0, keepdims=True), -FAR))
        top = top * SCALE_LOG2
        raw, total, mixed = [], 0.0, 0.0
        for s in range(window):
            shift = top if s == 0 else jnp.where(allowed[s], top, FAR)
            e = jnp.exp2(parts[s] * SCALE_LOG2 - shift)
            raw.append(e)
            total = total + jnp.sum(e, axis=0, keepdims=True)
            mixed = mixed + jnp.sum(e * probs_grad[s * BLOCK : (s + 1) * BLOCK, :], axis=0, keepdims=True)
        inverse = 1.0 / total
        delta = mixed * inverse
        for s in range(window):
            rows = slice(s * BLOCK, (s + 1) * BLOCK)
            weights = raw[s] * inverse
            weights_s[rows, cols] = weights.astype(jnp.bfloat16)
            score_grad_s[rows, cols] = (weights * (probs_grad[rows, :] - delta)).astype(jnp.bfloat16)

    attended_t = dot(value_all, weights_s[...], 0, 0)
    query_grad_t = dot(key_all, score_grad_s[...], 0, 0) * SCALE
    for h in range(HEADS):
        rows = slice(h * BLOCK, (h + 1) * BLOCK)
        attended_ref[:, rows] = attended_t[:, rows].T.astype(jnp.bfloat16)
        query_grad_ref[:, rows] = query_grad_t[:, rows].T.astype(jnp.bfloat16)

    key_grad = dot(score_grad_s[...], query_rows[...], 1, 0) * SCALE
    value_grad = dot(weights_s[...], grad_rows[...], 1, 0)

    def hand_out(slot, ref, at):
        rows = slice(slot * BLOCK, (slot + 1) * BLOCK)
        ref[at, :BLOCK, :] = key_grad[rows, :].astype(ref.dtype)
        ref[at, BLOCK:, :] = value_grad[rows, :].astype(ref.dtype)

    hand_out(0, kept_ref, 0)
    for k in range(1, half):
        hand_out(k, lin_out_ref, k - 1)
        hand_out(half - 1 + k, sib_out_ref, k - 1)
    hand_out(window - 1, sib_out_ref, half - 1)


def attention(window, doc_ids, queries, out_grad, own, lins, sibs, sib_own):
    half = window // 2
    rows, width = queries.shape
    flat = HEADS * BLOCK
    vmem = pl.BlockSpec(memory_space=pltpu.VMEM)
    operands = [doc_ids, queries, out_grad, own, *lins, *sibs, sib_own]
    return pl.pallas_call(
        lambda *refs: attention_kernel(window, refs),
        out_shape=[
            jax.ShapeDtypeStruct((rows, width), jnp.bfloat16),
            jax.ShapeDtypeStruct((rows, width), jnp.bfloat16),
            jax.ShapeDtypeStruct((1, 2 * BLOCK, HEAD_DIM), jnp.float32),
            jax.ShapeDtypeStruct((half - 1, 2 * BLOCK, HEAD_DIM), jnp.float32),
            jax.ShapeDtypeStruct((half, 2 * BLOCK, HEAD_DIM), jnp.bfloat16),
        ],
        in_specs=[pl.BlockSpec(memory_space=pltpu.SMEM)] + [vmem] * (len(operands) - 1),
        out_specs=[vmem] * 5,
        scratch_shapes=[
            pltpu.VMEM((window * BLOCK, HEAD_DIM), jnp.bfloat16),
            pltpu.VMEM((window * BLOCK, HEAD_DIM), jnp.bfloat16),
            pltpu.VMEM((flat, HEAD_DIM), jnp.bfloat16),
            pltpu.VMEM((flat, HEAD_DIM), jnp.bfloat16),
            pltpu.VMEM((window * BLOCK, flat), jnp.bfloat16),
            pltpu.VMEM((window * BLOCK, flat), jnp.bfloat16),
        ],
        compiler_params=pltpu.CompilerParams(vmem_limit_bytes=40 * 2**20),
        name="attention",
    )(*operands)


def local(devices, queries, key_rows, value_rows, out_grad, doc_ids):
    window = lax.axis_size("kv")
    half = window // 2

    def ahead(block, k):
        return lax.ppermute(block, AXES, [(i, (i + 2 * k) % devices) for i in range(devices)])

    def swapped(block):
        return lax.ppermute(block, AXES, [(i, i ^ 1) for i in range(devices)])

    own = jnp.concatenate([key_rows, value_rows], axis=0)
    lins = [ahead(own, k) for k in range(1, half + 1)]
    sib_own = swapped(own)
    sibs = [swapped(block) for block in lins]
    attended, query_grad, kept, lin_out, sib_out = attention(
        window, doc_ids, queries, out_grad, own, lins[: half - 1], sibs, sib_own
    )
    from_sib = swapped(sib_out)
    sent = [(lin_out[k] + from_sib[k].astype(jnp.float32)).astype(jnp.bfloat16) for k in range(half - 1)]
    sent.append(from_sib[half - 1])
    back = [ahead(block, -(k + 1)) for k, block in enumerate(sent)]
    core = lax.axis_index("kv") % 2
    total = kept[0]
    for block in back[: half - 1]:
        total = total + block.astype(jnp.float32)
    total = total + jnp.where(core == 0, from_sib[half - 1], back[half - 1]).astype(jnp.float32)
    total = total.astype(jnp.bfloat16)
    return attended, query_grad, total[:BLOCK], total[BLOCK:]


def solution(mesh):
    split = P(AXES, None)
    devices = mesh.shape["pb"] * mesh.shape["kv"]
    return jax.shard_map(
        functools.partial(local, devices),
        mesh=mesh,
        in_specs=(split, split, split, split, P()),
        out_specs=(split, split, split, split),
        check_vma=False,
    )
```

time: 187 us -> 35.2 us (0.19)
  loops' own time: 57.7 us -> 0 us
  waiting for transfers between devices: 55.4 us -> 11.2 us
  local copies, waits for them, and re-layouts: 37.2 us -> 3.32 us
  matrix products: 16.2 us -> 0 us
  Pallas kernels: 0 us -> 5.6 us
  other arithmetic: 5.38 us -> 0.1 us
  starting transfers between devices: 11.9 us -> 14.1 us
    another operation x3 -> x0, loops' own time: 57.7 us -> none  [the longest x1 22.1 us: local(): lax.scan(backward_turn, (start_carry, query_zero), (offsets, stored))[0]]
    ppermute x17 -> x14, waiting for transfers between devices: 55.4 us -> 11.2 us  [the longest x8 8.56 us: ahead(): lax.ppermute(block, AXES, [(i, (i + 2 * k) % devices) for i in range(devi...]
    dynamic_slice x47 -> x0, local copies, waits for them, and re-layouts: 28.7 us -> none  [the longest x24 15.3 us: tile_mask(): lax.dynamic_slice_in_dim(doc_ids, jnp.maximum(key_dev, 0) * per_dev, per_...]
    dot_general x56 -> x0, matrix products: 16.2 us -> none  [the longest x24 6.31 us: contract_last(): lax.dot_general(left, right, (((1,), (1,)), ((), ())), preferred_element_...]
    pallas_call x0 -> x1, Pallas kernels: none -> 5.6 us  [attention(): pl.pallas_call(lambda *refs: attention_kernel(window, refs), out_shape=[j...]
    reshape x34 -> x0, local copies, waits for them, and re-layouts: 4.6 us -> none  [the longest x32 4.37 us: tile_mask(): return jnp.repeat(allowed, HEADS, axis=0)]
    convert_element_type x3 -> x0, local copies, waits for them, and re-layouts: 2.26 us -> none  [the longest x1 0.82 us: local(): mixed_rows.reshape(row_count, HEADS * HEAD_DIM).astype(jnp.bfloat16)]
    ppermute x17 -> x14, starting transfers between devices: 11.9 us -> 14.1 us  [the longest x8 13.7 us: ahead(): lax.ppermute(block, AXES, [(i, (i + 2 * k) % devices) for i in range(devi...]
  transfers between devices with their start and end apart: 17 -> 14, of which waited for: 11 -> 9; matrix products, arithmetic and copies ran while one was open for 11% -> 0% of each run, Pallas kernels for 0% -> 0%
where the time goes in v1:
time: 35.2 us; the launch traced here: 35 us
  starting transfers between devices  14.1 us (40%)
  waiting for transfers between devices  11.2 us (32%)
  Pallas kernels  5.6 us (16%)
  local copies, waits for them, and re-layouts  3.32 us (9%)
  between operations  0.68 us (2%)
    ppermute x8, starting transfers between devices, ahead(): lax.ppermute(block, AXES, [(i, (i + 2 * k) % devices) for i in range(devi...  13.7 us
    ppermute x8, waiting for transfers between devices, ahead(): lax.ppermute(block, AXES, [(i, (i + 2 * k) % devices) for i in range(devi...  8.56 us
    pallas_call x1, Pallas kernels, attention(): pl.pallas_call(lambda *refs: attention_kernel(window, refs), out_shape=[j...  5.6 us
    unnamed x9, local copies, waits for them, and re-layouts  2.67 us
    ppermute x6, waiting for transfers between devices, swapped(): return lax.ppermute(block, AXES, [(i, i ^ 1) for i in range(devices)])  2.61 us
  transfers between devices with their start and end apart: 14, of which 9 were waited for; matrix products, arithmetic and copies ran while one was open for 0% of the time, Pallas kernels for 0%

profile of v1, /device:TPU:0, one launch (start us, length us, event | category | flops | bytes accessed | tf_op | source)
XLA Modules:
  0.0 35.0 jit_solution(7669306790488776406)
XLA Ops:
  0.6 0.8 %constant_dynamic-update-slice_fusion.1 = bf16[256,128]{1,0:T(8,128)(2,1)S(1)} fusion(bf16[128,128]{1,0:T(8,128)(2,1)} %param.6), kind=kLoop, calls=%fused_computation.13 | loop fusion | bytes 65536
  1.4 3.0 %collective-permute-start = (bf16[256,128]{1,0:T(8,128)(2,1)S(1)}, bf16[256,128]{1,0:T(8,128)(2,1)S(1)}, u32[]{:S(2)}, u32[]{:S(2)}) collective-permute-start(bf16[256,128]{1,0:T(8,128)(2,1)S(1)} %constant_dynamic-update-slice_fusion.refs_3_), channel_id=1, source_target_pairs={{0,2},{1,3},{2,4},{3,5},{4,6},{5,7},{6,8},{7,9},{8,10},{9,11},{10,... | collective-permute-start | bytes 196616 | tf_op jit(solution)/shard_map/ppermute | solution.py:159
  4.4 1.5 %collective-permute-start.1 = (bf16[256,128]{1,0:T(8,128)(2,1)S(1)}, bf16[256,128]{1,0:T(8,128)(2,1)S(1)}, u32[]{:S(2)}, u32[]{:S(2)}) collective-permute-start(bf16[256,128]{1,0:T(8,128)(2,1)S(1)} %constant_dynamic-update-slice_fusion.refs_3_), channel_id=1, source_target_pairs={{0,4},{1,5},{2,6},{3,7},{4,8},{5,9},{6,10},{7,11},{8,12},{9,13},{1... | collective-permute-start | bytes 196616 | tf_op jit(solution)/shard_map/ppermute | solution.py:159
  5.9 2.4 %collective-permute-start.2 = (bf16[256,128]{1,0:T(8,128)(2,1)S(1)}, bf16[256,128]{1,0:T(8,128)(2,1)S(1)}, u32[]{:S(2)}, u32[]{:S(2)}) collective-permute-start(bf16[256,128]{1,0:T(8,128)(2,1)S(1)} %constant_dynamic-update-slice_fusion.refs_3_), channel_id=1, source_target_pairs={{0,6},{1,7},{2,8},{3,9},{4,10},{5,11},{6,12},{7,13},{8,14},{9,15},... | collective-permute-start | bytes 196616 | tf_op jit(solution)/shard_map/ppermute | solution.py:159
  8.4 1.6 %collective-permute-start.6 = (bf16[256,128]{1,0:T(8,128)(2,1)S(1)}, bf16[256,128]{1,0:T(8,128)(2,1)S(1)}, u32[]{:S(2)}, u32[]{:S(2)}) collective-permute-start(bf16[256,128]{1,0:T(8,128)(2,1)S(1)} %constant_dynamic-update-slice_fusion.refs_3_), channel_id=1, source_target_pairs={{0,8},{1,9},{2,10},{3,11},{4,12},{5,13},{6,14},{7,15},{8,16},{9,17... | collective-permute-start | bytes 196616 | tf_op jit(solution)/shard_map/ppermute | solution.py:159
  10.0 1.7 %collective-permute-done.refs_4_ = bf16[256,128]{1,0:T(8,128)(2,1)S(1)} collective-permute-done((bf16[256,128]{1,0:T(8,128)(2,1)S(1)}, bf16[256,128]{1,0:T(8,128)(2,1)S(1)}, u32[]{:S(2)}, u32[]{:S(2)}) %collective-permute-start) | collective-permute-done | bytes 65568 | tf_op jit(solution)/shard_map/ppermute | solution.py:159
  11.6 0.3 collective-permute-done.1.refs_5_
  11.9 0.2 collective-permute-start.4
  12.2 1.1 %collective-permute-done.2.refs_6_ = bf16[256,128]{1,0:T(8,128)(2,1)S(1)} collective-permute-done((bf16[256,128]{1,0:T(8,128)(2,1)S(1)}, bf16[256,128]{1,0:T(8,128)(2,1)S(1)}, u32[]{:S(2)}, u32[]{:S(2)}) %collective-permute-start.2) | collective-permute-done | bytes 65568 | tf_op jit(solution)/shard_map/ppermute | solution.py:159
  13.2 1.2 %collective-permute-done.6 = bf16[256,128]{1,0:T(8,128)(2,1)S(1)} collective-permute-done((bf16[256,128]{1,0:T(8,128)(2,1)S(1)}, bf16[256,128]{1,0:T(8,128)(2,1)S(1)}, u32[]{:S(2)}, u32[]{:S(2)}) %collective-permute-start.6) | collective-permute-done | bytes 65568 | tf_op jit(solution)/shard_map/ppermute | solution.py:159
  14.5 1.2 %collective-permute-done.7.refs_10_ = bf16[256,128]{1,0:T(8,128)(2,1)S(1)} collective-permute-done((bf16[256,128]{1,0:T(8,128)(2,1)S(1)}, bf16[256,128]{1,0:T(8,128)(2,1)S(1)}, u32[]{:S(2)}, u32[]{:S(2)}) %collective-permute-start.7) | collective-permute-done | bytes 65568 | tf_op jit(solution)/shard_map/ppermute | solution.py:162
  15.7 0.9 %copy-done = bf16[128,1024]{1,0:T(8,128)(2,1)S(1)} copy-done((bf16[128,1024]{1,0:T(8,128)(2,1)S(1)}, bf16[128,1024]{1,0:T(8,128)(2,1)}, u32[]{:S(2)}) %copy-start) | copy-done | bytes 262168
  16.7 0.9 %copy-done.1 = bf16[128,1024]{1,0:T(8,128)(2,1)S(1)} copy-done((bf16[128,1024]{1,0:T(8,128)(2,1)S(1)}, bf16[128,1024]{1,0:T(8,128)(2,1)}, u32[]{:S(2)}) %copy-start.1) | copy-done | bytes 262168
  17.6 5.6 %attention.1 = (bf16[128,1024]{1,0:T(8,128)(2,1)}, bf16[128,1024]{1,0:T(8,128)(2,1)}, f32[1,256,128]{2,1,0:T(8,128)S(1)}, f32[3,256,128]{2,1,0:T(8,128)S(1)}, bf16[4,256,128]{2,1,0:T(8,128)(2,1)S(1)}) custom-call(s32[32]{0:T(128)S(1)} %copy-done.2, bf16[128,1024]{1,0:T(8,128)(2,1)S(1)} %copy-done, bf16[128,1024]{1,0:T(8,128)(2,1)S(1)} %copy-done.1, ...), custom_call_target="tpu_custom_call" | custom-call | tf_op jit(solution)/shard_map/attention/pallas_call | solution.py:130
  23.2 0.2 collective-permute-start.9
  23.4 1.4 %collective-permute-done.9 = bf16[4,256,128]{2,1,0:T(8,128)(2,1)S(1)} collective-permute-done((bf16[4,256,128]{2,1,0:T(8,128)(2,1)S(1)}, bf16[4,256,128]{2,1,0:T(8,128)(2,1)S(1)}, u32[]{:S(2)}, u32[]{:S(2)}) %collective-permute-start.9) | collective-permute-done | bytes 262176 | tf_op jit(solution)/shard_map/ppermute | solution.py:162
  24.8 2.4 %collective-permute-start.10 = (bf16[256,128]{1,0:T(8,128)(2,1)S(1)}, bf16[256,128]{1,0:T(8,128)(2,1)S(1)}, u32[]{:S(2)}, u32[]{:S(2)}) collective-permute-start(bf16[256,128]{1,0:T(8,128)(2,1)S(1)} %get-tuple-element.14), channel_id=1, source_target_pairs={{0,30},{1,31},{2,0},{3,1},{4,2},{5,3},{6,4},{7,5},{8,6},{9,7},{10,... | collective-permute-start | bytes 196616 | tf_op jit(solution)/shard_map/ppermute | solution.py:159
  27.2 0.6 %collective-permute-start.11 = (bf16[256,128]{1,0:T(8,128)(2,1)S(1)}, bf16[256,128]{1,0:T(8,128)(2,1)S(1)}, u32[]{:S(2)}, u32[]{:S(2)}) collective-permute-start(bf16[256,128]{1,0:T(8,128)(2,1)S(1)} %get-tuple-element.16), channel_id=1, source_target_pairs={{0,28},{1,29},{2,30},{3,31},{4,0},{5,1},{6,2},{7,3},{8,4},{9,5},{1... | collective-permute-start | bytes 196616 | tf_op jit(solution)/shard_map/ppermute | solution.py:159
  27.8 0.8 %collective-permute-start.12 = (bf16[256,128]{1,0:T(8,128)(2,1)S(1)}, bf16[256,128]{1,0:T(8,128)(2,1)S(1)}, u32[]{:S(2)}, u32[]{:S(2)}) collective-permute-start(bf16[256,128]{1,0:T(8,128)(2,1)S(1)} %get-tuple-element.15), channel_id=1, source_target_pairs={{0,26},{1,27},{2,28},{3,29},{4,30},{5,31},{6,0},{7,1},{8,2},{9,3},... | collective-permute-start | bytes 196616 | tf_op jit(solution)/shard_map/ppermute | solution.py:159
  28.6 1.3 %collective-permute-start.13 = (bf16[256,128]{1,0:T(8,128)(2,1)S(1)}, bf16[256,128]{1,0:T(8,128)(2,1)S(1)}, u32[]{:S(2)}, u32[]{:S(2)}) collective-permute-start(bf16[256,128]{1,0:T(8,128)(2,1)S(1)} %slice_bitcast_fusion), channel_id=1, source_target_pairs={{0,24},{1,25},{2,26},{3,27},{4,28},{5,29},{6,30},{7,31},{8,0},{9,1... | collective-permute-start | bytes 196616 | tf_op jit(solution)/shard_map/ppermute | solution.py:159
  30.0 2.2 %collective-permute-done.11 = bf16[256,128]{1,0:T(8,128)(2,1)S(1)} collective-permute-done((bf16[256,128]{1,0:T(8,128)(2,1)S(1)}, bf16[256,128]{1,0:T(8,128)(2,1)S(1)}, u32[]{:S(2)}, u32[]{:S(2)}) %collective-permute-start.11) | collective-permute-done | bytes 65568 | tf_op jit(solution)/shard_map/ppermute | solution.py:159
  32.2 0.8 %collective-permute-done.12 = bf16[256,128]{1,0:T(8,128)(2,1)S(1)} collective-permute-done((bf16[256,128]{1,0:T(8,128)(2,1)S(1)}, bf16[256,128]{1,0:T(8,128)(2,1)S(1)}, u32[]{:S(2)}, u32[]{:S(2)}) %collective-permute-start.12) | collective-permute-done | bytes 65568 | tf_op jit(solution)/shard_map/ppermute | solution.py:159
  33.0 1.3 %collective-permute-done.13 = bf16[256,128]{1,0:T(8,128)(2,1)S(1)} collective-permute-done((bf16[256,128]{1,0:T(8,128)(2,1)S(1)}, bf16[256,128]{1,0:T(8,128)(2,1)S(1)}, u32[]{:S(2)}, u32[]{:S(2)}) %collective-permute-start.13) | collective-permute-done | bytes 65568 | tf_op jit(solution)/shard_map/ppermute | solution.py:159
  34.4 0.6 %fusion.7 = (bf16[128,128]{1,0:T(8,128)(2,1)}, bf16[128,128]{1,0:T(8,128)(2,1)}) fusion(bf16[256,128]{1,0:T(8,128)(2,1)S(1)} %fusion.3), kind=kLoop, calls=%fused_computation.14 | loop fusion | bytes 131072 | tf_op jit(solution)/shard_map/slice | solution.py:181
  (19 shorter events, 0.2 us)
Async XLA Ops:
  0.6 0.8 %copy-start.3 = (bf16[128,128]{1,0:T(8,128)(2,1)S(1)}, bf16[128,128]{1,0:T(8,128)(2,1)}, u32[]{:S(2)}) copy-start(bf16[128,128]{1,0:T(8,128)(2,1)} %param.7) | copy-start | bytes 98308
  1.4 14.3 %copy-start.2 = (s32[32]{0:T(128)S(1)}, s32[32]{0:T(128)}, u32[]{:S(2)}) copy-start(s32[32]{0:T(128)} %refs_0_.1) | copy-start | bytes 388
  1.4 10.2 %collective-permute-start = (bf16[256,128]{1,0:T(8,128)(2,1)S(1)}, bf16[256,128]{1,0:T(8,128)(2,1)S(1)}, u32[]{:S(2)}, u32[]{:S(2)}) collective-permute-start(bf16[256,128]{1,0:T(8,128)(2,1)S(1)} %constant_dynamic-update-slice_fusion.refs_3_), channel_id=1, source_target_pairs={{0,2},{1,3},{2,4},{3,5},{4,6},{5,7},{6,8},{7,9},{8,10},{9,11},{10,... | collective-permute-start | bytes 196616 | tf_op jit(solution)/shard_map/ppermute | solution.py:159
  4.4 7.5 %collective-permute-start.1 = (bf16[256,128]{1,0:T(8,128)(2,1)S(1)}, bf16[256,128]{1,0:T(8,128)(2,1)S(1)}, u32[]{:S(2)}, u32[]{:S(2)}) collective-permute-start(bf16[256,128]{1,0:T(8,128)(2,1)S(1)} %constant_dynamic-update-slice_fusion.refs_3_), channel_id=1, source_target_pairs={{0,4},{1,5},{2,6},{3,7},{4,8},{5,9},{6,10},{7,11},{8,12},{9,13},{1... | collective-permute-start | bytes 196616 | tf_op jit(solution)/shard_map/ppermute | solution.py:159
  5.9 7.3 %collective-permute-start.2 = (bf16[256,128]{1,0:T(8,128)(2,1)S(1)}, bf16[256,128]{1,0:T(8,128)(2,1)S(1)}, u32[]{:S(2)}, u32[]{:S(2)}) collective-permute-start(bf16[256,128]{1,0:T(8,128)(2,1)S(1)} %constant_dynamic-update-slice_fusion.refs_3_), channel_id=1, source_target_pairs={{0,6},{1,7},{2,8},{3,9},{4,10},{5,11},{6,12},{7,13},{8,14},{9,15},... | collective-permute-start | bytes 196616 | tf_op jit(solution)/shard_map/ppermute | solution.py:159
  8.4 6.1 %collective-permute-start.6 = (bf16[256,128]{1,0:T(8,128)(2,1)S(1)}, bf16[256,128]{1,0:T(8,128)(2,1)S(1)}, u32[]{:S(2)}, u32[]{:S(2)}) collective-permute-start(bf16[256,128]{1,0:T(8,128)(2,1)S(1)} %constant_dynamic-update-slice_fusion.refs_3_), channel_id=1, source_target_pairs={{0,8},{1,9},{2,10},{3,11},{4,12},{5,13},{6,14},{7,15},{8,16},{9,17... | collective-permute-start | bytes 196616 | tf_op jit(solution)/shard_map/ppermute | solution.py:159
  10.0 4.5 %collective-permute-start.8 = (bf16[256,128]{1,0:T(8,128)(2,1)S(1)}, bf16[256,128]{1,0:T(8,128)(2,1)S(1)}, u32[]{:S(2)}, u32[]{:S(2)}) collective-permute-start(bf16[256,128]{1,0:T(8,128)(2,1)S(1)} %constant_dynamic-update-slice_fusion.refs_3_), channel_id=1, source_target_pairs={{0,1},{1,0},{2,3},{3,2},{4,5},{5,4},{6,7},{7,6},{8,9},{9,8},{10,11... | collective-permute-start | bytes 196616 | tf_op jit(solution)/shard_map/ppermute | solution.py:162
  11.6 2.8 %collective-permute-start.3 = (bf16[256,128]{1,0:T(8,128)(2,1)S(1)}, bf16[256,128]{1,0:T(8,128)(2,1)S(1)}, u32[]{:S(2)}, u32[]{:S(2)}) collective-permute-start(bf16[256,128]{1,0:T(8,128)(2,1)S(1)} %collective-permute-done.refs_4_), channel_id=1, source_target_pairs={{0,1},{1,0},{2,3},{3,2},{4,5},{5,4},{6,7},{7,6},{8,9},{9,8},{10,11... | collective-permute-start | bytes 196616 | tf_op jit(solution)/shard_map/ppermute | solution.py:162
  11.9 2.6 %collective-permute-start.4 = (bf16[256,128]{1,0:T(8,128)(2,1)S(1)}, bf16[256,128]{1,0:T(8,128)(2,1)S(1)}, u32[]{:S(2)}, u32[]{:S(2)}) collective-permute-start(bf16[256,128]{1,0:T(8,128)(2,1)S(1)} %collective-permute-done.1.refs_5_), channel_id=1, source_target_pairs={{0,1},{1,0},{2,3},{3,2},{4,5},{5,4},{6,7},{7,6},{8,9},{9,8},{10,11... | collective-permute-start | bytes 196616 | tf_op jit(solution)/shard_map/ppermute | solution.py:162
  13.2 1.3 %collective-permute-start.5 = (bf16[256,128]{1,0:T(8,128)(2,1)S(1)}, bf16[256,128]{1,0:T(8,128)(2,1)S(1)}, u32[]{:S(2)}, u32[]{:S(2)}) collective-permute-start(bf16[256,128]{1,0:T(8,128)(2,1)S(1)} %collective-permute-done.2.refs_6_), channel_id=1, source_target_pairs={{0,1},{1,0},{2,3},{3,2},{4,5},{5,4},{6,7},{7,6},{8,9},{9,8},{10,11... | collective-permute-start | bytes 196616 | tf_op jit(solution)/shard_map/ppermute | solution.py:162
  14.4 1.3 %collective-permute-start.7 = (bf16[256,128]{1,0:T(8,128)(2,1)S(1)}, bf16[256,128]{1,0:T(8,128)(2,1)S(1)}, u32[]{:S(2)}, u32[]{:S(2)}) collective-permute-start(bf16[256,128]{1,0:T(8,128)(2,1)S(1)} %collective-permute-done.6), channel_id=1, source_target_pairs={{0,1},{1,0},{2,3},{3,2},{4,5},{5,4},{6,7},{7,6},{8,9},{9,8},{10,11... | collective-permute-start | bytes 196616 | tf_op jit(solution)/shard_map/ppermute | solution.py:162
  15.7 1.0 %copy-start = (bf16[128,1024]{1,0:T(8,128)(2,1)S(1)}, bf16[128,1024]{1,0:T(8,128)(2,1)}, u32[]{:S(2)}) copy-start(bf16[128,1024]{1,0:T(8,128)(2,1)} %refs_1_.1) | copy-start | bytes 786436
  16.7 0.9 %copy-start.1 = (bf16[128,1024]{1,0:T(8,128)(2,1)S(1)}, bf16[128,1024]{1,0:T(8,128)(2,1)}, u32[]{:S(2)}) copy-start(bf16[128,1024]{1,0:T(8,128)(2,1)} %refs_2_.1) | copy-start | bytes 786436
  23.2 1.5 %collective-permute-start.9 = (bf16[4,256,128]{2,1,0:T(8,128)(2,1)S(1)}, bf16[4,256,128]{2,1,0:T(8,128)(2,1)S(1)}, u32[]{:S(2)}, u32[]{:S(2)}) collective-permute-start(bf16[4,256,128]{2,1,0:T(8,128)(2,1)S(1)} %get-tuple-element.13), channel_id=1, source_target_pairs={{0,1},{1,0},{2,3},{3,2},{4,5},{5,4},{6,7},{7,6},{8,9},{9,8},{10,11... | collective-permute-start | bytes 786440 | tf_op jit(solution)/shard_map/ppermute | solution.py:162
  24.8 5.2 %collective-permute-start.10 = (bf16[256,128]{1,0:T(8,128)(2,1)S(1)}, bf16[256,128]{1,0:T(8,128)(2,1)S(1)}, u32[]{:S(2)}, u32[]{:S(2)}) collective-permute-start(bf16[256,128]{1,0:T(8,128)(2,1)S(1)} %get-tuple-element.14), channel_id=1, source_target_pairs={{0,30},{1,31},{2,0},{3,1},{4,2},{5,3},{6,4},{7,5},{8,6},{9,7},{10,... | collective-permute-start | bytes 196616 | tf_op jit(solution)/shard_map/ppermute | solution.py:159
  27.2 5.0 %collective-permute-start.11 = (bf16[256,128]{1,0:T(8,128)(2,1)S(1)}, bf16[256,128]{1,0:T(8,128)(2,1)S(1)}, u32[]{:S(2)}, u32[]{:S(2)}) collective-permute-start(bf16[256,128]{1,0:T(8,128)(2,1)S(1)} %get-tuple-element.16), channel_id=1, source_target_pairs={{0,28},{1,29},{2,30},{3,31},{4,0},{5,1},{6,2},{7,3},{8,4},{9,5},{1... | collective-permute-start | bytes 196616 | tf_op jit(solution)/shard_map/ppermute | solution.py:159
  27.8 5.2 %collective-permute-start.12 = (bf16[256,128]{1,0:T(8,128)(2,1)S(1)}, bf16[256,128]{1,0:T(8,128)(2,1)S(1)}, u32[]{:S(2)}, u32[]{:S(2)}) collective-permute-start(bf16[256,128]{1,0:T(8,128)(2,1)S(1)} %get-tuple-element.15), channel_id=1, source_target_pairs={{0,26},{1,27},{2,28},{3,29},{4,30},{5,31},{6,0},{7,1},{8,2},{9,3},... | collective-permute-start | bytes 196616 | tf_op jit(solution)/shard_map/ppermute | solution.py:159
  28.6 5.7 %collective-permute-start.13 = (bf16[256,128]{1,0:T(8,128)(2,1)S(1)}, bf16[256,128]{1,0:T(8,128)(2,1)S(1)}, u32[]{:S(2)}, u32[]{:S(2)}) collective-permute-start(bf16[256,128]{1,0:T(8,128)(2,1)S(1)} %slice_bitcast_fusion), channel_id=1, source_target_pairs={{0,24},{1,25},{2,26},{3,27},{4,28},{5,29},{6,30},{7,31},{8,0},{9,1... | collective-permute-start | bytes 196616 | tf_op jit(solution)/shard_map/ppermute | solution.py:159

commit v2 on v1

v2 whole, which is shorter than its diff:
```python
import functools
import math

import jax
import jax.numpy as jnp
from jax import lax
from jax.experimental import pallas as pl
from jax.experimental.pallas import tpu as pltpu
from jax.sharding import PartitionSpec as P

HEADS = 8
HEAD_DIM = 128
BLOCK = 128
FLAT = HEADS * BLOCK
AXES = ("pb", "kv")
SCALE = HEAD_DIM ** (-0.5)
SCALE_LOG2 = SCALE / math.log(2.0)
FAR = 1e30
COLS = 256
MIB = 2**20

VMEM = pl.BlockSpec(memory_space=pltpu.VMEM)
SMEM = pl.BlockSpec(memory_space=pltpu.SMEM)
HBM = pl.BlockSpec(memory_space=pltpu.HBM)


def dot(left, right, left_dim, right_dim):
    return lax.dot_general(
        left, right, (((left_dim,), (right_dim,)), ((), ())), preferred_element_type=jnp.float32
    )


class Slots:
    def __init__(self, window):
        self.window = window
        self.half = half = window // 2
        lins = [("lin", k) for k in range(1, half)]
        sibs = [("sib", k) for k in range(1, half)]
        self.early = ["own"] + lins[:-1] + sibs[:-2]
        self.late = [sibs[-2], lins[-1], sibs[-1], "last"]
        self.order = sibs + ["last"] + ["own"] + lins

    def rows(self, slot):
        at = self.order.index(slot) * BLOCK
        return slice(at, at + BLOCK)

    def distance(self, slot, core):
        if slot == "last":
            return jnp.where(core == 0, self.window - 1, 1)
        return 2 * slot[1] if slot[0] == "lin" else 2 * slot[1] - 1 + 2 * core


def position():
    me = lax.axis_index("pb") * lax.axis_size("kv") + lax.axis_index("kv")
    return me, lax.rem(me, 2)


def reached(doc_ref, slots, slot):
    if slot == "own":
        return None
    me, core = position()
    at = me - slots.distance(slot, core)
    return (at >= 0) & (doc_ref[jnp.maximum(at, 0)] == doc_ref[me])


def stacked(refs, part):
    return jnp.concatenate([ref[part * BLOCK : (part + 1) * BLOCK, :] for ref in refs], axis=0)


def tile_of(column):
    return slice(column * COLS, (column + 1) * COLS)


def absorb(parts, probs_grad, allowed, top, total, mixed):
    new_top = top
    for part, ok in zip(parts, allowed):
        peak = jnp.max(part, axis=0, keepdims=True) * SCALE_LOG2
        new_top = jnp.maximum(new_top, peak if ok is None else jnp.where(ok, peak, -FAR))
    rescale = jnp.exp2(top - new_top)
    total, mixed = total * rescale, mixed * rescale
    powers = []
    for s, (part, ok) in enumerate(zip(parts, allowed)):
        shift = new_top if ok is None else jnp.where(ok, new_top, FAR)
        power = jnp.exp2(part * SCALE_LOG2 - shift)
        powers.append(power)
        total = total + jnp.sum(power, axis=0, keepdims=True)
        mixed = mixed + jnp.sum(power * probs_grad[s * BLOCK : (s + 1) * BLOCK, :], axis=0, keepdims=True)
    return powers, new_top, total, mixed, rescale


def early_kernel(slots, *refs):
    count = len(slots.early)
    doc_ref, query_ref, grad_ref = refs[:3]
    blocks = refs[3 : 3 + count]
    query_rows, grad_rows, powers_ref, probs_ref, stats_ref, sems = refs[3 + count :]
    copies = []
    for h in range(HEADS):
        rows = slice(h * BLOCK, (h + 1) * BLOCK)
        copies.append(pltpu.make_async_copy(query_ref.at[:, rows], query_rows.at[rows, :], sems.at[0, h]))
        copies.append(pltpu.make_async_copy(grad_ref.at[:, rows], grad_rows.at[rows, :], sems.at[1, h]))
    for copy in copies:
        copy.start()
    allowed = [reached(doc_ref, slots, slot) for slot in slots.early]
    key_row = lax.broadcasted_iota(jnp.int32, (BLOCK, COLS), 0)
    token = lax.broadcasted_iota(jnp.int32, (BLOCK, COLS), 1) % BLOCK
    causal = key_row <= token
    keys, values = stacked(blocks, 0), stacked(blocks, 1)
    for copy in copies:
        copy.wait()
    stats_ref[...] = jnp.zeros_like(stats_ref)
    for column in range(FLAT // COLS):
        cols = tile_of(column)
        scores = dot(keys, query_rows[cols, :], 1, 1)
        probs_grad = dot(values, grad_rows[cols, :], 1, 1)
        parts = [scores[s * BLOCK : (s + 1) * BLOCK, :] for s in range(count)]
        parts[0] = jnp.where(causal, parts[0], -FAR)
        start = jnp.full((1, COLS), -FAR, jnp.float32), jnp.zeros((1, COLS)), jnp.zeros((1, COLS))
        powers, top, total, mixed, _ = absorb(parts, probs_grad, allowed, *start)
        for s in range(count):
            powers_ref[s * BLOCK : (s + 1) * BLOCK, cols] = powers[s]
        probs_ref[:, cols] = probs_grad
        stats_ref[0:1, cols] = top
        stats_ref[1:2, cols] = total
        stats_ref[2:3, cols] = mixed


def late_kernel(slots, *refs):
    half = slots.half
    doc_ref, query_rows, grad_rows, powers_ref, probs_ref, stats_ref = refs[:6]
    blocks = list(refs[6 : 6 + len(slots.late)])
    sib_own_ref = refs[6 + len(slots.late)]
    weights_ref, score_grad_ref, sib_out_ref, last_ref = refs[7 + len(slots.late) :]
    _, core = position()

    @pl.when(core == 0)
    def _():
        last_ref[...] = blocks[-1][...]

    @pl.when(core == 1)
    def _():
        last_ref[...] = sib_own_ref[...]

    blocks[-1] = last_ref
    allowed = [reached(doc_ref, slots, slot) for slot in slots.late]
    keys, values = stacked(blocks, 0), stacked(blocks, 1)
    for column in range(FLAT // COLS):
        cols = tile_of(column)
        scores = dot(keys, query_rows[cols, :], 1, 1)
        probs_grad = dot(values, grad_rows[cols, :], 1, 1)
        parts = [scores[s * BLOCK : (s + 1) * BLOCK, :] for s in range(len(blocks))]
        start = tuple(stats_ref[row : row + 1, cols] for row in range(3))
        powers, _, total, mixed, rescale = absorb(parts, probs_grad, allowed, *start)
        inverse = 1.0 / total
        delta = mixed * inverse
        early_factor = rescale * inverse

        def put(slot, weights, probs):
            rows = slots.rows(slot)
            weights_ref[rows, cols] = weights.astype(jnp.bfloat16)
            score_grad_ref[rows, cols] = (weights * (probs - delta)).astype(jnp.bfloat16)

        for s, slot in enumerate(slots.early):
            rows = slice(s * BLOCK, (s + 1) * BLOCK)
            put(slot, powers_ref[rows, cols] * early_factor, probs_ref[rows, cols])
        for s, slot in enumerate(slots.late):
            put(slot, powers[s] * inverse, probs_grad[s * BLOCK : (s + 1) * BLOCK, :])

    rows = slice(0, half * BLOCK)
    key_grad = dot(score_grad_ref[rows, :], query_rows[...], 1, 0) * SCALE
    value_grad = dot(weights_ref[rows, :], grad_rows[...], 1, 0)
    for k in range(half):
        rows = slice(k * BLOCK, (k + 1) * BLOCK)
        sib_out_ref[k, :BLOCK, :] = key_grad[rows, :].astype(jnp.bfloat16)
        sib_out_ref[k, BLOCK:, :] = value_grad[rows, :].astype(jnp.bfloat16)


def mine_kernel(slots, weights_ref, score_grad_ref, query_rows, grad_rows, mine_ref):
    half = slots.half
    rows = slice(half * BLOCK, slots.window * BLOCK)
    key_grad = dot(score_grad_ref[rows, :], query_rows[...], 1, 0) * SCALE
    value_grad = dot(weights_ref[rows, :], grad_rows[...], 1, 0)
    for k in range(half):
        rows = slice(k * BLOCK, (k + 1) * BLOCK)
        mine_ref[k, :BLOCK, :] = key_grad[rows, :]
        mine_ref[k, BLOCK:, :] = value_grad[rows, :]


def query_side_kernel(slots, *refs):
    weights_ref, score_grad_ref, sib_own_ref = refs[:3]
    blocks = list(refs[3 : 3 + slots.window])
    attended_ref, query_grad_ref, last_ref = refs[3 + slots.window :]
    _, core = position()
    at = slots.order.index("last")

    @pl.when(core == 0)
    def _():
        last_ref[...] = blocks[at][...]

    @pl.when(core == 1)
    def _():
        last_ref[...] = sib_own_ref[...]

    blocks[at] = last_ref
    attended_t = dot(stacked(blocks, 1), weights_ref[...], 0, 0)
    query_grad_t = dot(stacked(blocks, 0), score_grad_ref[...], 0, 0) * SCALE
    for h in range(HEADS):
        rows = slice(h * BLOCK, (h + 1) * BLOCK)
        attended_ref[:, rows] = attended_t[:, rows].T.astype(jnp.bfloat16)
        query_grad_ref[:, rows] = query_grad_t[:, rows].T.astype(jnp.bfloat16)


def cost(blocks, products):
    flops = 2 * products * blocks * BLOCK * FLAT * HEAD_DIM
    return pl.CostEstimate(flops=flops, bytes_accessed=blocks * BLOCK * FLAT * 4, transcendentals=0)


def local(devices, queries, key_rows, value_rows, out_grad, doc_ids):
    window = lax.axis_size("kv")
    slots = Slots(window)
    half = slots.half
    bf16, f32 = jnp.bfloat16, jnp.float32
    shape = jax.ShapeDtypeStruct
    params = pltpu.CompilerParams(vmem_limit_bytes=3 * window * MIB)

    def ahead(block, k):
        return lax.ppermute(block, AXES, [(i, (i + 2 * k) % devices) for i in range(devices)])

    def swapped(block):
        return lax.ppermute(block, AXES, [(i, i ^ 1) for i in range(devices)])

    own = jnp.concatenate([key_rows, value_rows], axis=0)
    lins = [ahead(own, k) for k in range(1, half + 1)]
    sib_own = swapped(own)
    sibs = [swapped(block) for block in lins]
    held = {"own": own, "last": sibs[-1]}
    for k in range(1, half):
        held["lin", k] = lins[k - 1]
        held["sib", k] = sibs[k - 1]

    early = len(slots.early)
    query_rows, grad_rows, powers, probs_grad, stats = pl.pallas_call(
        functools.partial(early_kernel, slots),
        out_shape=[
            shape((FLAT, HEAD_DIM), bf16),
            shape((FLAT, HEAD_DIM), bf16),
            shape((early * BLOCK, FLAT), f32),
            shape((early * BLOCK, FLAT), f32),
            shape((8, FLAT), f32),
        ],
        in_specs=[SMEM, HBM, HBM] + [VMEM] * early,
        out_specs=[VMEM] * 5,
        scratch_shapes=[pltpu.SemaphoreType.DMA((2, HEADS))],
        compiler_params=params,
        cost_estimate=cost(early, 2),
        name="early_scores",
    )(doc_ids, queries, out_grad, *[held[slot] for slot in slots.early])

    weights, score_grad, sib_out = pl.pallas_call(
        functools.partial(late_kernel, slots),
        out_shape=[
            shape((window * BLOCK, FLAT), bf16),
            shape((window * BLOCK, FLAT), bf16),
            shape((half, 2 * BLOCK, HEAD_DIM), bf16),
        ],
        in_specs=[SMEM] + [VMEM] * (6 + len(slots.late)),
        out_specs=[VMEM] * 3,
        scratch_shapes=[pltpu.VMEM((2 * BLOCK, HEAD_DIM), bf16)],
        compiler_params=params,
        cost_estimate=cost(window, 3),
        name="late_scores",
    )(
        doc_ids, query_rows, grad_rows, powers, probs_grad, stats,
        *[held[slot] for slot in slots.late], sib_own,
    )
    from_sib = swapped(sib_out)

    mine = pl.pallas_call(
        functools.partial(mine_kernel, slots),
        out_shape=shape((half, 2 * BLOCK, HEAD_DIM), f32),
        in_specs=[VMEM] * 4,
        out_specs=VMEM,
        compiler_params=params,
        cost_estimate=cost(half, 2),
        name="own_parity_grads",
    )(weights, score_grad, query_rows, grad_rows)

    attended, query_grad = pl.pallas_call(
        functools.partial(query_side_kernel, slots),
        out_shape=[shape(queries.shape, bf16), shape(queries.shape, bf16)],
        in_specs=[VMEM] * (3 + window),
        out_specs=[VMEM] * 2,
        scratch_shapes=[pltpu.VMEM((2 * BLOCK, HEAD_DIM), bf16)],
        compiler_params=params,
        cost_estimate=cost(window, 2),
        name="query_side",
    )(weights, score_grad, sib_own, *[held[slot] for slot in slots.order])

    sent = [(mine[k] + from_sib[k - 1].astype(f32)).astype(bf16) for k in range(1, half)]
    sent.append(from_sib[half - 1])
    back = [ahead(block, -(k + 1)) for k, block in enumerate(sent)]
    core = lax.axis_index("kv") % 2
    total = mine[0]
    for block in back[: half - 1]:
        total = total + block.astype(f32)
    total = total + jnp.where(core == 0, from_sib[half - 1], back[half - 1]).astype(f32)
    total = total.astype(bf16)
    return attended, query_grad, total[:BLOCK], total[BLOCK:]


def solution(mesh):
    split = P(AXES, None)
    devices = mesh.shape["pb"] * mesh.shape["kv"]
    return jax.shard_map(
        functools.partial(local, devices),
        mesh=mesh,
        in_specs=(split, split, split, split, P()),
        out_specs=(split, split, split, split),
        check_vma=False,
    )
```

time: 35.2 us -> 37 us (1.051)
  waiting for transfers between devices: 11.2 us -> 5.29 us
  local copies, waits for them, and re-layouts: 3.32 us -> 6.94 us
  Pallas kernels: 5.6 us -> 7.36 us
  other arithmetic: 0.1 us -> 1.61 us
  starting transfers between devices: 14.1 us -> 14.7 us
    ppermute x8, waiting for transfers between devices: 8.56 us -> 4.86 us  [ahead(): lax.ppermute(block, AXES, [(i, (i + 2 * k) % devices) for i in range(devi...]
    unnamed x9 -> x11, local copies, waits for them, and re-layouts: 2.67 us -> 4.93 us
    ppermute x6, waiting for transfers between devices: 2.61 us -> 0.43 us  [swapped(): return lax.ppermute(block, AXES, [(i, i ^ 1) for i in range(devices)])]
    pallas_call x1 -> x4, Pallas kernels: 5.6 us -> 7.36 us  [the longest x1 2.94 us: local(): pl.pallas_call(functools.partial(late_kernel, slots), out_shape=[shape((w...]
    convert_element_type x2, other arithmetic: 0.1 us -> 1.61 us  [the longest x1 0.92 us: local(): total = total.astype(bf16)]
    concatenate x1, local copies, waits for them, and re-layouts: 0.01 us -> 0.77 us  [local(): own = jnp.concatenate([key_rows, value_rows], axis=0)]
    ppermute x6, starting transfers between devices: 0.41 us -> 1.09 us  [swapped(): return lax.ppermute(block, AXES, [(i, i ^ 1) for i in range(devices)])]
    squeeze x1, local copies, waits for them, and re-layouts: 0.01 us -> 0.62 us  [local(): from_sib[half - 1]]
  transfers between devices with their start and end apart: 14 -> 14, of which waited for: 9 -> 5; matrix products, arithmetic and copies ran while one was open for 0% -> 2% of each run, Pallas kernels for 0% -> 12%
where the time goes in v2:
time: 37 us; the launch traced here: 36.6 us
  starting transfers between devices  14.7 us (40%)
  Pallas kernels  7.36 us (20%)
  local copies, waits for them, and re-layouts  6.94 us (19%)
  waiting for transfers between devices  5.29 us (14%)
  other arithmetic  1.61 us (4%)
  between operations  0.72 us (2%)
    ppermute x8, starting transfers between devices, ahead(): lax.ppermute(block, AXES, [(i, (i + 2 * k) % devices) for i in range(devi...  13.6 us
    unnamed x11, local copies, waits for them, and re-layouts  4.93 us
    ppermute x8, waiting for transfers between devices, ahead(): lax.ppermute(block, AXES, [(i, (i + 2 * k) % devices) for i in range(devi...  4.86 us
    pallas_call x1, Pallas kernels, local(): pl.pallas_call(functools.partial(late_kernel, slots), out_shape=[shape((w...  2.94 us
    pallas_call x1, Pallas kernels, local(): pl.pallas_call(functools.partial(early_kernel, slots), out_shape=[shape((...  2.06 us
    pallas_call x1, Pallas kernels, local(): pl.pallas_call(functools.partial(query_side_kernel, slots), out_shape=[sh...  1.64 us
    ppermute x6, starting transfers between devices, swapped(): return lax.ppermute(block, AXES, [(i, i ^ 1) for i in range(devices)])  1.09 us
    convert_element_type x1, other arithmetic, local(): total = total.astype(bf16)  0.92 us
  transfers between devices with their start and end apart: 14, of which 5 were waited for; matrix products, arithmetic and copies ran while one was open for 2% of the time, Pallas kernels for 12%

profile of v2, /device:TPU:0, one launch (start us, length us, event | category | flops | bytes accessed | tf_op | source)
XLA Modules:
  0.0 36.6 jit_solution(8972476504042540239)
XLA Ops:
  0.6 0.8 %constant_dynamic-update-slice_fusion.1 = bf16[256,128]{1,0:T(8,128)(2,1)S(1)} fusion(bf16[128,128]{1,0:T(8,128)(2,1)} %param.6), kind=kLoop, calls=%fused_computation.17 | loop fusion | bytes 65536
  1.4 0.8 %constant_dynamic-update-slice_fusion.refs_3_.refs_7_ = bf16[256,128]{1,0:T(8,128)(2,1)S(1)} fusion(bf16[256,128]{1,0:T(8,128)(2,1)S(1)} %constant_dynamic-update-slice_fusion.1, bf16[128,128]{1,0:T(8,128)(2,1)} %param.7), kind=kLoop, calls=%fused_computation.16 | loop fusion | bytes 65536 | tf_op jit(solution)/shard_map/concatenate | solution.py:231
  2.2 2.9 %collective-permute-start = (bf16[256,128]{1,0:T(8,128)(2,1)S(1)}, bf16[256,128]{1,0:T(8,128)(2,1)S(1)}, u32[]{:S(2)}, u32[]{:S(2)}) collective-permute-start(bf16[256,128]{1,0:T(8,128)(2,1)S(1)} %constant_dynamic-update-slice_fusion.refs_3_.refs_7_), channel_id=1, source_target_pairs={{0,2},{1,3},{2,4},{3,5},{4,6},{5,7},{6,8},{7,9},{8,10},{9,11},{10,... | collective-permute-start | bytes 196616 | tf_op jit(solution)/shard_map/ppermute | solution.py:226
  5.1 1.5 %collective-permute-start.1 = (bf16[256,128]{1,0:T(8,128)(2,1)S(1)}, bf16[256,128]{1,0:T(8,128)(2,1)S(1)}, u32[]{:S(2)}, u32[]{:S(2)}) collective-permute-start(bf16[256,128]{1,0:T(8,128)(2,1)S(1)} %constant_dynamic-update-slice_fusion.refs_3_.refs_7_), channel_id=1, source_target_pairs={{0,4},{1,5},{2,6},{3,7},{4,8},{5,9},{6,10},{7,11},{8,12},{9,13},{1... | collective-permute-start | bytes 196616 | tf_op jit(solution)/shard_map/ppermute | solution.py:226
  6.6 2.4 %collective-permute-start.4 = (bf16[256,128]{1,0:T(8,128)(2,1)S(1)}, bf16[256,128]{1,0:T(8,128)(2,1)S(1)}, u32[]{:S(2)}, u32[]{:S(2)}) collective-permute-start(bf16[256,128]{1,0:T(8,128)(2,1)S(1)} %constant_dynamic-update-slice_fusion.refs_3_.refs_7_), channel_id=1, source_target_pairs={{0,6},{1,7},{2,8},{3,9},{4,10},{5,11},{6,12},{7,13},{8,14},{9,15},... | collective-permute-start | bytes 196616 | tf_op jit(solution)/shard_map/ppermute | solution.py:226
  9.1 1.6 %collective-permute-start.6 = (bf16[256,128]{1,0:T(8,128)(2,1)S(1)}, bf16[256,128]{1,0:T(8,128)(2,1)S(1)}, u32[]{:S(2)}, u32[]{:S(2)}) collective-permute-start(bf16[256,128]{1,0:T(8,128)(2,1)S(1)} %constant_dynamic-update-slice_fusion.refs_3_.refs_7_), channel_id=1, source_target_pairs={{0,8},{1,9},{2,10},{3,11},{4,12},{5,13},{6,14},{7,15},{8,16},{9,17... | collective-permute-start | bytes 196616 | tf_op jit(solution)/shard_map/ppermute | solution.py:226
  10.6 1.7 %collective-permute-done.refs_4_.refs_8_ = bf16[256,128]{1,0:T(8,128)(2,1)S(1)} collective-permute-done((bf16[256,128]{1,0:T(8,128)(2,1)S(1)}, bf16[256,128]{1,0:T(8,128)(2,1)S(1)}, u32[]{:S(2)}, u32[]{:S(2)}) %collective-permute-start) | collective-permute-done | bytes 65568 | tf_op jit(solution)/shard_map/ppermute | solution.py:226
  12.8 1.0 %collective-permute-done.4.refs_7_.refs_10_ = bf16[256,128]{1,0:T(8,128)(2,1)S(1)} collective-permute-done((bf16[256,128]{1,0:T(8,128)(2,1)S(1)}, bf16[256,128]{1,0:T(8,128)(2,1)S(1)}, u32[]{:S(2)}, u32[]{:S(2)}) %collective-permute-start.4) | collective-permute-done | bytes 65568 | tf_op jit(solution)/shard_map/ppermute | solution.py:226
  13.9 1.2 %collective-permute-done.6 = bf16[256,128]{1,0:T(8,128)(2,1)S(1)} collective-permute-done((bf16[256,128]{1,0:T(8,128)(2,1)S(1)}, bf16[256,128]{1,0:T(8,128)(2,1)S(1)}, u32[]{:S(2)}, u32[]{:S(2)}) %collective-permute-start.6) | collective-permute-done | bytes 65568 | tf_op jit(solution)/shard_map/ppermute | solution.py:226
  15.1 0.7 %copy-done.2 = s32[32]{0:T(128)S(1)} copy-done((s32[32]{0:T(128)S(1)}, s32[32]{0:T(128)}, u32[]{:S(2)}) %copy-start.2) | copy-done | bytes 152
  15.8 0.9 %copy-done.3 = bf16[128,1024]{1,0:T(8,128)(2,1)S(1)} copy-done((bf16[128,1024]{1,0:T(8,128)(2,1)S(1)}, bf16[128,1024]{1,0:T(8,128)(2,1)}, u32[]{:S(2)}) %copy-start.3) | copy-done | bytes 262168
  16.7 0.9 %copy-done.4 = bf16[128,1024]{1,0:T(8,128)(2,1)S(1)} copy-done((bf16[128,1024]{1,0:T(8,128)(2,1)S(1)}, bf16[128,1024]{1,0:T(8,128)(2,1)}, u32[]{:S(2)}) %copy-start.4) | copy-done | bytes 262168
  17.7 2.1 %early_scores.1 = (bf16[1024,128]{1,0:T(8,128)(2,1)S(1)}, bf16[1024,128]{1,0:T(8,128)(2,1)S(1)}, f32[512,1024]{1,0:T(8,128)S(1)}, f32[512,1024]{1,0:T(8,128)S(1)}, f32[8,1024]{1,0:T(8,128)S(1)}) custom-call(s32[32]{0:T(128)S(1)} %copy-done.2, bf16[128,1024]{1,0:T(8,128)(2,1)S(1)} %copy-done.3, bf16[128,1024]{1,0:T(8,128)(2,1)S(1)} %copy-done.4, ...), custom_call_target="tpu_custom_call" | custom-call | flops 268435456 | bytes 2097152 | tf_op jit(solution)/shard_map/early_scores/pallas_call | solution.py:241
  19.8 2.9 %late_scores.1 = (bf16[1024,1024]{1,0:T(8,128)(2,1)S(1)}, bf16[1024,1024]{1,0:T(8,128)(2,1)S(1)}, bf16[4,256,128]{2,1,0:T(8,128)(2,1)S(1)}) custom-call(s32[32]{0:T(128)S(1)} %copy-done.2, bf16[1024,128]{1,0:T(8,128)(2,1)S(1)} %get-tuple-element.14.refs_1_.query_rows, bf16[1024,128]{1,0:T(8,128)(2,1)S(1)} %get-tuple-element.15.refs_2_.grad_rows, ...), custom_call_target="tpu_custom_call" | custom-call | flops 805306368 | bytes 4194304 | tf_op jit(solution)/shard_map/late_scores/pallas_call | solution.py:258
  23.3 0.7 %own_parity_grads.1 = f32[4,256,128]{2,1,0:T(8,128)S(1)} custom-call(bf16[1024,1024]{1,0:T(8,128)(2,1)S(1)} %get-tuple-element.19.refs_0_.weights_ref, bf16[1024,1024]{1,0:T(8,128)(2,1)S(1)} %get-tuple-element.20.refs_1_.score_grad_ref, bf16[1024,128]{1,0:T(8,128)(2,1)S(1)} %get-tuple-element.14.refs_1_.query_rows, ...), custom_call_target="tpu_custom_call" | custom-call | flops 268435456 | bytes 2097152 | tf_op jit(solution)/shard_map/own_parity_grads/pallas_call | solution.py:277
  24.5 0.7 %fusion.8 = (bf16[256,128]{1,0:T(8,128)(2,1)}, bf16[256,128]{1,0:T(8,128)(2,1)}, bf16[256,128]{1,0:T(8,128)(2,1)}) fusion(f32[4,256,128]{2,1,0:T(8,128)S(1)} %own_parity_grads.1, bf16[4,256,128]{2,1,0:T(8,128)(2,1)S(1)} %collective-permute-done.9), kind=kLoop, calls=%fused_computation.12 | loop fusion | flops 294912 | bytes 786432 | tf_op jit(solution)/shard_map/convert_element_type | solution.py:298
  25.2 2.4 %collective-permute-start.10 = (bf16[256,128]{1,0:T(8,128)(2,1)}, bf16[256,128]{1,0:T(8,128)(2,1)S(1)}, u32[]{:S(2)}, u32[]{:S(2)}) collective-permute-start(bf16[256,128]{1,0:T(8,128)(2,1)} %get-tuple-element.24), channel_id=1, source_target_pairs={{0,30},{1,31},{2,0},{3,1},{4,2},{5,3},{6,4},{7,5},{8,6},{9,7},{10,... | collective-permute-start | bytes 196616 | tf_op jit(solution)/shard_map/ppermute | solution.py:226
  27.6 0.8 %collective-permute-start.11 = (bf16[256,128]{1,0:T(8,128)(2,1)}, bf16[256,128]{1,0:T(8,128)(2,1)}, u32[]{:S(2)}, u32[]{:S(2)}) collective-permute-start(bf16[256,128]{1,0:T(8,128)(2,1)} %get-tuple-element.26), channel_id=1, source_target_pairs={{0,28},{1,29},{2,30},{3,31},{4,0},{5,1},{6,2},{7,3},{8,4},{9,5},{1... | collective-permute-start | bytes 196616 | tf_op jit(solution)/shard_map/ppermute | solution.py:226
  28.4 0.8 %collective-permute-start.12 = (bf16[256,128]{1,0:T(8,128)(2,1)}, bf16[256,128]{1,0:T(8,128)(2,1)}, u32[]{:S(2)}, u32[]{:S(2)}) collective-permute-start(bf16[256,128]{1,0:T(8,128)(2,1)} %get-tuple-element.25), channel_id=1, source_target_pairs={{0,26},{1,27},{2,28},{3,29},{4,30},{5,31},{6,0},{7,1},{8,2},{9,3},... | collective-permute-start | bytes 196616 | tf_op jit(solution)/shard_map/ppermute | solution.py:226
  29.8 1.2 %collective-permute-start.13 = (bf16[256,128]{1,0:T(8,128)(2,1)}, bf16[256,128]{1,0:T(8,128)(2,1)}, u32[]{:S(2)}, u32[]{:S(2)}) collective-permute-start(bf16[256,128]{1,0:T(8,128)(2,1)} %slice_bitcast_fusion.1), channel_id=1, source_target_pairs={{0,24},{1,25},{2,26},{3,27},{4,28},{5,29},{6,30},{7,31},{8,0},{9,1... | collective-permute-start | bytes 196616 | tf_op jit(solution)/shard_map/ppermute | solution.py:226
  31.0 1.6 %copy-done.1 = bf16[1024,1024]{1,0:T(8,128)(2,1)S(1)} copy-done((bf16[1024,1024]{1,0:T(8,128)(2,1)S(1)}, bf16[1024,1024]{1,0:T(8,128)(2,1)}, u32[]{:S(2)}) %copy-start.1) | copy-done | bytes 2097176
  32.5 1.6 %query_side.1 = (bf16[128,1024]{1,0:T(8,128)(2,1)}, bf16[128,1024]{1,0:T(8,128)(2,1)}) custom-call(bf16[1024,1024]{1,0:T(8,128)(2,1)S(1)} %get-tuple-element.19.refs_0_.weights_ref, bf16[1024,1024]{1,0:T(8,128)(2,1)S(1)} %copy-done.1, bf16[256,128]{1,0:T(8,128)(2,1)S(1)} %collective-permute-done.8.refs_10_.refs_2_, ...), custom_call_target="tpu_custom_call" | custom-call | flops 536870912 | bytes 4194304 | tf_op jit(solution)/shard_map/query_side/pallas_call | solution.py:287
  34.2 0.9 %collective-permute-done.13 = bf16[256,128]{1,0:T(8,128)(2,1)} collective-permute-done((bf16[256,128]{1,0:T(8,128)(2,1)}, bf16[256,128]{1,0:T(8,128)(2,1)}, u32[]{:S(2)}, u32[]{:S(2)}) %collective-permute-start.13) | collective-permute-done | bytes 65568 | tf_op jit(solution)/shard_map/ppermute | solution.py:226
  35.1 0.9 %fusion.7 = bf16[256,128]{1,0:T(8,128)(2,1)S(1)} fusion(f32[4,256,128]{2,1,0:T(8,128)S(1)} %own_parity_grads.1, bf16[256,128]{1,0:T(8,128)(2,1)} %collective-permute-done.12, bf16[256,128]{1,0:T(8,128)(2,1)} %collective-permute-done.11, bf16[256,128]{1,0:T(8,128)(2,1)S(1)} %collective-permute-done.10, bf16[256,128]{1,0:T(8,128)(2,1)} %collective-permute-done.13, ...), kind=kLoop, calls=%fused_computation.11 | loop fusion | flops 327680 | bytes 524289 | tf_op jit(solution)/shard_map/convert_element_type | solution.py:306
  (24 shorter events, 2.8 us)
Async XLA Ops:
  2.2 10.2 %collective-permute-start = (bf16[256,128]{1,0:T(8,128)(2,1)S(1)}, bf16[256,128]{1,0:T(8,128)(2,1)S(1)}, u32[]{:S(2)}, u32[]{:S(2)}) collective-permute-start(bf16[256,128]{1,0:T(8,128)(2,1)S(1)} %constant_dynamic-update-slice_fusion.refs_3_.refs_7_), channel_id=1, source_target_pairs={{0,2},{1,3},{2,4},{3,5},{4,6},{5,7},{6,8},{7,9},{8,10},{9,11},{10,... | collective-permute-start | bytes 196616 | tf_op jit(solution)/shard_map/ppermute | solution.py:226
  5.1 7.7 %collective-permute-start.1 = (bf16[256,128]{1,0:T(8,128)(2,1)S(1)}, bf16[256,128]{1,0:T(8,128)(2,1)S(1)}, u32[]{:S(2)}, u32[]{:S(2)}) collective-permute-start(bf16[256,128]{1,0:T(8,128)(2,1)S(1)} %constant_dynamic-update-slice_fusion.refs_3_.refs_7_), channel_id=1, source_target_pairs={{0,4},{1,5},{2,6},{3,7},{4,8},{5,9},{6,10},{7,11},{8,12},{9,13},{1... | collective-permute-start | bytes 196616 | tf_op jit(solution)/shard_map/ppermute | solution.py:226
  6.6 7.3 %collective-permute-start.4 = (bf16[256,128]{1,0:T(8,128)(2,1)S(1)}, bf16[256,128]{1,0:T(8,128)(2,1)S(1)}, u32[]{:S(2)}, u32[]{:S(2)}) collective-permute-start(bf16[256,128]{1,0:T(8,128)(2,1)S(1)} %constant_dynamic-update-slice_fusion.refs_3_.refs_7_), channel_id=1, source_target_pairs={{0,6},{1,7},{2,8},{3,9},{4,10},{5,11},{6,12},{7,13},{8,14},{9,15},... | collective-permute-start | bytes 196616 | tf_op jit(solution)/shard_map/ppermute | solution.py:226
  9.1 6.1 %collective-permute-start.6 = (bf16[256,128]{1,0:T(8,128)(2,1)S(1)}, bf16[256,128]{1,0:T(8,128)(2,1)S(1)}, u32[]{:S(2)}, u32[]{:S(2)}) collective-permute-start(bf16[256,128]{1,0:T(8,128)(2,1)S(1)} %constant_dynamic-update-slice_fusion.refs_3_.refs_7_), channel_id=1, source_target_pairs={{0,8},{1,9},{2,10},{3,11},{4,12},{5,13},{6,14},{7,15},{8,16},{9,17... | collective-permute-start | bytes 196616 | tf_op jit(solution)/shard_map/ppermute | solution.py:226
  12.3 2.8 %collective-permute-start.2 = (bf16[256,128]{1,0:T(8,128)(2,1)S(1)}, bf16[256,128]{1,0:T(8,128)(2,1)S(1)}, u32[]{:S(2)}, u32[]{:S(2)}) collective-permute-start(bf16[256,128]{1,0:T(8,128)(2,1)S(1)} %collective-permute-done.refs_4_.refs_8_), channel_id=1, source_target_pairs={{0,1},{1,0},{2,3},{3,2},{4,5},{5,4},{6,7},{7,6},{8,9},{9,8},{10,11... | collective-permute-start | bytes 196616 | tf_op jit(solution)/shard_map/ppermute | solution.py:229
  12.3 7.4 %collective-permute-start.8 = (bf16[256,128]{1,0:T(8,128)(2,1)S(1)}, bf16[256,128]{1,0:T(8,128)(2,1)S(1)}, u32[]{:S(2)}, u32[]{:S(2)}) collective-permute-start(bf16[256,128]{1,0:T(8,128)(2,1)S(1)} %constant_dynamic-update-slice_fusion.refs_3_.refs_7_), channel_id=1, source_target_pairs={{0,1},{1,0},{2,3},{3,2},{4,5},{5,4},{6,7},{7,6},{8,9},{9,8},{10,11... | collective-permute-start | bytes 196616 | tf_op jit(solution)/shard_map/ppermute | solution.py:229
  12.8 6.9 %collective-permute-start.3 = (bf16[256,128]{1,0:T(8,128)(2,1)S(1)}, bf16[256,128]{1,0:T(8,128)(2,1)S(1)}, u32[]{:S(2)}, u32[]{:S(2)}) collective-permute-start(bf16[256,128]{1,0:T(8,128)(2,1)S(1)} %collective-permute-done.1.refs_5_.refs_9_), channel_id=1, source_target_pairs={{0,1},{1,0},{2,3},{3,2},{4,5},{5,4},{6,7},{7,6},{8,9},{9,8},{10,11... | collective-permute-start | bytes 196616 | tf_op jit(solution)/shard_map/ppermute | solution.py:229
  13.9 5.9 %collective-permute-start.5 = (bf16[256,128]{1,0:T(8,128)(2,1)S(1)}, bf16[256,128]{1,0:T(8,128)(2,1)S(1)}, u32[]{:S(2)}, u32[]{:S(2)}) collective-permute-start(bf16[256,128]{1,0:T(8,128)(2,1)S(1)} %collective-permute-done.4.refs_7_.refs_10_), channel_id=1, source_target_pairs={{0,1},{1,0},{2,3},{3,2},{4,5},{5,4},{6,7},{7,6},{8,9},{9,8},{10,11... | collective-permute-start | bytes 196616 | tf_op jit(solution)/shard_map/ppermute | solution.py:229
  15.1 4.7 %collective-permute-start.7 = (bf16[256,128]{1,0:T(8,128)(2,1)S(1)}, bf16[256,128]{1,0:T(8,128)(2,1)S(1)}, u32[]{:S(2)}, u32[]{:S(2)}) collective-permute-start(bf16[256,128]{1,0:T(8,128)(2,1)S(1)} %collective-permute-done.6), channel_id=1, source_target_pairs={{0,1},{1,0},{2,3},{3,2},{4,5},{5,4},{6,7},{7,6},{8,9},{9,8},{10,11... | collective-permute-start | bytes 196616 | tf_op jit(solution)/shard_map/ppermute | solution.py:229
  15.1 0.7 %copy-start.2 = (s32[32]{0:T(128)S(1)}, s32[32]{0:T(128)}, u32[]{:S(2)}) copy-start(s32[32]{0:T(128)} %refs_0_.3) | copy-start | bytes 388
  15.8 0.9 %copy-start.3 = (bf16[128,1024]{1,0:T(8,128)(2,1)S(1)}, bf16[128,1024]{1,0:T(8,128)(2,1)}, u32[]{:S(2)}) copy-start(bf16[128,1024]{1,0:T(8,128)(2,1)} %refs_1_.1) | copy-start | bytes 786436
  16.7 0.9 %copy-start.4 = (bf16[128,1024]{1,0:T(8,128)(2,1)S(1)}, bf16[128,1024]{1,0:T(8,128)(2,1)}, u32[]{:S(2)}) copy-start(bf16[128,1024]{1,0:T(8,128)(2,1)} %refs_2_.1) | copy-start | bytes 786436
  22.8 1.3 %copy-start = (bf16[1024,1024]{1,0:T(8,128)(2,1)}, bf16[1024,1024]{1,0:T(8,128)(2,1)S(1)}, u32[]{:S(2)}) copy-start(bf16[1024,1024]{1,0:T(8,128)(2,1)S(1)} %get-tuple-element.20.refs_1_.score_grad_ref) | copy-start | bytes 6291460
  22.8 1.7 %collective-permute-start.9 = (bf16[4,256,128]{2,1,0:T(8,128)(2,1)S(1)}, bf16[4,256,128]{2,1,0:T(8,128)(2,1)S(1)}, u32[]{:S(2)}, u32[]{:S(2)}) collective-permute-start(bf16[4,256,128]{2,1,0:T(8,128)(2,1)S(1)} %get-tuple-element.23), channel_id=1, source_target_pairs={{0,1},{1,0},{2,3},{3,2},{4,5},{5,4},{6,7},{7,6},{8,9},{9,8},{10,11... | collective-permute-start | bytes 786440 | tf_op jit(solution)/shard_map/ppermute | solution.py:229
  25.2 9.0 %collective-permute-start.10 = (bf16[256,128]{1,0:T(8,128)(2,1)}, bf16[256,128]{1,0:T(8,128)(2,1)S(1)}, u32[]{:S(2)}, u32[]{:S(2)}) collective-permute-start(bf16[256,128]{1,0:T(8,128)(2,1)} %get-tuple-element.24), channel_id=1, source_target_pairs={{0,30},{1,31},{2,0},{3,1},{4,2},{5,3},{6,4},{7,5},{8,6},{9,7},{10,... | collective-permute-start | bytes 196616 | tf_op jit(solution)/shard_map/ppermute | solution.py:226
  27.6 6.6 %collective-permute-start.11 = (bf16[256,128]{1,0:T(8,128)(2,1)}, bf16[256,128]{1,0:T(8,128)(2,1)}, u32[]{:S(2)}, u32[]{:S(2)}) collective-permute-start(bf16[256,128]{1,0:T(8,128)(2,1)} %get-tuple-element.26), channel_id=1, source_target_pairs={{0,28},{1,29},{2,30},{3,31},{4,0},{5,1},{6,2},{7,3},{8,4},{9,5},{1... | collective-permute-start | bytes 196616 | tf_op jit(solution)/shard_map/ppermute | solution.py:226
  28.4 5.8 %collective-permute-start.12 = (bf16[256,128]{1,0:T(8,128)(2,1)}, bf16[256,128]{1,0:T(8,128)(2,1)}, u32[]{:S(2)}, u32[]{:S(2)}) collective-permute-start(bf16[256,128]{1,0:T(8,128)(2,1)} %get-tuple-element.25), channel_id=1, source_target_pairs={{0,26},{1,27},{2,28},{3,29},{4,30},{5,31},{6,0},{7,1},{8,2},{9,3},... | collective-permute-start | bytes 196616 | tf_op jit(solution)/shard_map/ppermute | solution.py:226
  29.8 5.3 %collective-permute-start.13 = (bf16[256,128]{1,0:T(8,128)(2,1)}, bf16[256,128]{1,0:T(8,128)(2,1)}, u32[]{:S(2)}, u32[]{:S(2)}) collective-permute-start(bf16[256,128]{1,0:T(8,128)(2,1)} %slice_bitcast_fusion.1), channel_id=1, source_target_pairs={{0,24},{1,25},{2,26},{3,27},{4,28},{5,29},{6,30},{7,31},{8,0},{9,1... | collective-permute-start | bytes 196616 | tf_op jit(solution)/shard_map/ppermute | solution.py:226
  30.9 1.6 %copy-start.1 = (bf16[1024,1024]{1,0:T(8,128)(2,1)S(1)}, bf16[1024,1024]{1,0:T(8,128)(2,1)}, u32[]{:S(2)}) copy-start(bf16[1024,1024]{1,0:T(8,128)(2,1)} %copy-done) | copy-start | bytes 6291460

commit v3 on v2

v3 whole, which is shorter than its diff:
```python
import functools
import math

import jax
import jax.numpy as jnp
from jax import lax
from jax.experimental import pallas as pl
from jax.experimental.pallas import tpu as pltpu
from jax.sharding import PartitionSpec as P

HEADS = 8
HEAD_DIM = 128
BLOCK = 128
FLAT = HEADS * BLOCK
AXES = ("pb", "kv")
SCALE = HEAD_DIM ** (-0.5)
SCALE_LOG2 = SCALE / math.log(2.0)
FAR = 1e30
COLS = 256
MIB = 2**20

VMEM = pl.BlockSpec(memory_space=pltpu.VMEM)
HBM = pl.BlockSpec(memory_space=pltpu.HBM)


def dot(left, right, left_dim, right_dim):
    return lax.dot_general(
        left, right, (((left_dim,), (right_dim,)), ((), ())), preferred_element_type=jnp.float32
    )


class Slots:
    def __init__(self, window):
        self.window = window
        self.half = half = window // 2
        lins = [("lin", k) for k in range(1, half)]
        sibs = [("sib", k) for k in range(1, half)]
        self.middle = lins[:-1]
        self.late = sibs + [lins[-1], "last"]
        self.order = sibs + ["last"] + ["own"] + lins

    def rows(self, slot):
        at = self.order.index(slot) * BLOCK
        return slice(at, at + BLOCK)

    def distance(self, slot, core):
        if slot == "last":
            return jnp.where(core == 0, self.window - 1, 1)
        return 2 * slot[1] if slot[0] == "lin" else 2 * slot[1] - 1 + 2 * core


def position():
    me = lax.axis_index("pb") * lax.axis_size("kv") + lax.axis_index("kv")
    return me, lax.rem(me, 2)


def reached(doc_ref, slots, slot):
    me, core = position()
    at = me - slots.distance(slot, core)
    return (at >= 0) & (doc_ref[jnp.maximum(at, 0)] == doc_ref[me])


def stacked(refs, part):
    return jnp.concatenate([ref[part * BLOCK : (part + 1) * BLOCK, :] for ref in refs], axis=0)


def tile_of(column):
    return slice(column * COLS, (column + 1) * COLS)


def absorb(parts, probs_grad, biases, top, total, mixed):
    new_top = top
    for part, bias in zip(parts, biases):
        new_top = jnp.maximum(new_top, jnp.max(part, axis=0, keepdims=True) * SCALE_LOG2 + bias)
    rescale = jnp.exp2(top - new_top)
    total, mixed = total * rescale, mixed * rescale
    powers = []
    for s, (part, bias) in enumerate(zip(parts, biases)):
        power = jnp.exp2(part * SCALE_LOG2 - (new_top - bias))
        powers.append(power)
        total = total + jnp.sum(power, axis=0, keepdims=True)
        mixed = mixed + jnp.sum(power * probs_grad[s * BLOCK : (s + 1) * BLOCK, :], axis=0, keepdims=True)
    return powers, new_top, total, mixed


def pair_kernel(key_ref, value_ref, pair_ref, sems):
    copies = [
        pltpu.make_async_copy(ref, pair_ref.at[part * BLOCK : (part + 1) * BLOCK, :], sems.at[part])
        for part, ref in enumerate((key_ref, value_ref))
    ]
    for copy in copies:
        copy.start()
    for copy in copies:
        copy.wait()


def own_kernel(
    slots, doc_hbm, query_ref, grad_ref, own_ref,
    query_rows, grad_rows, bias_ref, powers_ref, probs_ref, stats_ref, doc_ref, doc_sem, sems,
):
    copies = [pltpu.make_async_copy(doc_hbm, doc_ref, doc_sem)]
    for h in range(HEADS):
        rows = slice(h * BLOCK, (h + 1) * BLOCK)
        copies.append(pltpu.make_async_copy(query_ref.at[:, rows], query_rows.at[rows, :], sems.at[0, h]))
        copies.append(pltpu.make_async_copy(grad_ref.at[:, rows], grad_rows.at[rows, :], sems.at[1, h]))
    for copy in copies:
        copy.start()
    key_row = lax.broadcasted_iota(jnp.int32, (BLOCK, COLS), 0)
    token = lax.broadcasted_iota(jnp.int32, (BLOCK, COLS), 1) % BLOCK
    causal = key_row <= token
    for copy in copies:
        copy.wait()
    for row, slot in enumerate(slots.middle + slots.late):
        bias = jnp.where(reached(doc_ref, slots, slot), 0.0, -FAR)
        bias_ref[row : row + 1, :] = jnp.full((1, FLAT), bias, jnp.float32)
    for column in range(FLAT // COLS):
        cols = tile_of(column)
        scores = dot(own_ref[:BLOCK, :], query_rows[cols, :], 1, 1)
        probs_grad = dot(own_ref[BLOCK:, :], grad_rows[cols, :], 1, 1)
        scores = jnp.where(causal, scores, -FAR)
        start = jnp.full((1, COLS), -FAR, jnp.float32), jnp.zeros((1, COLS)), jnp.zeros((1, COLS))
        put_stage([scores], probs_grad, [0.0], start, column, powers_ref, probs_ref, stats_ref)


def put_stage(parts, probs_grad, biases, start, column, powers_ref, probs_ref, stats_ref):
    cols = tile_of(column)
    powers, top, total, mixed = absorb(parts, probs_grad, biases, *start)
    for s, power in enumerate(powers):
        powers_ref[s * BLOCK : (s + 1) * BLOCK, cols] = power
    probs_ref[:, cols] = probs_grad
    for row, value in enumerate((top, total, mixed)):
        stats_ref[row : row + 1, cols] = value


def middle_kernel(slots, *refs):
    count = len(slots.middle)
    bias_ref, query_rows, grad_rows, before_ref = refs[:4]
    blocks = refs[4 : 4 + count]
    powers_ref, probs_ref, stats_ref = refs[4 + count :]
    keys, values = stacked(blocks, 0), stacked(blocks, 1)
    for column in range(FLAT // COLS):
        cols = tile_of(column)
        scores = dot(keys, query_rows[cols, :], 1, 1)
        probs_grad = dot(values, grad_rows[cols, :], 1, 1)
        parts = [scores[s * BLOCK : (s + 1) * BLOCK, :] for s in range(count)]
        start = tuple(before_ref[row : row + 1, cols] for row in range(3))
        biases = [bias_ref[row : row + 1, cols] for row in range(count)]
        put_stage(parts, probs_grad, biases, start, column, powers_ref, probs_ref, stats_ref)


def late_kernel(slots, *refs):
    half, count = slots.half, len(slots.late)
    bias_ref, query_rows, grad_rows = refs[:3]
    stages = [refs[3:6], refs[6:9]]
    blocks = list(refs[9 : 9 + count])
    sib_own_ref = refs[9 + count]
    weights_ref, score_grad_ref, sib_out_ref, last_ref = refs[10 + count :]
    _, core = position()

    @pl.when(core == 0)
    def _():
        last_ref[...] = blocks[-1][...]

    @pl.when(core == 1)
    def _():
        last_ref[...] = sib_own_ref[...]

    blocks[-1] = last_ref
    keys, values = stacked(blocks, 0), stacked(blocks, 1)
    for column in range(FLAT // COLS):
        cols = tile_of(column)
        scores = dot(keys, query_rows[cols, :], 1, 1)
        probs_grad = dot(values, grad_rows[cols, :], 1, 1)
        parts = [scores[s * BLOCK : (s + 1) * BLOCK, :] for s in range(count)]
        start = tuple(stages[-1][2][row : row + 1, cols] for row in range(3))
        first = len(slots.middle)
        biases = [bias_ref[row : row + 1, cols] for row in range(first, first + count)]
        powers, top, total, mixed = absorb(parts, probs_grad, biases, *start)
        inverse = 1.0 / total
        delta = mixed * inverse

        def put(slot, weights, probs):
            rows = slots.rows(slot)
            weights_ref[rows, cols] = weights.astype(jnp.bfloat16)
            score_grad_ref[rows, cols] = (weights * (probs - delta)).astype(jnp.bfloat16)

        for (powers_ref, probs_ref, stats_ref), group in zip(stages, (["own"], slots.middle)):
            factor = jnp.exp2(stats_ref[0:1, cols] - top) * inverse
            for s, slot in enumerate(group):
                rows = slice(s * BLOCK, (s + 1) * BLOCK)
                put(slot, powers_ref[rows, cols] * factor, probs_ref[rows, cols])
        for s, slot in enumerate(slots.late):
            put(slot, powers[s] * inverse, probs_grad[s * BLOCK : (s + 1) * BLOCK, :])

    rows = slice(0, half * BLOCK)
    key_grad = dot(score_grad_ref[rows, :], query_rows[...], 1, 0) * SCALE
    value_grad = dot(weights_ref[rows, :], grad_rows[...], 1, 0)
    for k in range(half):
        rows = slice(k * BLOCK, (k + 1) * BLOCK)
        sib_out_ref[k, :BLOCK, :] = key_grad[rows, :].astype(jnp.bfloat16)
        sib_out_ref[k, BLOCK:, :] = value_grad[rows, :].astype(jnp.bfloat16)


def mine_kernel(slots, weights_ref, score_grad_ref, query_rows, grad_rows, mine_ref):
    half = slots.half
    rows = slice(half * BLOCK, slots.window * BLOCK)
    key_grad = dot(score_grad_ref[rows, :], query_rows[...], 1, 0) * SCALE
    value_grad = dot(weights_ref[rows, :], grad_rows[...], 1, 0)
    for k in range(half):
        rows = slice(k * BLOCK, (k + 1) * BLOCK)
        mine_ref[k, :BLOCK, :] = key_grad[rows, :]
        mine_ref[k, BLOCK:, :] = value_grad[rows, :]


def query_side_kernel(slots, *refs):
    weights_ref, score_grad_ref, sib_own_ref = refs[:3]
    blocks = list(refs[3 : 3 + slots.window])
    attended_ref, query_grad_ref, last_ref = refs[3 + slots.window :]
    _, core = position()
    at = slots.order.index("last")

    @pl.when(core == 0)
    def _():
        last_ref[...] = blocks[at][...]

    @pl.when(core == 1)
    def _():
        last_ref[...] = sib_own_ref[...]

    blocks[at] = last_ref
    attended_t = dot(stacked(blocks, 1), weights_ref[...], 0, 0)
    query_grad_t = dot(stacked(blocks, 0), score_grad_ref[...], 0, 0) * SCALE
    for h in range(HEADS):
        rows = slice(h * BLOCK, (h + 1) * BLOCK)
        attended_ref[:, rows] = attended_t[:, rows].T.astype(jnp.bfloat16)
        query_grad_ref[:, rows] = query_grad_t[:, rows].T.astype(jnp.bfloat16)


def merge_kernel(mine_ref, from_sib_ref, *sent_refs):
    for k, ref in enumerate(sent_refs[:-1]):
        ref[...] = (mine_ref[k + 1] + from_sib_ref[k].astype(jnp.float32)).astype(jnp.bfloat16)
    sent_refs[-1][...] = from_sib_ref[len(sent_refs) - 1]


def total_kernel(mine_ref, from_sib_ref, *refs):
    back, (key_ref, value_ref) = refs[:-2], refs[-2:]
    _, core = position()
    near = from_sib_ref[len(back) - 1].astype(jnp.float32)
    total = mine_ref[0] + jnp.where(core == 0, near, back[-1][...].astype(jnp.float32))
    for ref in back[:-1]:
        total = total + ref[...].astype(jnp.float32)
    key_ref[...] = total[:BLOCK].astype(jnp.bfloat16)
    value_ref[...] = total[BLOCK:].astype(jnp.bfloat16)


def in_vmem(array):
    return pltpu.with_memory_space_constraint(array, pltpu.VMEM)


def in_hbm(array):
    return pltpu.with_memory_space_constraint(array, pltpu.HBM)


def cost(blocks, products):
    flops = 2 * products * blocks * BLOCK * FLAT * HEAD_DIM
    return pl.CostEstimate(flops=flops, bytes_accessed=blocks * BLOCK * FLAT * 4, transcendentals=0)


def local(devices, queries, key_rows, value_rows, out_grad, doc_ids):
    window = lax.axis_size("kv")
    slots = Slots(window)
    half = slots.half
    bf16, f32 = jnp.bfloat16, jnp.float32
    shape = jax.ShapeDtypeStruct
    small = pltpu.CompilerParams(vmem_limit_bytes=window * MIB // 4)
    params = pltpu.CompilerParams(vmem_limit_bytes=window * MIB)

    def ahead(block, k):
        return lax.ppermute(block, AXES, [(i, (i + 2 * k) % devices) for i in range(devices)])

    def swapped(block):
        return lax.ppermute(block, AXES, [(i, i ^ 1) for i in range(devices)])

    own = pl.pallas_call(
        pair_kernel,
        out_shape=pltpu.VMEM((2 * BLOCK, HEAD_DIM), bf16),
        in_specs=[HBM, HBM],
        out_specs=VMEM,
        scratch_shapes=[pltpu.SemaphoreType.DMA((2,))],
        compiler_params=small,
        name="pair_up",
    )(in_hbm(key_rows), in_hbm(value_rows))
    lins = [ahead(own, k) for k in range(1, half + 1)]
    sib_own = swapped(own)

    def stage(blocks):
        return [
            pltpu.VMEM((blocks * BLOCK, FLAT), f32),
            pltpu.VMEM((blocks * BLOCK, FLAT), f32),
            pltpu.VMEM((8, FLAT), f32),
        ]

    query_rows, grad_rows, bias, *own_stage = pl.pallas_call(
        functools.partial(own_kernel, slots),
        out_shape=[pltpu.VMEM((FLAT, HEAD_DIM), bf16)] * 2 + [pltpu.VMEM((window, FLAT), f32)] + stage(1),
        in_specs=[HBM, HBM, HBM, VMEM],
        out_specs=[VMEM] * 6,
        scratch_shapes=[
            pltpu.SMEM(doc_ids.shape, jnp.int32),
            pltpu.SemaphoreType.DMA,
            pltpu.SemaphoreType.DMA((2, HEADS)),
        ],
        compiler_params=params,
        cost_estimate=cost(1, 2),
        name="own_scores",
    )(in_hbm(doc_ids), in_hbm(queries), in_hbm(out_grad), own)

    lins[0], own_stage[2] = lax.optimization_barrier((lins[0], own_stage[2]))
    sibs = [swapped(block) for block in lins[: half - 2]]
    held = {("lin", k): lins[k - 1] for k in range(1, half - 1)}
    middle = len(slots.middle)
    *middle_stage, = pl.pallas_call(
        functools.partial(middle_kernel, slots),
        out_shape=stage(middle),
        in_specs=[VMEM] * (4 + middle),
        out_specs=[VMEM] * 3,
        compiler_params=params,
        cost_estimate=cost(middle, 2),
        name="middle_scores",
    )(bias, query_rows, grad_rows, own_stage[2], *[held[slot] for slot in slots.middle])

    lins[half - 2], lins[half - 1], middle_stage[2] = lax.optimization_barrier(
        (lins[half - 2], lins[half - 1], middle_stage[2])
    )
    sibs += [swapped(block) for block in lins[half - 2 :]]
    held |= {"own": own, "last": sibs[-1]}
    for k in range(1, half):
        held["lin", k] = lins[k - 1]
        held["sib", k] = sibs[k - 1]

    weights, score_grad, sib_out = pl.pallas_call(
        functools.partial(late_kernel, slots),
        out_shape=[
            pltpu.VMEM((window * BLOCK, FLAT), bf16),
            pltpu.VMEM((window * BLOCK, FLAT), bf16),
            pltpu.VMEM((half, 2 * BLOCK, HEAD_DIM), bf16),
        ],
        in_specs=[VMEM] * (10 + len(slots.late)),
        out_specs=[VMEM] * 3,
        scratch_shapes=[pltpu.VMEM((2 * BLOCK, HEAD_DIM), bf16)],
        compiler_params=params,
        cost_estimate=cost(window, 3),
        name="late_scores",
    )(
        bias, query_rows, grad_rows, *own_stage, *middle_stage,
        *[held[slot] for slot in slots.late], sib_own,
    )
    from_sib = swapped(sib_out)

    mine = pl.pallas_call(
        functools.partial(mine_kernel, slots),
        out_shape=pltpu.VMEM((half, 2 * BLOCK, HEAD_DIM), f32),
        in_specs=[VMEM] * 4,
        out_specs=VMEM,
        compiler_params=params,
        cost_estimate=cost(half, 2),
        name="own_parity_grads",
    )(weights, score_grad, query_rows, grad_rows)

    attended, query_grad = pl.pallas_call(
        functools.partial(query_side_kernel, slots),
        out_shape=[shape(queries.shape, bf16), shape(queries.shape, bf16)],
        in_specs=[VMEM] * (3 + window),
        out_specs=[VMEM] * 2,
        scratch_shapes=[pltpu.VMEM((2 * BLOCK, HEAD_DIM), bf16)],
        compiler_params=params,
        cost_estimate=cost(window, 2),
        name="query_side",
    )(in_vmem(weights), in_vmem(score_grad), sib_own, *[held[slot] for slot in slots.order])

    sent = pl.pallas_call(
        merge_kernel,
        out_shape=[pltpu.VMEM((2 * BLOCK, HEAD_DIM), bf16)] * half,
        in_specs=[VMEM] * 2,
        out_specs=[VMEM] * half,
        compiler_params=small,
        name="merge_siblings",
    )(mine, from_sib)
    back = [ahead(block, -(k + 1)) for k, block in enumerate(sent)]
    key_grad, value_grad = pl.pallas_call(
        total_kernel,
        out_shape=[shape((BLOCK, HEAD_DIM), bf16)] * 2,
        in_specs=[VMEM] * (2 + half),
        out_specs=[VMEM] * 2,
        compiler_params=small,
        name="total_grads",
    )(mine, from_sib, *back)
    return attended, query_grad, key_grad, value_grad


def solution(mesh):
    split = P(AXES, None)
    devices = mesh.shape["pb"] * mesh.shape["kv"]
    return jax.shard_map(
        functools.partial(local, devices),
        mesh=mesh,
        in_specs=(split, split, split, split, P()),
        out_specs=(split, split, split, split),
        check_vma=False,
    )
```

time: 37 us -> 31.4 us (0.85)
  local copies, waits for them, and re-layouts: 6.94 us -> 0 us
  waiting for transfers between devices: 5.29 us -> 6.92 us
  other arithmetic: 1.61 us -> 0 us
  Pallas kernels: 7.36 us -> 8.47 us
    unnamed x11 -> x0, local copies, waits for them, and re-layouts: 4.93 us -> none
    convert_element_type x2 -> x0, other arithmetic: 1.61 us -> none  [the longest x1 0.92 us: local(): total = total.astype(bf16)]
    ppermute x6, waiting for transfers between devices: 0.43 us -> 1.91 us  [swapped(): return lax.ppermute(block, AXES, [(i, i ^ 1) for i in range(devices)])]
    pallas_call x3 -> x7, Pallas kernels: 5.71 us -> 6.83 us  [the longest x1 2.5 us: local(): pl.pallas_call(functools.partial(late_kernel, slots), out_shape=[pltpu.VM...]
    concatenate x1 -> x0, local copies, waits for them, and re-layouts: 0.77 us -> none  [local(): own = jnp.concatenate([key_rows, value_rows], axis=0)]
    slice x1 -> x0, local copies, waits for them, and re-layouts: 0.63 us -> none  [local(): return (attended, query_grad, total[:BLOCK], total[BLOCK:])]
    squeeze x1 -> x0, local copies, waits for them, and re-layouts: 0.62 us -> none  [local(): from_sib[half - 1]]
  transfers between devices with their start and end apart: 14 -> 14, of which waited for: 5 -> 7; matrix products, arithmetic and copies ran while one was open for 2% -> 0% of each run, Pallas kernels for 12% -> 14%
where the time goes in v3:
time: 31.4 us; the launch traced here: 31.1 us
  starting transfers between devices  15 us (48%)
  Pallas kernels  8.47 us (27%)
  waiting for transfers between devices  6.92 us (22%)
  between operations  0.7 us (2%)
    ppermute x8, starting transfers between devices, ahead(): lax.ppermute(block, AXES, [(i, (i + 2 * k) % devices) for i in range(devi...  13.7 us
    ppermute x8, waiting for transfers between devices, ahead(): lax.ppermute(block, AXES, [(i, (i + 2 * k) % devices) for i in range(devi...  5.01 us
    pallas_call x1, Pallas kernels, local(): pl.pallas_call(functools.partial(late_kernel, slots), out_shape=[pltpu.VM...  2.5 us
    ppermute x6, waiting for transfers between devices, swapped(): return lax.ppermute(block, AXES, [(i, i ^ 1) for i in range(devices)])  1.91 us
    pallas_call x1, Pallas kernels, local(): pl.pallas_call(functools.partial(query_side_kernel, slots), out_shape=[sh...  1.63 us
    pallas_call x1, Pallas kernels, local(): pl.pallas_call(functools.partial(own_kernel, slots), out_shape=[pltpu.VME...  1.54 us
    ppermute x6, starting transfers between devices, swapped(): return lax.ppermute(block, AXES, [(i, i ^ 1) for i in range(devices)])  1.32 us
    pallas_call x1, Pallas kernels, local(): pl.pallas_call(pair_kernel, out_shape=pltpu.VMEM((2 * BLOCK, HEAD_DIM), b...  0.79 us
  transfers between devices with their start and end apart: 14, of which 7 were waited for; matrix products, arithmetic and copies ran while one was open for 0% of the time, Pallas kernels for 14%

profile of v3, /device:TPU:0, one launch (start us, length us, event | category | flops | bytes accessed | tf_op | source)
XLA Modules:
  0.0 31.1 jit_solution(4908195287810291962)
XLA Ops:
  0.6 0.8 %pair_up.1.own_ref.refs_7_ = bf16[256,128]{1,0:T(8,128)(2,1)S(1)} custom-call(bf16[128,128]{1,0:T(8,128)(2,1)} %key_ref.1, bf16[128,128]{1,0:T(8,128)(2,1)} %value_ref.1), custom_call_target="tpu_custom_call" | custom-call | tf_op jit(solution)/shard_map/pair_up/pallas_call | solution.py:284
  1.4 3.0 %collective-permute-start = (bf16[256,128]{1,0:T(8,128)(2,1)S(1)}, bf16[256,128]{1,0:T(8,128)(2,1)S(1)}, u32[]{:S(2)}, u32[]{:S(2)}) collective-permute-start(bf16[256,128]{1,0:T(8,128)(2,1)S(1)} %pair_up.1.own_ref.refs_7_), channel_id=1, source_target_pairs={{0,2},{1,3},{2,4},{3,5},{4,6},{5,7},{6,8},{7,9},{8,10},{9,11},{10,... | collective-permute-start | bytes 196616 | tf_op jit(solution)/shard_map/ppermute | solution.py:279
  4.4 1.5 %collective-permute-start.1 = (bf16[256,128]{1,0:T(8,128)(2,1)S(1)}, bf16[256,128]{1,0:T(8,128)(2,1)S(1)}, u32[]{:S(2)}, u32[]{:S(2)}) collective-permute-start(bf16[256,128]{1,0:T(8,128)(2,1)S(1)} %pair_up.1.own_ref.refs_7_), channel_id=1, source_target_pairs={{0,4},{1,5},{2,6},{3,7},{4,8},{5,9},{6,10},{7,11},{8,12},{9,13},{1... | collective-permute-start | bytes 196616 | tf_op jit(solution)/shard_map/ppermute | solution.py:279
  5.9 1.6 %collective-permute-start.3 = (bf16[256,128]{1,0:T(8,128)(2,1)S(1)}, bf16[256,128]{1,0:T(8,128)(2,1)S(1)}, u32[]{:S(2)}, u32[]{:S(2)}) collective-permute-start(bf16[256,128]{1,0:T(8,128)(2,1)S(1)} %pair_up.1.own_ref.refs_7_), channel_id=1, source_target_pairs={{0,8},{1,9},{2,10},{3,11},{4,12},{5,13},{6,14},{7,15},{8,16},{9,17... | collective-permute-start | bytes 196616 | tf_op jit(solution)/shard_map/ppermute | solution.py:279
  7.5 2.4 %collective-permute-start.2 = (bf16[256,128]{1,0:T(8,128)(2,1)S(1)}, bf16[256,128]{1,0:T(8,128)(2,1)S(1)}, u32[]{:S(2)}, u32[]{:S(2)}) collective-permute-start(bf16[256,128]{1,0:T(8,128)(2,1)S(1)} %pair_up.1.own_ref.refs_7_), channel_id=1, source_target_pairs={{0,6},{1,7},{2,8},{3,9},{4,10},{5,11},{6,12},{7,13},{8,14},{9,15},... | collective-permute-start | bytes 196616 | tf_op jit(solution)/shard_map/ppermute | solution.py:279
  10.0 1.5 %own_scores.1 = (bf16[1024,128]{1,0:T(8,128)(2,1)S(1)}, bf16[1024,128]{1,0:T(8,128)(2,1)S(1)}, f32[8,1024]{1,0:T(8,128)S(1)}, f32[128,1024]{1,0:T(8,128)S(1)}, f...) custom-call(s32[32]{0:T(128)} %doc_hbm.1, bf16[128,1024]{1,0:T(8,128)(2,1)} %query_ref.1, bf16[128,1024]{1,0:T(8,128)(2,1)} %grad_ref.1, ...), custom_call_target="tpu_custom_call" | custom-call | flops 67108864 | bytes 524288 | tf_op jit(solution)/shard_map/own_scores/pallas_call | solution.py:303
  11.5 0.6 %collective-permute-start.4 = (bf16[256,128]{1,0:T(8,128)(2,1)S(1)}, bf16[256,128]{1,0:T(8,128)(2,1)S(1)}, u32[]{:S(2)}, u32[]{:S(2)}) collective-permute-start(bf16[256,128]{1,0:T(8,128)(2,1)S(1)} %collective-permute-done.refs_4_.refs_8_), channel_id=1, source_target_pairs={{0,1},{1,0},{2,3},{3,2},{4,5},{5,4},{6,7},{7,6},{8,9},{9,8},{10,11... | collective-permute-start | bytes 196616 | tf_op jit(solution)/shard_map/ppermute | solution.py:282
  12.1 0.6 %middle_scores.1 = (f32[256,1024]{1,0:T(8,128)S(1)}, f32[256,1024]{1,0:T(8,128)S(1)}, f32[8,1024]{1,0:T(8,128)S(1)}) custom-call(f32[8,1024]{1,0:T(8,128)S(1)} %get-tuple-element.29.refs_0_, bf16[1024,128]{1,0:T(8,128)(2,1)S(1)} %get-tuple-element.30.refs_1_.query_rows, bf16[1024,128]{1,0:T(8,128)(2,1)S(1)} %get-tuple-element.31.refs_2_.grad_rows, ...), custom_call_target="tpu_custom_call" | custom-call | flops 134217728 | bytes 1048576 | tf_op jit(solution)/shard_map/middle_scores/pallas_call | solution.py:322
  12.7 1.8 %collective-permute-done.2.refs_12_.refs_10_ = bf16[256,128]{1,0:T(8,128)(2,1)S(1)} collective-permute-done((bf16[256,128]{1,0:T(8,128)(2,1)S(1)}, bf16[256,128]{1,0:T(8,128)(2,1)S(1)}, u32[]{:S(2)}, u32[]{:S(2)}) %collective-permute-start.2) | collective-permute-done | bytes 65568 | tf_op jit(solution)/shard_map/ppermute | solution.py:279
  14.5 0.5 %collective-permute-start.7 = (bf16[256,128]{1,0:T(8,128)(2,1)S(1)}, bf16[256,128]{1,0:T(8,128)(2,1)S(1)}, u32[]{:S(2)}, u32[]{:S(2)}) collective-permute-start(bf16[256,128]{1,0:T(8,128)(2,1)S(1)} %collective-permute-done.3), channel_id=1, source_target_pairs={{0,1},{1,0},{2,3},{3,2},{4,5},{5,4},{6,7},{7,6},{8,9},{9,8},{10,11... | collective-permute-start | bytes 196616 | tf_op jit(solution)/shard_map/ppermute | solution.py:282
  15.0 0.7 %collective-permute-done.5.refs_10_.refs_4_ = bf16[256,128]{1,0:T(8,128)(2,1)S(1)} collective-permute-done((bf16[256,128]{1,0:T(8,128)(2,1)S(1)}, bf16[256,128]{1,0:T(8,128)(2,1)S(1)}, u32[]{:S(2)}, u32[]{:S(2)}) %collective-permute-start.5) | collective-permute-done | bytes 65568 | tf_op jit(solution)/shard_map/ppermute | solution.py:282
  15.9 0.4 %collective-permute-done.6.refs_11_.refs_5_ = bf16[256,128]{1,0:T(8,128)(2,1)S(1)} collective-permute-done((bf16[256,128]{1,0:T(8,128)(2,1)S(1)}, bf16[256,128]{1,0:T(8,128)(2,1)S(1)}, u32[]{:S(2)}, u32[]{:S(2)}) %collective-permute-start.6) | collective-permute-done | bytes 65568 | tf_op jit(solution)/shard_map/ppermute | solution.py:282
  16.2 2.5 %late_scores.1 = (bf16[1024,1024]{1,0:T(8,128)(2,1)S(1)}, bf16[1024,1024]{1,0:T(8,128)(2,1)S(1)}, bf16[4,256,128]{2,1,0:T(8,128)(2,1)S(1)}) custom-call(f32[8,1024]{1,0:T(8,128)S(1)} %get-tuple-element.29.refs_0_, bf16[1024,128]{1,0:T(8,128)(2,1)S(1)} %get-tuple-element.30.refs_1_.query_rows, bf16[1024,128]{1,0:T(8,128)(2,1)S(1)} %get-tuple-element.31.refs_2_.grad_rows, ...), custom_call_target="tpu_custom_call" | custom-call | flops 805306368 | bytes 4194304 | tf_op jit(solution)/shard_map/late_scores/pallas_call | solution.py:341
  18.8 0.2 collective-permute-start.9
  19.0 0.7 %own_parity_grads.1.mine_ref = f32[4,256,128]{2,1,0:T(8,128)S(1)} custom-call(bf16[1024,1024]{1,0:T(8,128)(2,1)S(1)} %get-tuple-element.43.refs_0_.weights_ref, bf16[1024,1024]{1,0:T(8,128)(2,1)S(1)} %get-tuple-element.44.refs_1_.score_grad_ref, bf16[1024,128]{1,0:T(8,128)(2,1)S(1)} %get-tuple-element.30.refs_1_.query_rows, ...), custom_call_target="tpu_custom_call" | custom-call | flops 268435456 | bytes 2097152 | tf_op jit(solution)/shard_map/own_parity_grads/pallas_call | solution.py:360
  19.7 0.7 %collective-permute-done.9.from_sib_ref = bf16[4,256,128]{2,1,0:T(8,128)(2,1)S(1)} collective-permute-done((bf16[4,256,128]{2,1,0:T(8,128)(2,1)S(1)}, bf16[4,256,128]{2,1,0:T(8,128)(2,1)S(1)}, u32[]{:S(2)}, u32[]{:S(2)}) %collective-permute-start.9) | collective-permute-done | bytes 262176 | tf_op jit(solution)/shard_map/ppermute | solution.py:282
  20.4 2.4 %collective-permute-start.10 = (bf16[256,128]{1,0:T(8,128)(2,1)S(1)}, bf16[256,128]{1,0:T(8,128)(2,1)S(1)}, u32[]{:S(2)}, u32[]{:S(2)}) collective-permute-start(bf16[256,128]{1,0:T(8,128)(2,1)S(1)} %get-tuple-element.48), channel_id=1, source_target_pairs={{0,30},{1,31},{2,0},{3,1},{4,2},{5,3},{6,4},{7,5},{8,6},{9,7},{10,... | collective-permute-start | bytes 196616 | tf_op jit(solution)/shard_map/ppermute | solution.py:279
  22.8 1.4 %collective-permute-start.11 = (bf16[256,128]{1,0:T(8,128)(2,1)S(1)}, bf16[256,128]{1,0:T(8,128)(2,1)S(1)}, u32[]{:S(2)}, u32[]{:S(2)}) collective-permute-start(bf16[256,128]{1,0:T(8,128)(2,1)S(1)} %get-tuple-element.49), channel_id=1, source_target_pairs={{0,28},{1,29},{2,30},{3,31},{4,0},{5,1},{6,2},{7,3},{8,4},{9,5},{1... | collective-permute-start | bytes 196616 | tf_op jit(solution)/shard_map/ppermute | solution.py:279
  24.2 0.5 %collective-permute-start.12 = (bf16[256,128]{1,0:T(8,128)(2,1)S(1)}, bf16[256,128]{1,0:T(8,128)(2,1)S(1)}, u32[]{:S(2)}, u32[]{:S(2)}) collective-permute-start(bf16[256,128]{1,0:T(8,128)(2,1)S(1)} %get-tuple-element.50), channel_id=1, source_target_pairs={{0,26},{1,27},{2,28},{3,29},{4,30},{5,31},{6,0},{7,1},{8,2},{9,3},... | collective-permute-start | bytes 196616 | tf_op jit(solution)/shard_map/ppermute | solution.py:279
  24.7 0.9 %collective-permute-start.13 = (bf16[256,128]{1,0:T(8,128)(2,1)S(1)}, bf16[256,128]{1,0:T(8,128)(2,1)S(1)}, u32[]{:S(2)}, u32[]{:S(2)}) collective-permute-start(bf16[256,128]{1,0:T(8,128)(2,1)S(1)} %get-tuple-element.51), channel_id=1, source_target_pairs={{0,24},{1,25},{2,26},{3,27},{4,28},{5,29},{6,30},{7,31},{8,0},{9,1... | collective-permute-start | bytes 196616 | tf_op jit(solution)/shard_map/ppermute | solution.py:279
  25.6 1.6 %query_side.1 = (bf16[128,1024]{1,0:T(8,128)(2,1)}, bf16[128,1024]{1,0:T(8,128)(2,1)}) custom-call(bf16[1024,1024]{1,0:T(8,128)(2,1)S(1)} %get-tuple-element.43.refs_0_.weights_ref, bf16[1024,1024]{1,0:T(8,128)(2,1)S(1)} %get-tuple-element.44.refs_1_.score_grad_ref, bf16[256,128]{1,0:T(8,128)(2,1)S(1)} %collective-permute-done.8.refs_14_.refs_2_, ...), custom_call_target="tpu_custom_call" | custom-call | flops 536870912 | bytes 4194304 | tf_op jit(solution)/shard_map/query_side/pallas_call | solution.py:370
  27.2 2.1 %collective-permute-done.12.refs_2_ = bf16[256,128]{1,0:T(8,128)(2,1)S(1)} collective-permute-done((bf16[256,128]{1,0:T(8,128)(2,1)S(1)}, bf16[256,128]{1,0:T(8,128)(2,1)S(1)}, u32[]{:S(2)}, u32[]{:S(2)}) %collective-permute-start.12) | collective-permute-done | bytes 65568 | tf_op jit(solution)/shard_map/ppermute | solution.py:279
  29.4 1.1 %collective-permute-done.13.refs_3_ = bf16[256,128]{1,0:T(8,128)(2,1)S(1)} collective-permute-done((bf16[256,128]{1,0:T(8,128)(2,1)S(1)}, bf16[256,128]{1,0:T(8,128)(2,1)S(1)}, u32[]{:S(2)}, u32[]{:S(2)}) %collective-permute-start.13) | collective-permute-done | bytes 65568 | tf_op jit(solution)/shard_map/ppermute | solution.py:279
  30.4 0.7 %total_grads.1 = (bf16[128,128]{1,0:T(8,128)(2,1)}, bf16[128,128]{1,0:T(8,128)(2,1)}) custom-call(f32[4,256,128]{2,1,0:T(8,128)S(1)} %own_parity_grads.1.mine_ref, bf16[4,256,128]{2,1,0:T(8,128)(2,1)S(1)} %collective-permute-done.9.from_sib_ref, bf16[256,128]{1,0:T(8,128)(2,1)S(1)} %collective-permute-done.10.refs_0_, ...), custom_call_target="tpu_custom_call" | custom-call | tf_op jit(solution)/shard_map/total_grads/pallas_call | solution.py:390
  (12 shorter events, 0.2 us)
Async XLA Ops:
  1.4 10.1 %collective-permute-start = (bf16[256,128]{1,0:T(8,128)(2,1)S(1)}, bf16[256,128]{1,0:T(8,128)(2,1)S(1)}, u32[]{:S(2)}, u32[]{:S(2)}) collective-permute-start(bf16[256,128]{1,0:T(8,128)(2,1)S(1)} %pair_up.1.own_ref.refs_7_), channel_id=1, source_target_pairs={{0,2},{1,3},{2,4},{3,5},{4,6},{5,7},{6,8},{7,9},{8,10},{9,11},{10,... | collective-permute-start | bytes 196616 | tf_op jit(solution)/shard_map/ppermute | solution.py:279
  4.4 7.7 %collective-permute-start.1 = (bf16[256,128]{1,0:T(8,128)(2,1)S(1)}, bf16[256,128]{1,0:T(8,128)(2,1)S(1)}, u32[]{:S(2)}, u32[]{:S(2)}) collective-permute-start(bf16[256,128]{1,0:T(8,128)(2,1)S(1)} %pair_up.1.own_ref.refs_7_), channel_id=1, source_target_pairs={{0,4},{1,5},{2,6},{3,7},{4,8},{5,9},{6,10},{7,11},{8,12},{9,13},{1... | collective-permute-start | bytes 196616 | tf_op jit(solution)/shard_map/ppermute | solution.py:279
  5.9 6.8 %collective-permute-start.3 = (bf16[256,128]{1,0:T(8,128)(2,1)S(1)}, bf16[256,128]{1,0:T(8,128)(2,1)S(1)}, u32[]{:S(2)}, u32[]{:S(2)}) collective-permute-start(bf16[256,128]{1,0:T(8,128)(2,1)S(1)} %pair_up.1.own_ref.refs_7_), channel_id=1, source_target_pairs={{0,8},{1,9},{2,10},{3,11},{4,12},{5,13},{6,14},{7,15},{8,16},{9,17... | collective-permute-start | bytes 196616 | tf_op jit(solution)/shard_map/ppermute | solution.py:279
  7.5 7.0 %collective-permute-start.2 = (bf16[256,128]{1,0:T(8,128)(2,1)S(1)}, bf16[256,128]{1,0:T(8,128)(2,1)S(1)}, u32[]{:S(2)}, u32[]{:S(2)}) collective-permute-start(bf16[256,128]{1,0:T(8,128)(2,1)S(1)} %pair_up.1.own_ref.refs_7_), channel_id=1, source_target_pairs={{0,6},{1,7},{2,8},{3,9},{4,10},{5,11},{6,12},{7,13},{8,14},{9,15},... | collective-permute-start | bytes 196616 | tf_op jit(solution)/shard_map/ppermute | solution.py:279
  10.0 5.0 %collective-permute-start.8 = (bf16[256,128]{1,0:T(8,128)(2,1)S(1)}, bf16[256,128]{1,0:T(8,128)(2,1)S(1)}, u32[]{:S(2)}, u32[]{:S(2)}) collective-permute-start(bf16[256,128]{1,0:T(8,128)(2,1)S(1)} %pair_up.1.own_ref.refs_7_), channel_id=1, source_target_pairs={{0,1},{1,0},{2,3},{3,2},{4,5},{5,4},{6,7},{7,6},{8,9},{9,8},{10,11... | collective-permute-start | bytes 196616 | tf_op jit(solution)/shard_map/ppermute | solution.py:282
  11.5 4.2 %collective-permute-start.4 = (bf16[256,128]{1,0:T(8,128)(2,1)S(1)}, bf16[256,128]{1,0:T(8,128)(2,1)S(1)}, u32[]{:S(2)}, u32[]{:S(2)}) collective-permute-start(bf16[256,128]{1,0:T(8,128)(2,1)S(1)} %collective-permute-done.refs_4_.refs_8_), channel_id=1, source_target_pairs={{0,1},{1,0},{2,3},{3,2},{4,5},{5,4},{6,7},{7,6},{8,9},{9,8},{10,11... | collective-permute-start | bytes 196616 | tf_op jit(solution)/shard_map/ppermute | solution.py:282
  14.5 1.3 %collective-permute-start.5 = (bf16[256,128]{1,0:T(8,128)(2,1)S(1)}, bf16[256,128]{1,0:T(8,128)(2,1)S(1)}, u32[]{:S(2)}, u32[]{:S(2)}) collective-permute-start(bf16[256,128]{1,0:T(8,128)(2,1)S(1)} %collective-permute-done.1.refs_5_.refs_9_), channel_id=1, source_target_pairs={{0,1},{1,0},{2,3},{3,2},{4,5},{5,4},{6,7},{7,6},{8,9},{9,8},{10,11... | collective-permute-start | bytes 196616 | tf_op jit(solution)/shard_map/ppermute | solution.py:282
  14.5 1.4 %collective-permute-start.7 = (bf16[256,128]{1,0:T(8,128)(2,1)S(1)}, bf16[256,128]{1,0:T(8,128)(2,1)S(1)}, u32[]{:S(2)}, u32[]{:S(2)}) collective-permute-start(bf16[256,128]{1,0:T(8,128)(2,1)S(1)} %collective-permute-done.3), channel_id=1, source_target_pairs={{0,1},{1,0},{2,3},{3,2},{4,5},{5,4},{6,7},{7,6},{8,9},{9,8},{10,11... | collective-permute-start | bytes 196616 | tf_op jit(solution)/shard_map/ppermute | solution.py:282
  15.0 1.3 %collective-permute-start.6 = (bf16[256,128]{1,0:T(8,128)(2,1)S(1)}, bf16[256,128]{1,0:T(8,128)(2,1)S(1)}, u32[]{:S(2)}, u32[]{:S(2)}) collective-permute-start(bf16[256,128]{1,0:T(8,128)(2,1)S(1)} %collective-permute-done.2.refs_12_.refs_10_), channel_id=1, source_target_pairs={{0,1},{1,0},{2,3},{3,2},{4,5},{5,4},{6,7},{7,6},{8,9},{9,8},{10,11... | collective-permute-start | bytes 196616 | tf_op jit(solution)/shard_map/ppermute | solution.py:282
  18.8 1.6 %collective-permute-start.9 = (bf16[4,256,128]{2,1,0:T(8,128)(2,1)S(1)}, bf16[4,256,128]{2,1,0:T(8,128)(2,1)S(1)}, u32[]{:S(2)}, u32[]{:S(2)}) collective-permute-start(bf16[4,256,128]{2,1,0:T(8,128)(2,1)S(1)} %get-tuple-element.47), channel_id=1, source_target_pairs={{0,1},{1,0},{2,3},{3,2},{4,5},{5,4},{6,7},{7,6},{8,9},{9,8},{10,11... | collective-permute-start | bytes 786440 | tf_op jit(solution)/shard_map/ppermute | solution.py:282
  20.4 6.8 %collective-permute-start.10 = (bf16[256,128]{1,0:T(8,128)(2,1)S(1)}, bf16[256,128]{1,0:T(8,128)(2,1)S(1)}, u32[]{:S(2)}, u32[]{:S(2)}) collective-permute-start(bf16[256,128]{1,0:T(8,128)(2,1)S(1)} %get-tuple-element.48), channel_id=1, source_target_pairs={{0,30},{1,31},{2,0},{3,1},{4,2},{5,3},{6,4},{7,5},{8,6},{9,7},{10,... | collective-permute-start | bytes 196616 | tf_op jit(solution)/shard_map/ppermute | solution.py:279
  22.8 4.4 %collective-permute-start.11 = (bf16[256,128]{1,0:T(8,128)(2,1)S(1)}, bf16[256,128]{1,0:T(8,128)(2,1)S(1)}, u32[]{:S(2)}, u32[]{:S(2)}) collective-permute-start(bf16[256,128]{1,0:T(8,128)(2,1)S(1)} %get-tuple-element.49), channel_id=1, source_target_pairs={{0,28},{1,29},{2,30},{3,31},{4,0},{5,1},{6,2},{7,3},{8,4},{9,5},{1... | collective-permute-start | bytes 196616 | tf_op jit(solution)/shard_map/ppermute | solution.py:279
  24.2 5.2 %collective-permute-start.12 = (bf16[256,128]{1,0:T(8,128)(2,1)S(1)}, bf16[256,128]{1,0:T(8,128)(2,1)S(1)}, u32[]{:S(2)}, u32[]{:S(2)}) collective-permute-start(bf16[256,128]{1,0:T(8,128)(2,1)S(1)} %get-tuple-element.50), channel_id=1, source_target_pairs={{0,26},{1,27},{2,28},{3,29},{4,30},{5,31},{6,0},{7,1},{8,2},{9,3},... | collective-permute-start | bytes 196616 | tf_op jit(solution)/shard_map/ppermute | solution.py:279
  24.7 5.7 %collective-permute-start.13 = (bf16[256,128]{1,0:T(8,128)(2,1)S(1)}, bf16[256,128]{1,0:T(8,128)(2,1)S(1)}, u32[]{:S(2)}, u32[]{:S(2)}) collective-permute-start(bf16[256,128]{1,0:T(8,128)(2,1)S(1)} %get-tuple-element.51), channel_id=1, source_target_pairs={{0,24},{1,25},{2,26},{3,27},{4,28},{5,29},{6,30},{7,31},{8,0},{9,1... | collective-permute-start | bytes 196616 | tf_op jit(solution)/shard_map/ppermute | solution.py:279

commit v4 on v3

--- a/solution.py
+++ b/solution.py
@@ -29,6 +29,10 @@
     )
 
 
+def rows_of(block):
+    return slice(block * BLOCK, (block + 1) * BLOCK)
+
+
 class Slots:
     def __init__(self, window):
         self.window = window
@@ -36,12 +40,16 @@
         lins = [("lin", k) for k in range(1, half)]
         sibs = [("sib", k) for k in range(1, half)]
         self.middle = lins[:-1]
-        self.late = sibs + [lins[-1], "last"]
-        self.order = sibs + ["last"] + ["own"] + lins
-
-    def rows(self, slot):
-        at = self.order.index(slot) * BLOCK
-        return slice(at, at + BLOCK)
+        self.closing = sibs[:-1] + lins[-1:]
+        self.late = [sibs[-1], "last"]
+        self.stages = [["own"], self.middle, self.closing, self.late]
+        self.sibs = sibs + ["last"]
+        self.mine = ["own"] + lins
+
+    def place(self, slot):
+        for at, group in enumerate(self.stages):
+            if slot in group:
+                return at, rows_of(group.index(slot))
 
     def distance(self, slot, core):
         if slot == "last":
@@ -110,7 +118,7 @@
     causal = key_row <= token
     for copy in copies:
         copy.wait()
-    for row, slot in enumerate(slots.middle + slots.late):
+    for row, slot in enumerate(slots.middle + slots.closing + slots.late):
         bias = jnp.where(reached(doc_ref, slots, slot), 0.0, -FAR)
         bias_ref[row : row + 1, :] = jnp.full((1, FLAT), bias, jnp.float32)
     for column in range(FLAT // COLS):
@@ -132,8 +140,7 @@
         stats_ref[row : row + 1, cols] = value
 
 
-def middle_kernel(slots, *refs):
-    count = len(slots.middle)
+def stage_kernel(first, count, *refs):
     bias_ref, query_rows, grad_rows, before_ref = refs[:4]
     blocks = refs[4 : 4 + count]
     powers_ref, probs_ref, stats_ref = refs[4 + count :]
@@ -142,19 +149,32 @@
         cols = tile_of(column)
         scores = dot(keys, query_rows[cols, :], 1, 1)
         probs_grad = dot(values, grad_rows[cols, :], 1, 1)
-        parts = [scores[s * BLOCK : (s + 1) * BLOCK, :] for s in range(count)]
+        parts = [scores[rows_of(s), :] for s in range(count)]
         start = tuple(before_ref[row : row + 1, cols] for row in range(3))
-        biases = [bias_ref[row : row + 1, cols] for row in range(count)]
+        biases = [bias_ref[row : row + 1, cols] for row in range(first, first + count)]
         put_stage(parts, probs_grad, biases, start, column, powers_ref, probs_ref, stats_ref)
 
 
+def put_weights(slot_rows, cols, powers, factor, probs, delta, weights_ref, score_grad_ref):
+    weights = powers * factor
+    weights_ref[slot_rows, cols] = weights.astype(jnp.bfloat16)
+    score_grad_ref[slot_rows, cols] = (weights * (probs - delta)).astype(jnp.bfloat16)
+
+
+def put_grads(weights_ref, score_grad_ref, query_rows, grad_rows, out_ref):
+    key_grad = dot(score_grad_ref[...], query_rows[...], 1, 0) * SCALE
+    value_grad = dot(weights_ref[...], grad_rows[...], 1, 0)
+    for k in range(out_ref.shape[0]):
+        out_ref[k, :BLOCK, :] = key_grad[rows_of(k), :].astype(out_ref.dtype)
+        out_ref[k, BLOCK:, :] = value_grad[rows_of(k), :].astype(out_ref.dtype)
+
+
 def late_kernel(slots, *refs):
-    half, count = slots.half, len(slots.late)
-    bias_ref, query_rows, grad_rows = refs[:3]
-    stages = [refs[3:6], refs[6:9]]
-    blocks = list(refs[9 : 9 + count])
-    sib_own_ref = refs[9 + count]
-    weights_ref, score_grad_ref, sib_out_ref, last_ref = refs[10 + count :]
+    count = len(slots.late)
+    bias_ref, query_rows, grad_rows, powers_ref, probs_ref, before_ref = refs[:6]
+    blocks = list(refs[6 : 6 + count])
+    sib_own_ref = refs[6 + count]
+    weights_ref, score_grad_ref, sib_out_ref, stats_ref, last_ref = refs[7 + count :]
     _, core = position()
 
     @pl.when(core == 0)
@@ -167,69 +187,68 @@
 
     blocks[-1] = last_ref
     keys, values = stacked(blocks, 0), stacked(blocks, 1)
+    first = slots.window - 1 - count
     for column in range(FLAT // COLS):
         cols = tile_of(column)
         scores = dot(keys, query_rows[cols, :], 1, 1)
         probs_grad = dot(values, grad_rows[cols, :], 1, 1)
-        parts = [scores[s * BLOCK : (s + 1) * BLOCK, :] for s in range(count)]
-        start = tuple(stages[-1][2][row : row + 1, cols] for row in range(3))
-        first = len(slots.middle)
+        parts = [scores[rows_of(s), :] for s in range(count)]
+        start = tuple(before_ref[row : row + 1, cols] for row in range(3))
         biases = [bias_ref[row : row + 1, cols] for row in range(first, first + count)]
         powers, top, total, mixed = absorb(parts, probs_grad, biases, *start)
         inverse = 1.0 / total
         delta = mixed * inverse
-
-        def put(slot, weights, probs):
-            rows = slots.rows(slot)
-            weights_ref[rows, cols] = weights.astype(jnp.bfloat16)
-            score_grad_ref[rows, cols] = (weights * (probs - delta)).astype(jnp.bfloat16)
-
-        for (powers_ref, probs_ref, stats_ref), group in zip(stages, (["own"], slots.middle)):
-            factor = jnp.exp2(stats_ref[0:1, cols] - top) * inverse
-            for s, slot in enumerate(group):
-                rows = slice(s * BLOCK, (s + 1) * BLOCK)
-                put(slot, powers_ref[rows, cols] * factor, probs_ref[rows, cols])
-        for s, slot in enumerate(slots.late):
-            put(slot, powers[s] * inverse, probs_grad[s * BLOCK : (s + 1) * BLOCK, :])
-
-    rows = slice(0, half * BLOCK)
-    key_grad = dot(score_grad_ref[rows, :], query_rows[...], 1, 0) * SCALE
-    value_grad = dot(weights_ref[rows, :], grad_rows[...], 1, 0)
-    for k in range(half):
-        rows = slice(k * BLOCK, (k + 1) * BLOCK)
-        sib_out_ref[k, :BLOCK, :] = key_grad[rows, :].astype(jnp.bfloat16)
-        sib_out_ref[k, BLOCK:, :] = value_grad[rows, :].astype(jnp.bfloat16)
-
-
-def mine_kernel(slots, weights_ref, score_grad_ref, query_rows, grad_rows, mine_ref):
+        for row, value in enumerate((top, inverse, delta)):
+            stats_ref[row : row + 1, cols] = value
+        factor = jnp.exp2(start[0] - top) * inverse
+        for s, slot in enumerate(slots.sibs):
+            at, rows = slots.place(slot)
+            if slot in slots.late:
+                piece = powers[slots.late.index(slot)], inverse, probs_grad[rows, :]
+            else:
+                piece = powers_ref[rows, cols], factor, probs_ref[rows, cols]
+            put_weights(rows_of(s), cols, *piece, delta, weights_ref, score_grad_ref)
+    put_grads(weights_ref, score_grad_ref, query_rows, grad_rows, sib_out_ref)
+
+
+def mine_kernel(slots, *refs):
+    query_rows, grad_rows, final_ref = refs[:3]
+    stages = [refs[3 + 3 * at : 6 + 3 * at] for at in range(3)]
+    weights_ref, score_grad_ref, mine_ref = refs[12:]
+    for column in range(FLAT // COLS):
+        cols = tile_of(column)
+        top, inverse, delta = (final_ref[row : row + 1, cols] for row in range(3))
+        factors = [jnp.exp2(stats_ref[0:1, cols] - top) * inverse for _, _, stats_ref in stages]
+        for s, slot in enumerate(slots.mine):
+            at, rows = slots.place(slot)
+            piece = stages[at][0][rows, cols], factors[at], stages[at][1][rows, cols]
+            put_weights(rows_of(s), cols, *piece, delta, weights_ref, score_grad_ref)
+    put_grads(weights_ref, score_grad_ref, query_rows, grad_rows, mine_ref)
+
+
+def query_side_kernel(slots, *refs):
+    sib_weights, sib_score_grad, mine_weights, mine_score_grad, sib_own_ref = refs[:5]
+    blocks = list(refs[5 : 5 + slots.window])
+    attended_ref, query_grad_ref, last_ref = refs[5 + slots.window :]
+    _, core = position()
     half = slots.half
-    rows = slice(half * BLOCK, slots.window * BLOCK)
-    key_grad = dot(score_grad_ref[rows, :], query_rows[...], 1, 0) * SCALE
-    value_grad = dot(weights_ref[rows, :], grad_rows[...], 1, 0)
-    for k in range(half):
-        rows = slice(k * BLOCK, (k + 1) * BLOCK)
-        mine_ref[k, :BLOCK, :] = key_grad[rows, :]
-        mine_ref[k, BLOCK:, :] = value_grad[rows, :]
-
-
-def query_side_kernel(slots, *refs):
-    weights_ref, score_grad_ref, sib_own_ref = refs[:3]
-    blocks = list(refs[3 : 3 + slots.window])
-    attended_ref, query_grad_ref, last_ref = refs[3 + slots.window :]
-    _, core = position()
-    at = slots.order.index("last")
 
     @pl.when(core == 0)
     def _():
-        last_ref[...] = blocks[at][...]
+        last_ref[...] = blocks[half - 1][...]
 
     @pl.when(core == 1)
     def _():
         last_ref[...] = sib_own_ref[...]
 
-    blocks[at] = last_ref
-    attended_t = dot(stacked(blocks, 1), weights_ref[...], 0, 0)
-    query_grad_t = dot(stacked(blocks, 0), score_grad_ref[...], 0, 0) * SCALE
+    blocks[half - 1] = last_ref
+
+    def mixed(part, sib_ref, mine_ref):
+        sib = dot(stacked(blocks[:half], part), sib_ref[...], 0, 0)
+        return sib + dot(stacked(blocks[half:], part), mine_ref[...], 0, 0)
+
+    attended_t = mixed(1, sib_weights, mine_weights)
+    query_grad_t = mixed(0, sib_score_grad, mine_score_grad) * SCALE
     for h in range(HEADS):
         rows = slice(h * BLOCK, (h + 1) * BLOCK)
         attended_ref[:, rows] = attended_t[:, rows].T.astype(jnp.bfloat16)
@@ -278,6 +297,11 @@
     def ahead(block, k):
         return lax.ppermute(block, AXES, [(i, (i + 2 * k) % devices) for i in range(devices)])
 
+    def ahead_odd(block, k, back=False):
+        route = [(i, i + 2 * k if i + 2 * k < devices else i ^ 1) for i in range(1, devices, 2)]
+        route += [(i, i - 2 * k if i >= 2 * k else i ^ 1) for i in range(0, devices, 2)]
+        return lax.ppermute(block, AXES, [pair[::-1] for pair in route] if back else route)
+
     def swapped(block):
         return lax.ppermute(block, AXES, [(i, i ^ 1) for i in range(devices)])
 
@@ -290,7 +314,7 @@
         compiler_params=small,
         name="pair_up",
     )(in_hbm(key_rows), in_hbm(value_rows))
-    lins = [ahead(own, k) for k in range(1, half + 1)]
+    lins = [ahead(own, k) for k in range(1, half)] + [ahead_odd(own, half)]
     sib_own = swapped(own)
 
     def stage(blocks):
@@ -318,17 +342,23 @@
     lins[0], own_stage[2] = lax.optimization_barrier((lins[0], own_stage[2]))
     sibs = [swapped(block) for block in lins[: half - 2]]
     held = {("lin", k): lins[k - 1] for k in range(1, half - 1)}
-    middle = len(slots.middle)
-    *middle_stage, = pl.pallas_call(
-        functools.partial(middle_kernel, slots),
-        out_shape=stage(middle),
-        in_specs=[VMEM] * (4 + middle),
-        out_specs=[VMEM] * 3,
-        compiler_params=params,
-        cost_estimate=cost(middle, 2),
-        name="middle_scores",
-    )(bias, query_rows, grad_rows, own_stage[2], *[held[slot] for slot in slots.middle])
-
+
+    def next_stage(at, before):
+        group = slots.stages[at]
+        first = sum(len(earlier) for earlier in slots.stages[1:at])
+        return list(
+            pl.pallas_call(
+                functools.partial(stage_kernel, first, len(group)),
+                out_shape=stage(len(group)),
+                in_specs=[VMEM] * (4 + len(group)),
+                out_specs=[VMEM] * 3,
+                compiler_params=params,
+                cost_estimate=cost(len(group), 2),
+                name="stage_scores",
+            )(bias, query_rows, grad_rows, before, *[held[slot] for slot in group])
+        )
+
+    middle_stage = next_stage(1, own_stage[2])
     lins[half - 2], lins[half - 1], middle_stage[2] = lax.optimization_barrier(
         (lins[half - 2], lins[half - 1], middle_stage[2])
     )
@@ -337,46 +367,44 @@
     for k in range(1, half):
         held["lin", k] = lins[k - 1]
         held["sib", k] = sibs[k - 1]
-
-    weights, score_grad, sib_out = pl.pallas_call(
+    closing_stage = next_stage(2, middle_stage[2])
+
+    weights = [pltpu.VMEM((half * BLOCK, FLAT), bf16)] * 2
+    sib_weights, sib_score_grad, sib_out, final = pl.pallas_call(
         functools.partial(late_kernel, slots),
-        out_shape=[
-            pltpu.VMEM((window * BLOCK, FLAT), bf16),
-            pltpu.VMEM((window * BLOCK, FLAT), bf16),
-            pltpu.VMEM((half, 2 * BLOCK, HEAD_DIM), bf16),
-        ],
-        in_specs=[VMEM] * (10 + len(slots.late)),
-        out_specs=[VMEM] * 3,
+        out_shape=weights + [pltpu.VMEM((half, 2 * BLOCK, HEAD_DIM), bf16), pltpu.VMEM((8, FLAT), f32)],
+        in_specs=[VMEM] * (7 + len(slots.late)),
+        out_specs=[VMEM] * 4,
         scratch_shapes=[pltpu.VMEM((2 * BLOCK, HEAD_DIM), bf16)],
         compiler_params=params,
-        cost_estimate=cost(window, 3),
+        cost_estimate=cost(window, 2),
         name="late_scores",
-    )(
-        bias, query_rows, grad_rows, *own_stage, *middle_stage,
-        *[held[slot] for slot in slots.late], sib_own,
-    )
+    )(bias, query_rows, grad_rows, *closing_stage, *[held[slot] for slot in slots.late], sib_own)
     from_sib = swapped(sib_out)
 
-    mine = pl.pallas_call(
+    mine_weights, mine_score_grad, mine = pl.pallas_call(
         functools.partial(mine_kernel, slots),
-        out_shape=pltpu.VMEM((half, 2 * BLOCK, HEAD_DIM), f32),
-        in_specs=[VMEM] * 4,
-        out_specs=VMEM,
+        out_shape=weights + [pltpu.VMEM((half, 2 * BLOCK, HEAD_DIM), f32)],
+        in_specs=[VMEM] * 12,
+        out_specs=[VMEM] * 3,
         compiler_params=params,
         cost_estimate=cost(half, 2),
         name="own_parity_grads",
-    )(weights, score_grad, query_rows, grad_rows)
+    )(query_rows, grad_rows, final, *own_stage, *middle_stage, *closing_stage)
 
     attended, query_grad = pl.pallas_call(
         functools.partial(query_side_kernel, slots),
         out_shape=[shape(queries.shape, bf16), shape(queries.shape, bf16)],
-        in_specs=[VMEM] * (3 + window),
+        in_specs=[VMEM] * (5 + window),
         out_specs=[VMEM] * 2,
         scratch_shapes=[pltpu.VMEM((2 * BLOCK, HEAD_DIM), bf16)],
         compiler_params=params,
         cost_estimate=cost(window, 2),
         name="query_side",
-    )(in_vmem(weights), in_vmem(score_grad), sib_own, *[held[slot] for slot in slots.order])
+    )(
+        *[in_vmem(part) for part in (sib_weights, sib_score_grad, mine_weights, mine_score_grad)],
+        sib_own, *[held[slot] for slot in slots.sibs + slots.mine],
+    )
 
     sent = pl.pallas_call(
         merge_kernel,

time: 31.4 us -> 29.3 us (0.933)
  starting transfers between devices: 15 us -> 13.5 us
  waiting for transfers between devices: 6.92 us -> 6.59 us
    ppermute x8 -> x7, starting transfers between devices: 13.7 us -> 12 us  [ahead(): lax.ppermute(block, AXES, [(i, (i + 2 * k) % devices) for i in range(devi...]
    ppermute x6, waiting for transfers between devices: 1.91 us -> 0.47 us  [swapped(): return lax.ppermute(block, AXES, [(i, i ^ 1) for i in range(devices)])]
    ppermute x8 -> x7, waiting for transfers between devices: 5.01 us -> 6.12 us  [ahead(): lax.ppermute(block, AXES, [(i, (i + 2 * k) % devices) for i in range(devi...]
    pallas_call x3 -> x4, Pallas kernels: 3.79 us -> 3.53 us  [the longest x2 1.38 us: next_stage(): pl.pallas_call(functools.partial(stage_kernel, first, len(group)), out_sh...]
  transfers between devices with their start and end apart: 14 -> 14, of which waited for: 7 -> 8; matrix products, arithmetic and copies ran while one was open for 0% -> 0% of each run, Pallas kernels for 14% -> 18%
where the time goes in v4:
time: 29.3 us; the launch traced here: 29 us
  starting transfers between devices  13.5 us (46%)
  Pallas kernels  8.22 us (28%)
  waiting for transfers between devices  6.59 us (22%)
  between operations  0.71 us (2%)
    ppermute x7, starting transfers between devices, ahead(): lax.ppermute(block, AXES, [(i, (i + 2 * k) % devices) for i in range(devi...  12 us
    ppermute x7, waiting for transfers between devices, ahead(): lax.ppermute(block, AXES, [(i, (i + 2 * k) % devices) for i in range(devi...  6.12 us
    pallas_call x1, Pallas kernels, local(): pl.pallas_call(functools.partial(query_side_kernel, slots), out_shape=[sh...  1.64 us
    pallas_call x1, Pallas kernels, local(): pl.pallas_call(functools.partial(own_kernel, slots), out_shape=[pltpu.VME...  1.54 us
    ppermute x6, starting transfers between devices, swapped(): return lax.ppermute(block, AXES, [(i, i ^ 1) for i in range(devices)])  1.44 us
    pallas_call x2, Pallas kernels, next_stage(): pl.pallas_call(functools.partial(stage_kernel, first, len(group)), out_sh...  1.38 us
    pallas_call x1, Pallas kernels, local(): pl.pallas_call(functools.partial(late_kernel, slots), out_shape=weights +...  1.36 us
    pallas_call x1, Pallas kernels, local(): pl.pallas_call(pair_kernel, out_shape=pltpu.VMEM((2 * BLOCK, HEAD_DIM), b...  0.79 us
  transfers between devices with their start and end apart: 14, of which 8 were waited for; matrix products, arithmetic and copies ran while one was open for 0% of the time, Pallas kernels for 18%

profile of v4, /device:TPU:0, one launch (start us, length us, event | category | flops | bytes accessed | tf_op | source)
XLA Modules:
  0.0 29.0 jit_solution(18342668848101916454)
XLA Ops:
  0.6 0.8 %pair_up.1.own_ref.refs_9_ = bf16[256,128]{1,0:T(8,128)(2,1)S(1)} custom-call(bf16[128,128]{1,0:T(8,128)(2,1)} %key_ref.1, bf16[128,128]{1,0:T(8,128)(2,1)} %value_ref.1), custom_call_target="tpu_custom_call" | custom-call | tf_op jit(solution)/shard_map/pair_up/pallas_call | solution.py:308
  1.4 3.0 %collective-permute-start.2 = (bf16[256,128]{1,0:T(8,128)(2,1)S(1)}, bf16[256,128]{1,0:T(8,128)(2,1)S(1)}, u32[]{:S(2)}, u32[]{:S(2)}) collective-permute-start(bf16[256,128]{1,0:T(8,128)(2,1)S(1)} %pair_up.1.own_ref.refs_9_), channel_id=1, source_target_pairs={{0,2},{1,3},{2,4},{3,5},{4,6},{5,7},{6,8},{7,9},{8,10},{9,11},{10,... | collective-permute-start | bytes 196616 | tf_op jit(solution)/shard_map/ppermute | solution.py:298
  4.4 1.5 %collective-permute-start.3 = (bf16[256,128]{1,0:T(8,128)(2,1)S(1)}, bf16[256,128]{1,0:T(8,128)(2,1)S(1)}, u32[]{:S(2)}, u32[]{:S(2)}) collective-permute-start(bf16[256,128]{1,0:T(8,128)(2,1)S(1)} %pair_up.1.own_ref.refs_9_), channel_id=1, source_target_pairs={{0,4},{1,5},{2,6},{3,7},{4,8},{5,9},{6,10},{7,11},{8,12},{9,13},{1... | collective-permute-start | bytes 196616 | tf_op jit(solution)/shard_map/ppermute | solution.py:298
  5.9 2.4 %collective-permute-start = (bf16[256,128]{1,0:T(8,128)(2,1)S(1)}, bf16[256,128]{1,0:T(8,128)(2,1)S(1)}, u32[]{:S(2)}, u32[]{:S(2)}) collective-permute-start(bf16[256,128]{1,0:T(8,128)(2,1)S(1)} %pair_up.1.own_ref.refs_9_), channel_id=1, source_target_pairs={{0,6},{1,7},{2,8},{3,9},{4,10},{5,11},{6,12},{7,13},{8,14},{9,15},... | collective-permute-start | bytes 196616 | tf_op jit(solution)/shard_map/ppermute | solution.py:298
  8.4 1.5 %own_scores.1 = (bf16[1024,128]{1,0:T(8,128)(2,1)S(1)}, bf16[1024,128]{1,0:T(8,128)(2,1)S(1)}, f32[8,1024]{1,0:T(8,128)S(1)}, f32[128,1024]{1,0:T(8,128)S(1)}, f...) custom-call(s32[32]{0:T(128)} %doc_hbm.1, bf16[128,1024]{1,0:T(8,128)(2,1)} %query_ref.1, bf16[128,1024]{1,0:T(8,128)(2,1)} %grad_ref.1, ...), custom_call_target="tpu_custom_call" | custom-call | flops 67108864 | bytes 524288 | tf_op jit(solution)/shard_map/own_scores/pallas_call | solution.py:327
  9.9 1.7 %collective-permute-done.2.refs_4_.refs_10_ = bf16[256,128]{1,0:T(8,128)(2,1)S(1)} collective-permute-done((bf16[256,128]{1,0:T(8,128)(2,1)S(1)}, bf16[256,128]{1,0:T(8,128)(2,1)S(1)}, u32[]{:S(2)}, u32[]{:S(2)}) %collective-permute-start.2) | collective-permute-done | bytes 65568 | tf_op jit(solution)/shard_map/ppermute | solution.py:298
  11.6 0.3 %collective-permute-done.3.refs_5_.refs_11_ = bf16[256,128]{1,0:T(8,128)(2,1)S(1)} collective-permute-done((bf16[256,128]{1,0:T(8,128)(2,1)S(1)}, bf16[256,128]{1,0:T(8,128)(2,1)S(1)}, u32[]{:S(2)}, u32[]{:S(2)}) %collective-permute-start.3) | collective-permute-done | bytes 65568 | tf_op jit(solution)/shard_map/ppermute | solution.py:298
  11.9 0.5 %collective-permute-start.4 = (bf16[256,128]{1,0:T(8,128)(2,1)S(1)}, bf16[256,128]{1,0:T(8,128)(2,1)S(1)}, u32[]{:S(2)}, u32[]{:S(2)}) collective-permute-start(bf16[256,128]{1,0:T(8,128)(2,1)S(1)} %collective-permute-done.2.refs_4_.refs_10_), channel_id=1, source_target_pairs={{0,1},{1,0},{2,3},{3,2},{4,5},{5,4},{6,7},{7,6},{8,9},{9,8},{10,11... | collective-permute-start | bytes 196616 | tf_op jit(solution)/shard_map/ppermute | solution.py:306
  12.4 0.6 %stage_scores.2 = (f32[256,1024]{1,0:T(8,128)S(1)}, f32[256,1024]{1,0:T(8,128)S(1)}, f32[8,1024]{1,0:T(8,128)S(1)}) custom-call(f32[8,1024]{1,0:T(8,128)S(1)} %get-tuple-element.36.refs_0_, bf16[1024,128]{1,0:T(8,128)(2,1)S(1)} %get-tuple-element.37.refs_1_.refs_0_, bf16[1024,128]{1,0:T(8,128)(2,1)S(1)} %get-tuple-element.38.refs_2_.refs_1_, ...), custom_call_target="tpu_custom_call" | custom-call | flops 134217728 | bytes 1048576 | tf_op jit(solution)/shard_map/stage_scores/pallas_call | solution.py:350
  13.0 0.9 %collective-permute-done.refs_6_.refs_12_ = bf16[256,128]{1,0:T(8,128)(2,1)S(1)} collective-permute-done((bf16[256,128]{1,0:T(8,128)(2,1)S(1)}, bf16[256,128]{1,0:T(8,128)(2,1)S(1)}, u32[]{:S(2)}, u32[]{:S(2)}) %collective-permute-start) | collective-permute-done | bytes 65568 | tf_op jit(solution)/shard_map/ppermute | solution.py:298
  13.9 0.5 %collective-permute-start.6 = (bf16[256,128]{1,0:T(8,128)(2,1)S(1)}, bf16[256,128]{1,0:T(8,128)(2,1)S(1)}, u32[]{:S(2)}, u32[]{:S(2)}) collective-permute-start(bf16[256,128]{1,0:T(8,128)(2,1)S(1)} %collective-permute-done.refs_6_.refs_12_), channel_id=1, source_target_pairs={{0,1},{1,0},{2,3},{3,2},{4,5},{5,4},{6,7},{7,6},{8,9},{9,8},{10,11... | collective-permute-start | bytes 196616 | tf_op jit(solution)/shard_map/ppermute | solution.py:306
  14.4 0.8 %stage_scores.3 = (f32[384,1024]{1,0:T(8,128)S(1)}, f32[384,1024]{1,0:T(8,128)S(1)}, f32[8,1024]{1,0:T(8,128)S(1)}) custom-call(f32[8,1024]{1,0:T(8,128)S(1)} %get-tuple-element.36.refs_0_, bf16[1024,128]{1,0:T(8,128)(2,1)S(1)} %get-tuple-element.37.refs_1_.refs_0_, bf16[1024,128]{1,0:T(8,128)(2,1)S(1)} %get-tuple-element.38.refs_2_.refs_1_, ...), custom_call_target="tpu_custom_call" | custom-call | flops 201326592 | bytes 1572864 | tf_op jit(solution)/shard_map/stage_scores/pallas_call | solution.py:350
  15.3 1.4 %late_scores.1 = (bf16[512,1024]{1,0:T(8,128)(2,1)S(1)}, bf16[512,1024]{1,0:T(8,128)(2,1)S(1)}, bf16[4,256,128]{2,1,0:T(8,128)(2,1)S(1)}, f32[8,1024]{1,0:T(8,128)S(1)}) custom-call(f32[8,1024]{1,0:T(8,128)S(1)} %get-tuple-element.36.refs_0_, bf16[1024,128]{1,0:T(8,128)(2,1)S(1)} %get-tuple-element.37.refs_1_.refs_0_, ...), custom_call_target="tpu_custom_call" | custom-call | flops 536870912 | bytes 4194304 | tf_op jit(solution)/shard_map/late_scores/pallas_call | solution.py:373
  16.7 0.4 %collective-permute-start.9 = (bf16[4,256,128]{2,1,0:T(8,128)(2,1)S(1)}, bf16[4,256,128]{2,1,0:T(8,128)(2,1)S(1)}, u32[]{:S(2)}, u32[]{:S(2)}) collective-permute-start(bf16[4,256,128]{2,1,0:T(8,128)(2,1)S(1)} %get-tuple-element.61), channel_id=1, source_target_pairs={{0,1},{1,0},{2,3},{3,2},{4,5},{5,4},{6,7},{7,6},{8,9},{9,8},{10,11... | collective-permute-start | bytes 786440 | tf_op jit(solution)/shard_map/ppermute | solution.py:306
  17.1 0.8 %own_parity_grads.1 = (bf16[512,1024]{1,0:T(8,128)(2,1)S(1)}, bf16[512,1024]{1,0:T(8,128)(2,1)S(1)}, f32[4,256,128]{2,1,0:T(8,128)S(1)}) custom-call(bf16[1024,128]{1,0:T(8,128)(2,1)S(1)} %get-tuple-element.37.refs_1_.refs_0_, bf16[1024,128]{1,0:T(8,128)(2,1)S(1)} %get-tuple-element.38.refs_2_.refs_1_, f32[8,1024]{1,0:T(8,128)S(1)} %get-tuple-element.51.refs_2_, ...), custom_call_target="tpu_custom_call" | custom-call | flops 268435456 | bytes 2097152 | tf_op jit(solution)/shard_map/own_parity_grads/pallas_call | solution.py:385
  17.9 0.4 %collective-permute-done.9.from_sib_ref = bf16[4,256,128]{2,1,0:T(8,128)(2,1)S(1)} collective-permute-done((bf16[4,256,128]{2,1,0:T(8,128)(2,1)S(1)}, bf16[4,256,128]{2,1,0:T(8,128)(2,1)S(1)}, u32[]{:S(2)}, u32[]{:S(2)}) %collective-permute-start.9) | collective-permute-done | bytes 262176 | tf_op jit(solution)/shard_map/ppermute | solution.py:306
  18.3 3.2 %collective-permute-start.10 = (bf16[256,128]{1,0:T(8,128)(2,1)S(1)}, bf16[256,128]{1,0:T(8,128)(2,1)S(1)}, u32[]{:S(2)}, u32[]{:S(2)}) collective-permute-start(bf16[256,128]{1,0:T(8,128)(2,1)S(1)} %get-tuple-element.62), channel_id=1, source_target_pairs={{0,30},{1,31},{2,0},{3,1},{4,2},{5,3},{6,4},{7,5},{8,6},{9,7},{10,... | collective-permute-start | bytes 196616 | tf_op jit(solution)/shard_map/ppermute | solution.py:298
  21.5 1.4 %collective-permute-start.11 = (bf16[256,128]{1,0:T(8,128)(2,1)S(1)}, bf16[256,128]{1,0:T(8,128)(2,1)S(1)}, u32[]{:S(2)}, u32[]{:S(2)}) collective-permute-start(bf16[256,128]{1,0:T(8,128)(2,1)S(1)} %get-tuple-element.63), channel_id=1, source_target_pairs={{0,28},{1,29},{2,30},{3,31},{4,0},{5,1},{6,2},{7,3},{8,4},{9,5},{1... | collective-permute-start | bytes 196616 | tf_op jit(solution)/shard_map/ppermute | solution.py:298
  23.0 0.4 %collective-permute-start.13 = (bf16[256,128]{1,0:T(8,128)(2,1)S(1)}, bf16[256,128]{1,0:T(8,128)(2,1)S(1)}, u32[]{:S(2)}, u32[]{:S(2)}) collective-permute-start(bf16[256,128]{1,0:T(8,128)(2,1)S(1)} %get-tuple-element.65), channel_id=1, source_target_pairs={{0,24},{1,25},{2,26},{3,27},{4,28},{5,29},{6,30},{7,31},{8,0},{9,1... | collective-permute-start | bytes 196616 | tf_op jit(solution)/shard_map/ppermute | solution.py:298
  23.4 1.6 %query_side.1 = (bf16[128,1024]{1,0:T(8,128)(2,1)}, bf16[128,1024]{1,0:T(8,128)(2,1)}) custom-call(bf16[512,1024]{1,0:T(8,128)(2,1)S(1)} %get-tuple-element.49.refs_0_, bf16[512,1024]{1,0:T(8,128)(2,1)S(1)} %get-tuple-element.50.refs_1_, bf16[512,1024]{1,0:T(8,128)(2,1)S(1)} %get-tuple-element.56.refs_2_, bf16[512,1024]{1,0:T(8,128)(2,1)S(1)} %get-tuple-element.57.refs_3_, ...), custom_call_target="tpu_custom_call" | custom-call | flops 536870912 | bytes 4194304 | tf_op jit(solution)/shard_map/query_side/pallas_call | solution.py:395
  25.1 0.7 %collective-permute-done.11.refs_1_ = bf16[256,128]{1,0:T(8,128)(2,1)S(1)} collective-permute-done((bf16[256,128]{1,0:T(8,128)(2,1)S(1)}, bf16[256,128]{1,0:T(8,128)(2,1)S(1)}, u32[]{:S(2)}, u32[]{:S(2)}) %collective-permute-start.11) | collective-permute-done | bytes 65568 | tf_op jit(solution)/shard_map/ppermute | solution.py:298
  25.8 2.3 %collective-permute-done.12.refs_2_ = bf16[256,128]{1,0:T(8,128)(2,1)S(1)} collective-permute-done((bf16[256,128]{1,0:T(8,128)(2,1)S(1)}, bf16[256,128]{1,0:T(8,128)(2,1)S(1)}, u32[]{:S(2)}, u32[]{:S(2)}) %collective-permute-start.12) | collective-permute-done | bytes 65568 | tf_op jit(solution)/shard_map/ppermute | solution.py:298
  28.1 0.2 collective-permute-done.13.refs_3_
  28.3 0.7 %total_grads.1 = (bf16[128,128]{1,0:T(8,128)(2,1)}, bf16[128,128]{1,0:T(8,128)(2,1)}) custom-call(f32[4,256,128]{2,1,0:T(8,128)S(1)} %get-tuple-element.60.mine_ref, bf16[4,256,128]{2,1,0:T(8,128)(2,1)S(1)} %collective-permute-done.9.from_sib_ref, bf16[256,128]{1,0:T(8,128)(2,1)S(1)} %collective-permute-done.10.refs_0_, ...), custom_call_target="tpu_custom_call" | custom-call | tf_op jit(solution)/shard_map/total_grads/pallas_call | solution.py:418
  (13 shorter events, 0.2 us)
Async XLA Ops:
  1.4 10.2 %collective-permute-start.2 = (bf16[256,128]{1,0:T(8,128)(2,1)S(1)}, bf16[256,128]{1,0:T(8,128)(2,1)S(1)}, u32[]{:S(2)}, u32[]{:S(2)}) collective-permute-start(bf16[256,128]{1,0:T(8,128)(2,1)S(1)} %pair_up.1.own_ref.refs_9_), channel_id=1, source_target_pairs={{0,2},{1,3},{2,4},{3,5},{4,6},{5,7},{6,8},{7,9},{8,10},{9,11},{10,... | collective-permute-start | bytes 196616 | tf_op jit(solution)/shard_map/ppermute | solution.py:298
  4.4 7.5 %collective-permute-start.3 = (bf16[256,128]{1,0:T(8,128)(2,1)S(1)}, bf16[256,128]{1,0:T(8,128)(2,1)S(1)}, u32[]{:S(2)}, u32[]{:S(2)}) collective-permute-start(bf16[256,128]{1,0:T(8,128)(2,1)S(1)} %pair_up.1.own_ref.refs_9_), channel_id=1, source_target_pairs={{0,4},{1,5},{2,6},{3,7},{4,8},{5,9},{6,10},{7,11},{8,12},{9,13},{1... | collective-permute-start | bytes 196616 | tf_op jit(solution)/shard_map/ppermute | solution.py:298
  5.9 7.1 %collective-permute-start.1 = (bf16[256,128]{1,0:T(8,128)(2,1)S(1)}, bf16[256,128]{1,0:T(8,128)(2,1)S(1)}, u32[]{:S(2)}, u32[]{:S(2)}) collective-permute-start(bf16[256,128]{1,0:T(8,128)(2,1)S(1)} %pair_up.1.own_ref.refs_9_), channel_id=1, source_target_pairs={{1,9},{3,11},{5,13},{7,15},{9,17},{11,19},{13,21},{15,23},{17,25},... | collective-permute-start | bytes 196616 | tf_op jit(solution)/shard_map/ppermute | solution.py:303
  5.9 8.0 %collective-permute-start = (bf16[256,128]{1,0:T(8,128)(2,1)S(1)}, bf16[256,128]{1,0:T(8,128)(2,1)S(1)}, u32[]{:S(2)}, u32[]{:S(2)}) collective-permute-start(bf16[256,128]{1,0:T(8,128)(2,1)S(1)} %pair_up.1.own_ref.refs_9_), channel_id=1, source_target_pairs={{0,6},{1,7},{2,8},{3,9},{4,10},{5,11},{6,12},{7,13},{8,14},{9,15},... | collective-permute-start | bytes 196616 | tf_op jit(solution)/shard_map/ppermute | solution.py:298
  11.9 2.5 %collective-permute-start.5 = (bf16[256,128]{1,0:T(8,128)(2,1)S(1)}, bf16[256,128]{1,0:T(8,128)(2,1)S(1)}, u32[]{:S(2)}, u32[]{:S(2)}) collective-permute-start(bf16[256,128]{1,0:T(8,128)(2,1)S(1)} %collective-permute-done.3.refs_5_.refs_11_), channel_id=1, source_target_pairs={{0,1},{1,0},{2,3},{3,2},{4,5},{5,4},{6,7},{7,6},{8,9},{9,8},{10,11... | collective-permute-start | bytes 196616 | tf_op jit(solution)/shard_map/ppermute | solution.py:306
  11.9 2.5 %collective-permute-start.4 = (bf16[256,128]{1,0:T(8,128)(2,1)S(1)}, bf16[256,128]{1,0:T(8,128)(2,1)S(1)}, u32[]{:S(2)}, u32[]{:S(2)}) collective-permute-start(bf16[256,128]{1,0:T(8,128)(2,1)S(1)} %collective-permute-done.2.refs_4_.refs_10_), channel_id=1, source_target_pairs={{0,1},{1,0},{2,3},{3,2},{4,5},{5,4},{6,7},{7,6},{8,9},{9,8},{10,11... | collective-permute-start | bytes 196616 | tf_op jit(solution)/shard_map/ppermute | solution.py:306
  12.4 2.8 %collective-permute-start.8 = (bf16[256,128]{1,0:T(8,128)(2,1)S(1)}, bf16[256,128]{1,0:T(8,128)(2,1)S(1)}, u32[]{:S(2)}, u32[]{:S(2)}) collective-permute-start(bf16[256,128]{1,0:T(8,128)(2,1)S(1)} %pair_up.1.own_ref.refs_9_), channel_id=1, source_target_pairs={{0,1},{1,0},{2,3},{3,2},{4,5},{5,4},{6,7},{7,6},{8,9},{9,8},{10,11... | collective-permute-start | bytes 196616 | tf_op jit(solution)/shard_map/ppermute | solution.py:306
  13.9 1.3 %collective-permute-start.7 = (bf16[256,128]{1,0:T(8,128)(2,1)S(1)}, bf16[256,128]{1,0:T(8,128)(2,1)S(1)}, u32[]{:S(2)}, u32[]{:S(2)}) collective-permute-start(bf16[256,128]{1,0:T(8,128)(2,1)S(1)} %collective-permute-done.1), channel_id=1, source_target_pairs={{0,1},{1,0},{2,3},{3,2},{4,5},{5,4},{6,7},{7,6},{8,9},{9,8},{10,11... | collective-permute-start | bytes 196616 | tf_op jit(solution)/shard_map/ppermute | solution.py:306
  13.9 1.4 %collective-permute-start.6 = (bf16[256,128]{1,0:T(8,128)(2,1)S(1)}, bf16[256,128]{1,0:T(8,128)(2,1)S(1)}, u32[]{:S(2)}, u32[]{:S(2)}) collective-permute-start(bf16[256,128]{1,0:T(8,128)(2,1)S(1)} %collective-permute-done.refs_6_.refs_12_), channel_id=1, source_target_pairs={{0,1},{1,0},{2,3},{3,2},{4,5},{5,4},{6,7},{7,6},{8,9},{9,8},{10,11... | collective-permute-start | bytes 196616 | tf_op jit(solution)/shard_map/ppermute | solution.py:306
  16.7 1.6 %collective-permute-start.9 = (bf16[4,256,128]{2,1,0:T(8,128)(2,1)S(1)}, bf16[4,256,128]{2,1,0:T(8,128)(2,1)S(1)}, u32[]{:S(2)}, u32[]{:S(2)}) collective-permute-start(bf16[4,256,128]{2,1,0:T(8,128)(2,1)S(1)} %get-tuple-element.61), channel_id=1, source_target_pairs={{0,1},{1,0},{2,3},{3,2},{4,5},{5,4},{6,7},{7,6},{8,9},{9,8},{10,11... | collective-permute-start | bytes 786440 | tf_op jit(solution)/shard_map/ppermute | solution.py:306
  18.3 6.7 %collective-permute-start.10 = (bf16[256,128]{1,0:T(8,128)(2,1)S(1)}, bf16[256,128]{1,0:T(8,128)(2,1)S(1)}, u32[]{:S(2)}, u32[]{:S(2)}) collective-permute-start(bf16[256,128]{1,0:T(8,128)(2,1)S(1)} %get-tuple-element.62), channel_id=1, source_target_pairs={{0,30},{1,31},{2,0},{3,1},{4,2},{5,3},{6,4},{7,5},{8,6},{9,7},{10,... | collective-permute-start | bytes 196616 | tf_op jit(solution)/shard_map/ppermute | solution.py:298
  21.5 4.3 %collective-permute-start.11 = (bf16[256,128]{1,0:T(8,128)(2,1)S(1)}, bf16[256,128]{1,0:T(8,128)(2,1)S(1)}, u32[]{:S(2)}, u32[]{:S(2)}) collective-permute-start(bf16[256,128]{1,0:T(8,128)(2,1)S(1)} %get-tuple-element.63), channel_id=1, source_target_pairs={{0,28},{1,29},{2,30},{3,31},{4,0},{5,1},{6,2},{7,3},{8,4},{9,5},{1... | collective-permute-start | bytes 196616 | tf_op jit(solution)/shard_map/ppermute | solution.py:298
  22.9 5.2 %collective-permute-start.12 = (bf16[256,128]{1,0:T(8,128)(2,1)S(1)}, bf16[256,128]{1,0:T(8,128)(2,1)S(1)}, u32[]{:S(2)}, u32[]{:S(2)}) collective-permute-start(bf16[256,128]{1,0:T(8,128)(2,1)S(1)} %get-tuple-element.64), channel_id=1, source_target_pairs={{0,26},{1,27},{2,28},{3,29},{4,30},{5,31},{6,0},{7,1},{8,2},{9,3},... | collective-permute-start | bytes 196616 | tf_op jit(solution)/shard_map/ppermute | solution.py:298
  23.0 5.4 %collective-permute-start.13 = (bf16[256,128]{1,0:T(8,128)(2,1)S(1)}, bf16[256,128]{1,0:T(8,128)(2,1)S(1)}, u32[]{:S(2)}, u32[]{:S(2)}) collective-permute-start(bf16[256,128]{1,0:T(8,128)(2,1)S(1)} %get-tuple-element.65), channel_id=1, source_target_pairs={{0,24},{1,25},{2,26},{3,27},{4,28},{5,29},{6,30},{7,31},{8,0},{9,1... | collective-permute-start | bytes 196616 | tf_op jit(solution)/shard_map/ppermute | solution.py:298

commit v5 on v4

--- a/solution.py
+++ b/solution.py
@@ -37,34 +37,38 @@
     def __init__(self, window):
         self.window = window
         self.half = half = window // 2
-        lins = [("lin", k) for k in range(1, half)]
-        sibs = [("sib", k) for k in range(1, half)]
+        self.arrival = list(range(1, half))
+        lins = [("lin", k) for k in self.arrival]
+        sibs = [("sib", k) for k in self.arrival]
         self.middle = lins[:-1]
         self.closing = sibs[:-1] + lins[-1:]
         self.late = [sibs[-1], "last"]
         self.stages = [["own"], self.middle, self.closing, self.late]
-        self.sibs = sibs + ["last"]
-        self.mine = ["own"] + lins
+        self.sibs = [("sib", k) for k in range(1, half)] + ["last"]
+        self.mine = ["own"] + [("lin", k) for k in range(1, half)]
 
     def place(self, slot):
         for at, group in enumerate(self.stages):
             if slot in group:
                 return at, rows_of(group.index(slot))
 
-    def distance(self, slot, core):
+    def distance(self, slot):
+        _, chip, core = position()
         if slot == "last":
             return jnp.where(core == 0, self.window - 1, 1)
-        return 2 * slot[1] if slot[0] == "lin" else 2 * slot[1] - 1 + 2 * core
+        kind, m = slot
+        chips = lax.rem(chip - lax.bitwise_xor(chip, m) + self.half, self.half)
+        return 2 * chips if kind == "lin" else 2 * chips - 1 + 2 * core
 
 
 def position():
-    me = lax.axis_index("pb") * lax.axis_size("kv") + lax.axis_index("kv")
-    return me, lax.rem(me, 2)
+    column = lax.axis_index("kv")
+    return lax.axis_index("pb") * lax.axis_size("kv") + column, column // 2, lax.rem(column, 2)
 
 
 def reached(doc_ref, slots, slot):
-    me, core = position()
-    at = me - slots.distance(slot, core)
+    me, _, _ = position()
+    at = me - slots.distance(slot)
     return (at >= 0) & (doc_ref[jnp.maximum(at, 0)] == doc_ref[me])
 
 
@@ -175,7 +179,7 @@
     blocks = list(refs[6 : 6 + count])
     sib_own_ref = refs[6 + count]
     weights_ref, score_grad_ref, sib_out_ref, stats_ref, last_ref = refs[7 + count :]
-    _, core = position()
+    _, _, core = position()
 
     @pl.when(core == 0)
     def _():
@@ -230,7 +234,7 @@
     sib_weights, sib_score_grad, mine_weights, mine_score_grad, sib_own_ref = refs[:5]
     blocks = list(refs[5 : 5 + slots.window])
     attended_ref, query_grad_ref, last_ref = refs[5 + slots.window :]
-    _, core = position()
+    _, _, core = position()
     half = slots.half
 
     @pl.when(core == 0)
@@ -258,16 +262,20 @@
 def merge_kernel(mine_ref, from_sib_ref, *sent_refs):
     for k, ref in enumerate(sent_refs[:-1]):
         ref[...] = (mine_ref[k + 1] + from_sib_ref[k].astype(jnp.float32)).astype(jnp.bfloat16)
-    sent_refs[-1][...] = from_sib_ref[len(sent_refs) - 1]
-
-
-def total_kernel(mine_ref, from_sib_ref, *refs):
+    _, _, core = position()
+    far = from_sib_ref[len(sent_refs) - 1]
+    sent_refs[-1][...] = jnp.where(core == 1, far, jnp.zeros_like(far))
+
+
+def total_kernel(order, mine_ref, from_sib_ref, *refs):
     back, (key_ref, value_ref) = refs[:-2], refs[-2:]
-    _, core = position()
-    near = from_sib_ref[len(back) - 1].astype(jnp.float32)
-    total = mine_ref[0] + jnp.where(core == 0, near, back[-1][...].astype(jnp.float32))
-    for ref in back[:-1]:
-        total = total + ref[...].astype(jnp.float32)
+    _, _, core = position()
+    half = len(order)
+    near = from_sib_ref[half - 1].astype(jnp.float32)
+    total = mine_ref[0] + jnp.where(core == 0, near, back[order.index(half)][...].astype(jnp.float32))
+    for k, ref in zip(order, back):
+        if k < half:
+            total = total + ref[...].astype(jnp.float32)
     key_ref[...] = total[:BLOCK].astype(jnp.bfloat16)
     value_ref[...] = total[BLOCK:].astype(jnp.bfloat16)
 
@@ -294,8 +302,16 @@
     small = pltpu.CompilerParams(vmem_limit_bytes=window * MIB // 4)
     params = pltpu.CompilerParams(vmem_limit_bytes=window * MIB)
 
-    def ahead(block, k):
-        return lax.ppermute(block, AXES, [(i, (i + 2 * k) % devices) for i in range(devices)])
+    def ahead(block, m, back=False):
+        top = 1 << (m.bit_length() - 1)
+        route = []
+        for i in range(devices):
+            run, chip, core = i // window, i // 2 % half, i % 2
+            run, to = (run, chip ^ m) if not chip & top else (run + 1, chip ^ m)
+            if run * window == devices:
+                run, to = 0, chip ^ top
+            route.append((i, run * window + 2 * to + core))
+        return lax.ppermute(block, AXES, [pair[::-1] for pair in route] if back else route)
 
     def ahead_odd(block, k, back=False):
         route = [(i, i + 2 * k if i + 2 * k < devices else i ^ 1) for i in range(1, devices, 2)]
@@ -314,7 +330,7 @@
         compiler_params=small,
         name="pair_up",
     )(in_hbm(key_rows), in_hbm(value_rows))
-    lins = [ahead(own, k) for k in range(1, half)] + [ahead_odd(own, half)]
+    lins = [ahead(own, k) for k in slots.arrival] + [ahead_odd(own, half)]
     sib_own = swapped(own)
 
     def stage(blocks):
@@ -341,7 +357,7 @@
 
     lins[0], own_stage[2] = lax.optimization_barrier((lins[0], own_stage[2]))
     sibs = [swapped(block) for block in lins[: half - 2]]
-    held = {("lin", k): lins[k - 1] for k in range(1, half - 1)}
+    held = {("lin", k): block for k, block in zip(slots.arrival[:-1], lins)}
 
     def next_stage(at, before):
         group = slots.stages[at]
@@ -359,14 +375,14 @@
         )
 
     middle_stage = next_stage(1, own_stage[2])
-    lins[half - 2], lins[half - 1], middle_stage[2] = lax.optimization_barrier(
-        (lins[half - 2], lins[half - 1], middle_stage[2])
+    lins[half - 1], lins[half - 2], middle_stage[2] = lax.optimization_barrier(
+        (lins[half - 1], lins[half - 2], middle_stage[2])
     )
     sibs += [swapped(block) for block in lins[half - 2 :]]
     held |= {"own": own, "last": sibs[-1]}
-    for k in range(1, half):
-        held["lin", k] = lins[k - 1]
-        held["sib", k] = sibs[k - 1]
+    for k, block, swap in zip(slots.arrival, lins, sibs):
+        held["lin", k] = block
+        held["sib", k] = swap
     closing_stage = next_stage(2, middle_stage[2])
 
     weights = [pltpu.VMEM((half * BLOCK, FLAT), bf16)] * 2
@@ -414,9 +430,12 @@
         compiler_params=small,
         name="merge_siblings",
     )(mine, from_sib)
-    back = [ahead(block, -(k + 1)) for k, block in enumerate(sent)]
+    order = list(range(half, 0, -1))[1:] + [half]
+    back = [
+        ahead(sent[k - 1], k, back=True) if k < half else ahead_odd(sent[k - 1], half, back=True) for k in order
+    ]
     key_grad, value_grad = pl.pallas_call(
-        total_kernel,
+        functools.partial(total_kernel, order),
         out_shape=[shape((BLOCK, HEAD_DIM), bf16)] * 2,
         in_specs=[VMEM] * (2 + half),
         out_specs=[VMEM] * 2,

time: 29.3 us -> 27.5 us (0.939)
  waiting for transfers between devices: 6.59 us -> 3.11 us
  starting transfers between devices: 13.5 us -> 15.1 us
    ppermute x7 -> x6, waiting for transfers between devices: 6.12 us -> 1.92 us  [ahead(): lax.ppermute(block, AXES, [pair[::-1] for pair in route] if back else route)]
    ppermute x1 -> x2, starting transfers between devices: 0.01 us -> 1.15 us  [ahead_odd(): lax.ppermute(block, AXES, [pair[::-1] for pair in route] if back else route)]
    ppermute x7 -> x6, starting transfers between devices: 12 us -> 12.6 us  [ahead(): lax.ppermute(block, AXES, [pair[::-1] for pair in route] if back else route)]
    ppermute x6, waiting for transfers between devices: 0.47 us -> 0.94 us  [swapped(): return lax.ppermute(block, AXES, [(i, i ^ 1) for i in range(devices)])]
  transfers between devices with their start and end apart: 14 -> 14, of which waited for: 8 -> 4; matrix products, arithmetic and copies ran while one was open for 0% -> 0% of each run, Pallas kernels for 18% -> 20%
where the time goes in v5:
time: 27.5 us; the launch traced here: 27.2 us
  starting transfers between devices  15.1 us (55%)
  Pallas kernels  8.22 us (30%)
  waiting for transfers between devices  3.11 us (11%)
  between operations  0.73 us (3%)
    ppermute x6, starting transfers between devices, ahead(): lax.ppermute(block, AXES, [pair[::-1] for pair in route] if back else route)  12.6 us
    ppermute x6, waiting for transfers between devices, ahead(): lax.ppermute(block, AXES, [pair[::-1] for pair in route] if back else route)  1.92 us
    pallas_call x1, Pallas kernels, local(): pl.pallas_call(functools.partial(query_side_kernel, slots), out_shape=[sh...  1.64 us
    pallas_call x1, Pallas kernels, local(): pl.pallas_call(functools.partial(own_kernel, slots), out_shape=[pltpu.VME...  1.54 us
    ppermute x6, starting transfers between devices, swapped(): return lax.ppermute(block, AXES, [(i, i ^ 1) for i in range(devices)])  1.38 us
    pallas_call x2, Pallas kernels, next_stage(): pl.pallas_call(functools.partial(stage_kernel, first, len(group)), out_sh...  1.38 us
    pallas_call x1, Pallas kernels, local(): pl.pallas_call(functools.partial(late_kernel, slots), out_shape=weights +...  1.36 us
    ppermute x2, starting transfers between devices, ahead_odd(): lax.ppermute(block, AXES, [pair[::-1] for pair in route] if back else route)  1.15 us
  transfers between devices with their start and end apart: 14, of which 4 were waited for; matrix products, arithmetic and copies ran while one was open for 0% of the time, Pallas kernels for 20%

profile of v5, /device:TPU:0, one launch (start us, length us, event | category | flops | bytes accessed | tf_op | source)
XLA Modules:
  0.0 27.2 jit_solution(10106130116230265497)
XLA Ops:
  0.6 0.8 %pair_up.1.own_ref.refs_9_ = bf16[256,128]{1,0:T(8,128)(2,1)S(1)} custom-call(bf16[128,128]{1,0:T(8,128)(2,1)} %key_ref.1, bf16[128,128]{1,0:T(8,128)(2,1)} %value_ref.1), custom_call_target="tpu_custom_call" | custom-call | tf_op jit(solution)/shard_map/pair_up/pallas_call | solution.py:324
  1.4 3.0 %collective-permute-start.2 = (bf16[256,128]{1,0:T(8,128)(2,1)S(1)}, bf16[256,128]{1,0:T(8,128)(2,1)S(1)}, u32[]{:S(2)}, u32[]{:S(2)}) collective-permute-start(bf16[256,128]{1,0:T(8,128)(2,1)S(1)} %pair_up.1.own_ref.refs_9_), channel_id=1, source_target_pairs={{0,2},{1,3},{2,8},{3,9},{4,6},{5,7},{6,12},{7,13},{8,10},{9,11},{1... | collective-permute-start | bytes 196616 | tf_op jit(solution)/shard_map/ppermute | solution.py:314
  4.4 1.5 %collective-permute-start.3 = (bf16[256,128]{1,0:T(8,128)(2,1)S(1)}, bf16[256,128]{1,0:T(8,128)(2,1)S(1)}, u32[]{:S(2)}, u32[]{:S(2)}) collective-permute-start(bf16[256,128]{1,0:T(8,128)(2,1)S(1)} %pair_up.1.own_ref.refs_9_), channel_id=1, source_target_pairs={{0,4},{1,5},{2,6},{3,7},{4,8},{5,9},{6,10},{7,11},{8,12},{9,13},{1... | collective-permute-start | bytes 196616 | tf_op jit(solution)/shard_map/ppermute | solution.py:314
  5.9 2.5 %collective-permute-start.1 = (bf16[256,128]{1,0:T(8,128)(2,1)S(1)}, bf16[256,128]{1,0:T(8,128)(2,1)S(1)}, u32[]{:S(2)}, u32[]{:S(2)}) collective-permute-start(bf16[256,128]{1,0:T(8,128)(2,1)S(1)} %pair_up.1.own_ref.refs_9_), channel_id=1, source_target_pairs={{0,6},{1,7},{2,4},{3,5},{4,10},{5,11},{6,8},{7,9},{8,14},{9,15},{1... | collective-permute-start | bytes 196616 | tf_op jit(solution)/shard_map/ppermute | solution.py:314
  8.4 1.5 %own_scores.1 = (bf16[1024,128]{1,0:T(8,128)(2,1)S(1)}, bf16[1024,128]{1,0:T(8,128)(2,1)S(1)}, f32[8,1024]{1,0:T(8,128)S(1)}, f32[128,1024]{1,0:T(8,128)S(1)}, f...) custom-call(s32[32]{0:T(128)} %doc_hbm.1, bf16[128,1024]{1,0:T(8,128)(2,1)} %query_ref.1, bf16[128,1024]{1,0:T(8,128)(2,1)} %grad_ref.1, ...), custom_call_target="tpu_custom_call" | custom-call | flops 67108864 | bytes 524288 | tf_op jit(solution)/shard_map/own_scores/pallas_call | solution.py:343
  10.0 1.9 %collective-permute-done.3.refs_5_.refs_11_ = bf16[256,128]{1,0:T(8,128)(2,1)S(1)} collective-permute-done((bf16[256,128]{1,0:T(8,128)(2,1)S(1)}, bf16[256,128]{1,0:T(8,128)(2,1)S(1)}, u32[]{:S(2)}, u32[]{:S(2)}) %collective-permute-start.3) | collective-permute-done | bytes 65568 | tf_op jit(solution)/shard_map/ppermute | solution.py:314
  11.9 0.5 %collective-permute-start.4 = (bf16[256,128]{1,0:T(8,128)(2,1)S(1)}, bf16[256,128]{1,0:T(8,128)(2,1)S(1)}, u32[]{:S(2)}, u32[]{:S(2)}) collective-permute-start(bf16[256,128]{1,0:T(8,128)(2,1)S(1)} %collective-permute-done.2.refs_4_.refs_10_), channel_id=1, source_target_pairs={{0,1},{1,0},{2,3},{3,2},{4,5},{5,4},{6,7},{7,6},{8,9},{9,8},{10,11... | collective-permute-start | bytes 196616 | tf_op jit(solution)/shard_map/ppermute | solution.py:322
  12.4 0.0 collective-permute-start.8
  12.4 0.6 %stage_scores.2 = (f32[256,1024]{1,0:T(8,128)S(1)}, f32[256,1024]{1,0:T(8,128)S(1)}, f32[8,1024]{1,0:T(8,128)S(1)}) custom-call(f32[8,1024]{1,0:T(8,128)S(1)} %get-tuple-element.36.refs_0_, bf16[1024,128]{1,0:T(8,128)(2,1)S(1)} %get-tuple-element.37.refs_1_.refs_0_, bf16[1024,128]{1,0:T(8,128)(2,1)S(1)} %get-tuple-element.38.refs_2_.refs_1_, ...), custom_call_target="tpu_custom_call" | custom-call | flops 134217728 | bytes 1048576 | tf_op jit(solution)/shard_map/stage_scores/pallas_call | solution.py:366
  13.0 0.6 %collective-permute-start.7 = (bf16[256,128]{1,0:T(8,128)(2,1)S(1)}, bf16[256,128]{1,0:T(8,128)(2,1)S(1)}, u32[]{:S(2)}, u32[]{:S(2)}) collective-permute-start(bf16[256,128]{1,0:T(8,128)(2,1)S(1)} %collective-permute-done), channel_id=1, source_target_pairs={{0,1},{1,0},{2,3},{3,2},{4,5},{5,4},{6,7},{7,6},{8,9},{9,8},{10,11... | collective-permute-start | bytes 196616 | tf_op jit(solution)/shard_map/ppermute | solution.py:322
  13.6 0.1 collective-permute-start.6
  13.7 0.8 %stage_scores.3 = (f32[384,1024]{1,0:T(8,128)S(1)}, f32[384,1024]{1,0:T(8,128)S(1)}, f32[8,1024]{1,0:T(8,128)S(1)}) custom-call(f32[8,1024]{1,0:T(8,128)S(1)} %get-tuple-element.36.refs_0_, bf16[1024,128]{1,0:T(8,128)(2,1)S(1)} %get-tuple-element.37.refs_1_.refs_0_, bf16[1024,128]{1,0:T(8,128)(2,1)S(1)} %get-tuple-element.38.refs_2_.refs_1_, ...), custom_call_target="tpu_custom_call" | custom-call | flops 201326592 | bytes 1572864 | tf_op jit(solution)/shard_map/stage_scores/pallas_call | solution.py:366
  14.5 0.3 %collective-permute-done.6.refs_6_.refs_7_ = bf16[256,128]{1,0:T(8,128)(2,1)S(1)} collective-permute-done((bf16[256,128]{1,0:T(8,128)(2,1)S(1)}, bf16[256,128]{1,0:T(8,128)(2,1)S(1)}, u32[]{:S(2)}, u32[]{:S(2)}) %collective-permute-start.6) | collective-permute-done | bytes 65568 | tf_op jit(solution)/shard_map/ppermute | solution.py:322
  14.9 1.4 %late_scores.1 = (bf16[512,1024]{1,0:T(8,128)(2,1)S(1)}, bf16[512,1024]{1,0:T(8,128)(2,1)S(1)}, bf16[4,256,128]{2,1,0:T(8,128)(2,1)S(1)}, f32[8,1024]{1,0:T(8,128)S(1)}) custom-call(f32[8,1024]{1,0:T(8,128)S(1)} %get-tuple-element.36.refs_0_, bf16[1024,128]{1,0:T(8,128)(2,1)S(1)} %get-tuple-element.37.refs_1_.refs_0_, ...), custom_call_target="tpu_custom_call" | custom-call | flops 536870912 | bytes 4194304 | tf_op jit(solution)/shard_map/late_scores/pallas_call | solution.py:389
  16.2 0.2 collective-permute-start.9
  16.5 0.8 %own_parity_grads.1 = (bf16[512,1024]{1,0:T(8,128)(2,1)S(1)}, bf16[512,1024]{1,0:T(8,128)(2,1)S(1)}, f32[4,256,128]{2,1,0:T(8,128)S(1)}) custom-call(bf16[1024,128]{1,0:T(8,128)(2,1)S(1)} %get-tuple-element.37.refs_1_.refs_0_, bf16[1024,128]{1,0:T(8,128)(2,1)S(1)} %get-tuple-element.38.refs_2_.refs_1_, f32[8,1024]{1,0:T(8,128)S(1)} %get-tuple-element.51.refs_2_, ...), custom_call_target="tpu_custom_call" | custom-call | flops 268435456 | bytes 2097152 | tf_op jit(solution)/shard_map/own_parity_grads/pallas_call | solution.py:401
  17.2 0.6 %collective-permute-done.9.from_sib_ref = bf16[4,256,128]{2,1,0:T(8,128)(2,1)S(1)} collective-permute-done((bf16[4,256,128]{2,1,0:T(8,128)(2,1)S(1)}, bf16[4,256,128]{2,1,0:T(8,128)(2,1)S(1)}, u32[]{:S(2)}, u32[]{:S(2)}) %collective-permute-start.9) | collective-permute-done | bytes 262176 | tf_op jit(solution)/shard_map/ppermute | solution.py:322
  17.9 2.7 %collective-permute-start.10 = (bf16[256,128]{1,0:T(8,128)(2,1)S(1)}, bf16[256,128]{1,0:T(8,128)(2,1)S(1)}, u32[]{:S(2)}, u32[]{:S(2)}) collective-permute-start(bf16[256,128]{1,0:T(8,128)(2,1)S(1)} %get-tuple-element.62), channel_id=1, source_target_pairs={{6,0},{7,1},{4,2},{5,3},{10,4},{11,5},{8,6},{9,7},{14,8},{15,9},{1... | collective-permute-start | bytes 196616 | tf_op jit(solution)/shard_map/ppermute | solution.py:314
  20.6 1.1 %collective-permute-start.11 = (bf16[256,128]{1,0:T(8,128)(2,1)S(1)}, bf16[256,128]{1,0:T(8,128)(2,1)S(1)}, u32[]{:S(2)}, u32[]{:S(2)}) collective-permute-start(bf16[256,128]{1,0:T(8,128)(2,1)S(1)} %get-tuple-element.63), channel_id=1, source_target_pairs={{4,0},{5,1},{6,2},{7,3},{8,4},{9,5},{10,6},{11,7},{12,8},{13,9},{1... | collective-permute-start | bytes 196616 | tf_op jit(solution)/shard_map/ppermute | solution.py:314
  21.8 1.7 %collective-permute-start.12 = (bf16[256,128]{1,0:T(8,128)(2,1)S(1)}, bf16[256,128]{1,0:T(8,128)(2,1)S(1)}, u32[]{:S(2)}, u32[]{:S(2)}) collective-permute-start(bf16[256,128]{1,0:T(8,128)(2,1)S(1)} %get-tuple-element.64), channel_id=1, source_target_pairs={{2,0},{3,1},{8,2},{9,3},{6,4},{7,5},{12,6},{13,7},{10,8},{11,9},{1... | collective-permute-start | bytes 196616 | tf_op jit(solution)/shard_map/ppermute | solution.py:314
  23.5 1.1 %collective-permute-start.13 = (bf16[256,128]{1,0:T(8,128)(2,1)S(1)}, bf16[256,128]{1,0:T(8,128)(2,1)S(1)}, u32[]{:S(2)}, u32[]{:S(2)}) collective-permute-start(bf16[256,128]{1,0:T(8,128)(2,1)S(1)} %get-tuple-element.65), channel_id=1, source_target_pairs={{9,1},{11,3},{13,5},{15,7},{17,9},{19,11},{21,13},{23,15},{25,17},... | collective-permute-start | bytes 196616 | tf_op jit(solution)/shard_map/ppermute | solution.py:319
  24.6 1.6 %query_side.1 = (bf16[128,1024]{1,0:T(8,128)(2,1)}, bf16[128,1024]{1,0:T(8,128)(2,1)}) custom-call(bf16[512,1024]{1,0:T(8,128)(2,1)S(1)} %get-tuple-element.49.refs_0_, bf16[512,1024]{1,0:T(8,128)(2,1)S(1)} %get-tuple-element.50.refs_1_, bf16[512,1024]{1,0:T(8,128)(2,1)S(1)} %get-tuple-element.56.refs_2_, bf16[512,1024]{1,0:T(8,128)(2,1)S(1)} %get-tuple-element.57.refs_3_, ...), custom_call_target="tpu_custom_call" | custom-call | flops 536870912 | bytes 4194304 | tf_op jit(solution)/shard_map/query_side/pallas_call | solution.py:411
  26.3 0.3 collective-permute-done.13.refs_3_
  26.5 0.7 %total_grads.1 = (bf16[128,128]{1,0:T(8,128)(2,1)}, bf16[128,128]{1,0:T(8,128)(2,1)}) custom-call(f32[4,256,128]{2,1,0:T(8,128)S(1)} %get-tuple-element.60.mine_ref, bf16[4,256,128]{2,1,0:T(8,128)(2,1)S(1)} %collective-permute-done.9.from_sib_ref, bf16[256,128]{1,0:T(8,128)(2,1)S(1)} %collective-permute-done.10.refs_0_, ...), custom_call_target="tpu_custom_call" | custom-call | tf_op jit(solution)/shard_map/total_grads/pallas_call | solution.py:437
  (13 shorter events, 0.1 us)
Async XLA Ops:
  1.4 8.6 %collective-permute-start.2 = (bf16[256,128]{1,0:T(8,128)(2,1)S(1)}, bf16[256,128]{1,0:T(8,128)(2,1)S(1)}, u32[]{:S(2)}, u32[]{:S(2)}) collective-permute-start(bf16[256,128]{1,0:T(8,128)(2,1)S(1)} %pair_up.1.own_ref.refs_9_), channel_id=1, source_target_pairs={{0,2},{1,3},{2,8},{3,9},{4,6},{5,7},{6,12},{7,13},{8,10},{9,11},{1... | collective-permute-start | bytes 196616 | tf_op jit(solution)/shard_map/ppermute | solution.py:314
  4.4 7.5 %collective-permute-start.3 = (bf16[256,128]{1,0:T(8,128)(2,1)S(1)}, bf16[256,128]{1,0:T(8,128)(2,1)S(1)}, u32[]{:S(2)}, u32[]{:S(2)}) collective-permute-start(bf16[256,128]{1,0:T(8,128)(2,1)S(1)} %pair_up.1.own_ref.refs_9_), channel_id=1, source_target_pairs={{0,4},{1,5},{2,6},{3,7},{4,8},{5,9},{6,10},{7,11},{8,12},{9,13},{1... | collective-permute-start | bytes 196616 | tf_op jit(solution)/shard_map/ppermute | solution.py:314
  5.9 7.1 %collective-permute-start.1 = (bf16[256,128]{1,0:T(8,128)(2,1)S(1)}, bf16[256,128]{1,0:T(8,128)(2,1)S(1)}, u32[]{:S(2)}, u32[]{:S(2)}) collective-permute-start(bf16[256,128]{1,0:T(8,128)(2,1)S(1)} %pair_up.1.own_ref.refs_9_), channel_id=1, source_target_pairs={{0,6},{1,7},{2,4},{3,5},{4,10},{5,11},{6,8},{7,9},{8,14},{9,15},{1... | collective-permute-start | bytes 196616 | tf_op jit(solution)/shard_map/ppermute | solution.py:314
  8.4 4.6 %collective-permute-start = (bf16[256,128]{1,0:T(8,128)(2,1)S(1)}, bf16[256,128]{1,0:T(8,128)(2,1)S(1)}, u32[]{:S(2)}, u32[]{:S(2)}) collective-permute-start(bf16[256,128]{1,0:T(8,128)(2,1)S(1)} %pair_up.1.own_ref.refs_9_), channel_id=1, source_target_pairs={{1,9},{3,11},{5,13},{7,15},{9,17},{11,19},{13,21},{15,23},{17,25},... | collective-permute-start | bytes 196616 | tf_op jit(solution)/shard_map/ppermute | solution.py:319
  11.9 1.8 %collective-permute-start.5 = (bf16[256,128]{1,0:T(8,128)(2,1)S(1)}, bf16[256,128]{1,0:T(8,128)(2,1)S(1)}, u32[]{:S(2)}, u32[]{:S(2)}) collective-permute-start(bf16[256,128]{1,0:T(8,128)(2,1)S(1)} %collective-permute-done.3.refs_5_.refs_11_), channel_id=1, source_target_pairs={{0,1},{1,0},{2,3},{3,2},{4,5},{5,4},{6,7},{7,6},{8,9},{9,8},{10,11... | collective-permute-start | bytes 196616 | tf_op jit(solution)/shard_map/ppermute | solution.py:322
  11.9 1.8 %collective-permute-start.4 = (bf16[256,128]{1,0:T(8,128)(2,1)S(1)}, bf16[256,128]{1,0:T(8,128)(2,1)S(1)}, u32[]{:S(2)}, u32[]{:S(2)}) collective-permute-start(bf16[256,128]{1,0:T(8,128)(2,1)S(1)} %collective-permute-done.2.refs_4_.refs_10_), channel_id=1, source_target_pairs={{0,1},{1,0},{2,3},{3,2},{4,5},{5,4},{6,7},{7,6},{8,9},{9,8},{10,11... | collective-permute-start | bytes 196616 | tf_op jit(solution)/shard_map/ppermute | solution.py:322
  12.4 2.1 %collective-permute-start.8 = (bf16[256,128]{1,0:T(8,128)(2,1)S(1)}, bf16[256,128]{1,0:T(8,128)(2,1)S(1)}, u32[]{:S(2)}, u32[]{:S(2)}) collective-permute-start(bf16[256,128]{1,0:T(8,128)(2,1)S(1)} %pair_up.1.own_ref.refs_9_), channel_id=1, source_target_pairs={{0,1},{1,0},{2,3},{3,2},{4,5},{5,4},{6,7},{7,6},{8,9},{9,8},{10,11... | collective-permute-start | bytes 196616 | tf_op jit(solution)/shard_map/ppermute | solution.py:322
  13.0 1.5 %collective-permute-start.7 = (bf16[256,128]{1,0:T(8,128)(2,1)S(1)}, bf16[256,128]{1,0:T(8,128)(2,1)S(1)}, u32[]{:S(2)}, u32[]{:S(2)}) collective-permute-start(bf16[256,128]{1,0:T(8,128)(2,1)S(1)} %collective-permute-done), channel_id=1, source_target_pairs={{0,1},{1,0},{2,3},{3,2},{4,5},{5,4},{6,7},{7,6},{8,9},{9,8},{10,11... | collective-permute-start | bytes 196616 | tf_op jit(solution)/shard_map/ppermute | solution.py:322
  13.6 1.3 %collective-permute-start.6 = (bf16[256,128]{1,0:T(8,128)(2,1)S(1)}, bf16[256,128]{1,0:T(8,128)(2,1)S(1)}, u32[]{:S(2)}, u32[]{:S(2)}) collective-permute-start(bf16[256,128]{1,0:T(8,128)(2,1)S(1)} %collective-permute-done.1.refs_6_.refs_12_), channel_id=1, source_target_pairs={{0,1},{1,0},{2,3},{3,2},{4,5},{5,4},{6,7},{7,6},{8,9},{9,8},{10,11... | collective-permute-start | bytes 196616 | tf_op jit(solution)/shard_map/ppermute | solution.py:322
  16.2 1.6 %collective-permute-start.9 = (bf16[4,256,128]{2,1,0:T(8,128)(2,1)S(1)}, bf16[4,256,128]{2,1,0:T(8,128)(2,1)S(1)}, u32[]{:S(2)}, u32[]{:S(2)}) collective-permute-start(bf16[4,256,128]{2,1,0:T(8,128)(2,1)S(1)} %get-tuple-element.61), channel_id=1, source_target_pairs={{0,1},{1,0},{2,3},{3,2},{4,5},{5,4},{6,7},{7,6},{8,9},{9,8},{10,11... | collective-permute-start | bytes 786440 | tf_op jit(solution)/shard_map/ppermute | solution.py:322
  17.9 8.4 %collective-permute-start.10 = (bf16[256,128]{1,0:T(8,128)(2,1)S(1)}, bf16[256,128]{1,0:T(8,128)(2,1)S(1)}, u32[]{:S(2)}, u32[]{:S(2)}) collective-permute-start(bf16[256,128]{1,0:T(8,128)(2,1)S(1)} %get-tuple-element.62), channel_id=1, source_target_pairs={{6,0},{7,1},{4,2},{5,3},{10,4},{11,5},{8,6},{9,7},{14,8},{15,9},{1... | collective-permute-start | bytes 196616 | tf_op jit(solution)/shard_map/ppermute | solution.py:314
  20.6 5.6 %collective-permute-start.11 = (bf16[256,128]{1,0:T(8,128)(2,1)S(1)}, bf16[256,128]{1,0:T(8,128)(2,1)S(1)}, u32[]{:S(2)}, u32[]{:S(2)}) collective-permute-start(bf16[256,128]{1,0:T(8,128)(2,1)S(1)} %get-tuple-element.63), channel_id=1, source_target_pairs={{4,0},{5,1},{6,2},{7,3},{8,4},{9,5},{10,6},{11,7},{12,8},{13,9},{1... | collective-permute-start | bytes 196616 | tf_op jit(solution)/shard_map/ppermute | solution.py:314
  21.8 4.5 %collective-permute-start.12 = (bf16[256,128]{1,0:T(8,128)(2,1)S(1)}, bf16[256,128]{1,0:T(8,128)(2,1)S(1)}, u32[]{:S(2)}, u32[]{:S(2)}) collective-permute-start(bf16[256,128]{1,0:T(8,128)(2,1)S(1)} %get-tuple-element.64), channel_id=1, source_target_pairs={{2,0},{3,1},{8,2},{9,3},{6,4},{7,5},{12,6},{13,7},{10,8},{11,9},{1... | collective-permute-start | bytes 196616 | tf_op jit(solution)/shard_map/ppermute | solution.py:314
  23.5 3.1 %collective-permute-start.13 = (bf16[256,128]{1,0:T(8,128)(2,1)S(1)}, bf16[256,128]{1,0:T(8,128)(2,1)S(1)}, u32[]{:S(2)}, u32[]{:S(2)}) collective-permute-start(bf16[256,128]{1,0:T(8,128)(2,1)S(1)} %get-tuple-element.65), channel_id=1, source_target_pairs={{9,1},{11,3},{13,5},{15,7},{17,9},{19,11},{21,13},{23,15},{25,17},... | collective-permute-start | bytes 196616 | tf_op jit(solution)/shard_map/ppermute | solution.py:319

commit v6 on v5

--- a/solution.py
+++ b/solution.py
@@ -44,11 +44,11 @@
         self.closing = sibs[:-1] + lins[-1:]
         self.late = [sibs[-1], "last"]
         self.stages = [["own"], self.middle, self.closing, self.late]
-        self.sibs = [("sib", k) for k in range(1, half)] + ["last"]
-        self.mine = ["own"] + [("lin", k) for k in range(1, half)]
+        self.swapped = self.closing[:-1] + ["swap"] + self.closing[-1:]
+        self.mine = ["own"] + self.middle + ["keep"]
 
     def place(self, slot):
-        for at, group in enumerate(self.stages):
+        for at, group in enumerate([*self.stages[:-1], ["keep"]]):
             if slot in group:
                 return at, rows_of(group.index(slot))
 
@@ -173,109 +173,130 @@
         out_ref[k, BLOCK:, :] = value_grad[rows_of(k), :].astype(out_ref.dtype)
 
 
-def late_kernel(slots, *refs):
-    count = len(slots.late)
-    bias_ref, query_rows, grad_rows, powers_ref, probs_ref, before_ref = refs[:6]
-    blocks = list(refs[6 : 6 + count])
-    sib_own_ref = refs[6 + count]
-    weights_ref, score_grad_ref, sib_out_ref, stats_ref, last_ref = refs[7 + count :]
-    _, _, core = position()
-
+def put_either(core, even, odd, ref):
     @pl.when(core == 0)
     def _():
-        last_ref[...] = blocks[-1][...]
+        ref[...] = even[...]
 
     @pl.when(core == 1)
     def _():
-        last_ref[...] = sib_own_ref[...]
-
-    blocks[-1] = last_ref
+        ref[...] = odd[...]
+
+
+def late_kernel(slots, *refs):
+    bias_ref, query_rows, grad_rows, powers_ref, probs_ref, before_ref = refs[:6]
+    sib_ref, far_ref, sib_own_ref = refs[6:9]
+    keep_powers, keep_probs, final_ref, weights_ref, score_grad_ref, swap_ref, lin_ref, last_ref = refs[9:]
+    _, _, core = position()
+    even = core == 0
+    half = slots.half
+    put_either(core, far_ref, sib_own_ref, last_ref)
+    blocks = [sib_ref, last_ref]
     keys, values = stacked(blocks, 0), stacked(blocks, 1)
-    first = slots.window - 1 - count
+    first = slots.window - 1 - len(blocks)
     for column in range(FLAT // COLS):
         cols = tile_of(column)
         scores = dot(keys, query_rows[cols, :], 1, 1)
         probs_grad = dot(values, grad_rows[cols, :], 1, 1)
-        parts = [scores[rows_of(s), :] for s in range(count)]
+        parts = [scores[rows_of(s), :] for s in range(2)]
         start = tuple(before_ref[row : row + 1, cols] for row in range(3))
-        biases = [bias_ref[row : row + 1, cols] for row in range(first, first + count)]
+        biases = [bias_ref[row : row + 1, cols] for row in range(first, first + 2)]
         powers, top, total, mixed = absorb(parts, probs_grad, biases, *start)
         inverse = 1.0 / total
         delta = mixed * inverse
         for row, value in enumerate((top, inverse, delta)):
-            stats_ref[row : row + 1, cols] = value
+            final_ref[row : row + 1, cols] = value
+        sib_probs, last_probs = probs_grad[rows_of(0), :], probs_grad[rows_of(1), :]
+        keep_powers[:, cols] = jnp.where(even, powers[0], powers[1])
+        keep_probs[:, cols] = jnp.where(even, sib_probs, last_probs)
         factor = jnp.exp2(start[0] - top) * inverse
-        for s, slot in enumerate(slots.sibs):
-            at, rows = slots.place(slot)
-            if slot in slots.late:
-                piece = powers[slots.late.index(slot)], inverse, probs_grad[rows, :]
+        for s, slot in enumerate(slots.swapped):
+            if slot == "swap":
+                piece = jnp.where(even, powers[1], powers[0]), inverse, jnp.where(even, last_probs, sib_probs)
             else:
+                _, rows = slots.place(slot)
                 piece = powers_ref[rows, cols], factor, probs_ref[rows, cols]
             put_weights(rows_of(s), cols, *piece, delta, weights_ref, score_grad_ref)
-    put_grads(weights_ref, score_grad_ref, query_rows, grad_rows, sib_out_ref)
+    key_grad = dot(score_grad_ref[...], query_rows[...], 1, 0) * SCALE
+    value_grad = dot(weights_ref[...], grad_rows[...], 1, 0)
+    for k in range(half):
+        swap_ref[k, :BLOCK, :] = key_grad[rows_of(k), :].astype(jnp.bfloat16)
+        swap_ref[k, BLOCK:, :] = value_grad[rows_of(k), :].astype(jnp.bfloat16)
+    lin_ref[:BLOCK, :] = key_grad[rows_of(half - 1), :]
+    lin_ref[BLOCK:, :] = value_grad[rows_of(half - 1), :]
 
 
 def mine_kernel(slots, *refs):
     query_rows, grad_rows, final_ref = refs[:3]
-    stages = [refs[3 + 3 * at : 6 + 3 * at] for at in range(3)]
-    weights_ref, score_grad_ref, mine_ref = refs[12:]
+    stages = {0: refs[3:6], 1: refs[6:9], 3: (*refs[9:11], final_ref)}
+    weights_ref, score_grad_ref, mine_ref = refs[11:]
     for column in range(FLAT // COLS):
         cols = tile_of(column)
         top, inverse, delta = (final_ref[row : row + 1, cols] for row in range(3))
-        factors = [jnp.exp2(stats_ref[0:1, cols] - top) * inverse for _, _, stats_ref in stages]
         for s, slot in enumerate(slots.mine):
             at, rows = slots.place(slot)
-            piece = stages[at][0][rows, cols], factors[at], stages[at][1][rows, cols]
+            powers_ref, probs_ref, stats_ref = stages[at]
+            factor = jnp.exp2(stats_ref[0:1, cols] - top) * inverse
+            piece = powers_ref[rows, cols], factor, probs_ref[rows, cols]
             put_weights(rows_of(s), cols, *piece, delta, weights_ref, score_grad_ref)
-    put_grads(weights_ref, score_grad_ref, query_rows, grad_rows, mine_ref)
+    key_grad = dot(score_grad_ref[...], query_rows[...], 1, 0) * SCALE
+    value_grad = dot(weights_ref[...], grad_rows[...], 1, 0)
+    for k in range(slots.half):
+        mine_ref[k, :BLOCK, :] = key_grad[rows_of(k), :]
+        mine_ref[k, BLOCK:, :] = value_grad[rows_of(k), :]
 
 
 def query_side_kernel(slots, *refs):
-    sib_weights, sib_score_grad, mine_weights, mine_score_grad, sib_own_ref = refs[:5]
-    blocks = list(refs[5 : 5 + slots.window])
-    attended_ref, query_grad_ref, last_ref = refs[5 + slots.window :]
+    half = slots.half
+    swap_weights, swap_score_grad, mine_weights, mine_score_grad = refs[:4]
+    swapped, mine = list(refs[4 : 3 + half]), list(refs[3 + half : 2 + 2 * half])
+    sib_ref, far_ref, sib_own_ref, attended_out, query_grad_out = refs[2 + 2 * half : 7 + 2 * half]
+    swap_ref, keep_ref, attended_ref, query_grad_ref, sems = refs[7 + 2 * half :]
     _, _, core = position()
-    half = slots.half
-
-    @pl.when(core == 0)
-    def _():
-        last_ref[...] = blocks[half - 1][...]
-
-    @pl.when(core == 1)
-    def _():
-        last_ref[...] = sib_own_ref[...]
-
-    blocks[half - 1] = last_ref
-
-    def mixed(part, sib_ref, mine_ref):
-        sib = dot(stacked(blocks[:half], part), sib_ref[...], 0, 0)
-        return sib + dot(stacked(blocks[half:], part), mine_ref[...], 0, 0)
-
-    attended_t = mixed(1, sib_weights, mine_weights)
-    query_grad_t = mixed(0, sib_score_grad, mine_score_grad) * SCALE
-    for h in range(HEADS):
-        rows = slice(h * BLOCK, (h + 1) * BLOCK)
-        attended_ref[:, rows] = attended_t[:, rows].T.astype(jnp.bfloat16)
-        query_grad_ref[:, rows] = query_grad_t[:, rows].T.astype(jnp.bfloat16)
-
-
-def merge_kernel(mine_ref, from_sib_ref, *sent_refs):
+    put_either(core, far_ref, sib_ref, swap_ref)
+    put_either(core, sib_ref, sib_own_ref, keep_ref)
+    swapped.insert(half - 2, swap_ref)
+    mine.append(keep_ref)
+
+    def mixed(part, swap_part, mine_part):
+        return dot(stacked(swapped, part), swap_part[...], 0, 0) + dot(stacked(mine, part), mine_part[...], 0, 0)
+
+    def put(result_t, ref, out, sem):
+        for h in range(HEADS):
+            ref[:, rows_of(h)] = result_t[:, rows_of(h)].T.astype(jnp.bfloat16)
+        copy = pltpu.make_async_copy(ref, out, sem)
+        copy.start()
+        return copy
+
+    attended_copy = put(mixed(1, swap_weights, mine_weights), attended_ref, attended_out, sems.at[0])
+    query_grad_t = mixed(0, swap_score_grad, mine_score_grad) * SCALE
+    query_grad_copy = put(query_grad_t, query_grad_ref, query_grad_out, sems.at[1])
+    attended_copy.wait()
+    query_grad_copy.wait()
+
+
+def merge_kernel(mine_ref, lin_ref, from_sib_ref, *sent_refs):
+    half = mine_ref.shape[0]
+    f32, bf16 = jnp.float32, jnp.bfloat16
     for k, ref in enumerate(sent_refs[:-1]):
-        ref[...] = (mine_ref[k + 1] + from_sib_ref[k].astype(jnp.float32)).astype(jnp.bfloat16)
+        ref[...] = (mine_ref[k + 1] + from_sib_ref[k].astype(f32)).astype(bf16)
     _, _, core = position()
-    far = from_sib_ref[len(sent_refs) - 1]
-    sent_refs[-1][...] = jnp.where(core == 1, far, jnp.zeros_like(far))
-
-
-def total_kernel(order, mine_ref, from_sib_ref, *refs):
+    far = from_sib_ref[half - 2].astype(f32)
+    sent_refs[-1][: 2 * BLOCK, :] = (jnp.where(core == 0, lin_ref[...], 0.0) + far).astype(bf16)
+    sent_refs[-1][2 * BLOCK :, :] = (mine_ref[half - 1] + from_sib_ref[half - 1].astype(f32)).astype(bf16)
+
+
+def pass_kernel(mine_ref, far_ref, out_ref):
+    _, _, core = position()
+    near = mine_ref[mine_ref.shape[0] - 1].astype(jnp.bfloat16)
+    out_ref[...] = jnp.where(core == 0, far_ref[2 * BLOCK :, :], near)
+
+
+def total_kernel(mine_ref, far_ref, passed_ref, *refs):
     back, (key_ref, value_ref) = refs[:-2], refs[-2:]
-    _, _, core = position()
-    half = len(order)
-    near = from_sib_ref[half - 1].astype(jnp.float32)
-    total = mine_ref[0] + jnp.where(core == 0, near, back[order.index(half)][...].astype(jnp.float32))
-    for k, ref in zip(order, back):
-        if k < half:
-            total = total + ref[...].astype(jnp.float32)
+    total = mine_ref[0] + far_ref[: 2 * BLOCK, :].astype(jnp.float32) + passed_ref[...].astype(jnp.float32)
+    for ref in back:
+        total = total + ref[...].astype(jnp.float32)
     key_ref[...] = total[:BLOCK].astype(jnp.bfloat16)
     value_ref[...] = total[BLOCK:].astype(jnp.bfloat16)
 
@@ -302,21 +323,27 @@
     small = pltpu.CompilerParams(vmem_limit_bytes=window * MIB // 4)
     params = pltpu.CompilerParams(vmem_limit_bytes=window * MIB)
 
+    def target(i, m):
+        top = 1 << (m.bit_length() - 1)
+        run, chip, core = i // window, i // 2 % half, i % 2
+        run, to = (run, chip ^ m) if not chip & top else (run + 1, chip ^ m)
+        if run * window == devices:
+            run, to = 0, chip ^ top
+        return run * window + 2 * to + core
+
     def ahead(block, m, back=False):
-        top = 1 << (m.bit_length() - 1)
-        route = []
-        for i in range(devices):
-            run, chip, core = i // window, i // 2 % half, i % 2
-            run, to = (run, chip ^ m) if not chip & top else (run + 1, chip ^ m)
-            if run * window == devices:
-                run, to = 0, chip ^ top
-            route.append((i, run * window + 2 * to + core))
+        route = [(i, target(i, m)) for i in range(devices)]
         return lax.ppermute(block, AXES, [pair[::-1] for pair in route] if back else route)
 
-    def ahead_odd(block, k, back=False):
-        route = [(i, i + 2 * k if i + 2 * k < devices else i ^ 1) for i in range(1, devices, 2)]
-        route += [(i, i - 2 * k if i >= 2 * k else i ^ 1) for i in range(0, devices, 2)]
-        return lax.ppermute(block, AXES, [pair[::-1] for pair in route] if back else route)
+    def back_mixed(block):
+        route = [(target(i, half - 1), i) for i in range(0, devices, 2)]
+        route += [((i + window) % devices, i) for i in range(1, devices, 2)]
+        return lax.ppermute(block, AXES, route)
+
+    def ahead_odd(block):
+        route = [(i, i + window if i + window < devices else i ^ 1) for i in range(1, devices, 2)]
+        route += [(i, i - window if i >= window else i ^ 1) for i in range(0, devices, 2)]
+        return lax.ppermute(block, AXES, route)
 
     def swapped(block):
         return lax.ppermute(block, AXES, [(i, i ^ 1) for i in range(devices)])
@@ -330,7 +357,7 @@
         compiler_params=small,
         name="pair_up",
     )(in_hbm(key_rows), in_hbm(value_rows))
-    lins = [ahead(own, k) for k in slots.arrival] + [ahead_odd(own, half)]
+    lins = [ahead(own, k) for k in slots.arrival] + [ahead_odd(own)]
     sib_own = swapped(own)
 
     def stage(blocks):
@@ -385,63 +412,82 @@
         held["sib", k] = swap
     closing_stage = next_stage(2, middle_stage[2])
 
+    sib, far, near = held[slots.late[0]], held["last"], sib_own
     weights = [pltpu.VMEM((half * BLOCK, FLAT), bf16)] * 2
-    sib_weights, sib_score_grad, sib_out, final = pl.pallas_call(
+    *keep, final, swap_weights, swap_score_grad, swap_out, lin_out = pl.pallas_call(
         functools.partial(late_kernel, slots),
-        out_shape=weights + [pltpu.VMEM((half, 2 * BLOCK, HEAD_DIM), bf16), pltpu.VMEM((8, FLAT), f32)],
-        in_specs=[VMEM] * (7 + len(slots.late)),
-        out_specs=[VMEM] * 4,
+        out_shape=stage(1)
+        + weights
+        + [pltpu.VMEM((half, 2 * BLOCK, HEAD_DIM), bf16), pltpu.VMEM((2 * BLOCK, HEAD_DIM), f32)],
+        in_specs=[VMEM] * 9,
+        out_specs=[VMEM] * 7,
         scratch_shapes=[pltpu.VMEM((2 * BLOCK, HEAD_DIM), bf16)],
         compiler_params=params,
         cost_estimate=cost(window, 2),
         name="late_scores",
-    )(bias, query_rows, grad_rows, *closing_stage, *[held[slot] for slot in slots.late], sib_own)
-    from_sib = swapped(sib_out)
+    )(bias, query_rows, grad_rows, *closing_stage, sib, far, near)
+    from_sib = swapped(swap_out)
 
     mine_weights, mine_score_grad, mine = pl.pallas_call(
         functools.partial(mine_kernel, slots),
         out_shape=weights + [pltpu.VMEM((half, 2 * BLOCK, HEAD_DIM), f32)],
-        in_specs=[VMEM] * 12,
+        in_specs=[VMEM] * 11,
         out_specs=[VMEM] * 3,
         compiler_params=params,
         cost_estimate=cost(half, 2),
-        name="own_parity_grads",
-    )(query_rows, grad_rows, final, *own_stage, *middle_stage, *closing_stage)
+        name="other_grads",
+    )(query_rows, grad_rows, final, *own_stage, *middle_stage, *keep)
 
     attended, query_grad = pl.pallas_call(
         functools.partial(query_side_kernel, slots),
-        out_shape=[shape(queries.shape, bf16), shape(queries.shape, bf16)],
-        in_specs=[VMEM] * (5 + window),
-        out_specs=[VMEM] * 2,
-        scratch_shapes=[pltpu.VMEM((2 * BLOCK, HEAD_DIM), bf16)],
+        out_shape=[shape(queries.shape, bf16)] * 2,
+        in_specs=[VMEM] * (5 + 2 * half),
+        out_specs=[HBM] * 2,
+        scratch_shapes=[
+            pltpu.VMEM((2 * BLOCK, HEAD_DIM), bf16),
+            pltpu.VMEM((2 * BLOCK, HEAD_DIM), bf16),
+            pltpu.VMEM(queries.shape, bf16),
+            pltpu.VMEM(queries.shape, bf16),
+            pltpu.SemaphoreType.DMA((2,)),
+        ],
         compiler_params=params,
         cost_estimate=cost(window, 2),
         name="query_side",
     )(
-        *[in_vmem(part) for part in (sib_weights, sib_score_grad, mine_weights, mine_score_grad)],
-        sib_own, *[held[slot] for slot in slots.sibs + slots.mine],
+        *[in_vmem(part) for part in (swap_weights, swap_score_grad, mine_weights, mine_score_grad)],
+        *[held[slot] for slot in slots.closing + ["own"] + slots.middle],
+        sib, far, near,
     )
 
-    sent = pl.pallas_call(
+    block = pltpu.VMEM((2 * BLOCK, HEAD_DIM), bf16)
+    *sent, sent_far = pl.pallas_call(
         merge_kernel,
-        out_shape=[pltpu.VMEM((2 * BLOCK, HEAD_DIM), bf16)] * half,
-        in_specs=[VMEM] * 2,
-        out_specs=[VMEM] * half,
+        out_shape=[block] * (half - 2) + [pltpu.VMEM((4 * BLOCK, HEAD_DIM), bf16)],
+        in_specs=[VMEM] * 3,
+        out_specs=[VMEM] * (half - 1),
         compiler_params=small,
         name="merge_siblings",
-    )(mine, from_sib)
-    order = list(range(half, 0, -1))[1:] + [half]
-    back = [
-        ahead(sent[k - 1], k, back=True) if k < half else ahead_odd(sent[k - 1], half, back=True) for k in order
-    ]
+    )(mine, lin_out, from_sib)
+    back_far = back_mixed(sent_far)
+    passed = swapped(
+        pl.pallas_call(
+            pass_kernel,
+            out_shape=block,
+            in_specs=[VMEM] * 2,
+            out_specs=VMEM,
+            compiler_params=small,
+            name="pass_on",
+        )(mine, back_far)
+    )
+    back = [ahead(sent[m - 1], m, back=True) for m in range(half - 2, 0, -1)]
     key_grad, value_grad = pl.pallas_call(
-        functools.partial(total_kernel, order),
+        total_kernel,
         out_shape=[shape((BLOCK, HEAD_DIM), bf16)] * 2,
-        in_specs=[VMEM] * (2 + half),
+        in_specs=[VMEM] * (1 + half),
         out_specs=[VMEM] * 2,
         compiler_params=small,
         name="total_grads",
-    )(mine, from_sib, *back)
+    )(mine, back_far, passed, *back)
     return attended, query_grad, key_grad, value_grad
 
 

time: 27.5 us -> 27.3 us (level)
  starting transfers between devices: 15.1 us -> 14.1 us
  waiting for transfers between devices: 3.11 us -> 4 us
    ppermute x6 -> x5, starting transfers between devices: 12.6 us -> 9.86 us  [ahead(): lax.ppermute(block, AXES, [pair[::-1] for pair in route] if back else route)]
    ppermute x2, starting transfers between devices: 1.15 us -> 2.74 us  [the longest x1 2.74 us: back_mixed(): return lax.ppermute(block, AXES, route)]
    ppermute x2, waiting for transfers between devices: 0.25 us -> 1.04 us  [the longest x1 1.04 us: back_mixed(): return lax.ppermute(block, AXES, route)]
    pallas_call x3 -> x4, Pallas kernels: 2.08 us -> 2.18 us  [the longest x1 1.46 us: local(): pl.pallas_call(functools.partial(late_kernel, slots), out_shape=stage(1)...]
    ppermute x6 -> x5, waiting for transfers between devices: 1.92 us -> 2.01 us  [ahead(): lax.ppermute(block, AXES, [pair[::-1] for pair in route] if back else route)]
    ppermute x6 -> x7, starting transfers between devices: 1.38 us -> 1.45 us  [swapped(): return lax.ppermute(block, AXES, [(i, i ^ 1) for i in range(devices)])]
    ppermute x6 -> x7, waiting for transfers between devices: 0.94 us -> 0.95 us  [swapped(): return lax.ppermute(block, AXES, [(i, i ^ 1) for i in range(devices)])]
  transfers between devices with their start and end apart: 14 -> 14, of which waited for: 4 -> 5; matrix products, arithmetic and copies ran while one was open for 0% -> 0% of each run, Pallas kernels for 20% -> 20%
where the time goes in v6:
time: 27.3 us; the launch traced here: 27.1 us
  starting transfers between devices  14.1 us (52%)
  Pallas kernels  8.26 us (30%)
  waiting for transfers between devices  4 us (15%)
  between operations  0.75 us (3%)
    ppermute x5, starting transfers between devices, ahead(): lax.ppermute(block, AXES, [pair[::-1] for pair in route] if back else route)  9.86 us
    ppermute x1, starting transfers between devices, back_mixed(): return lax.ppermute(block, AXES, route)  2.74 us
    ppermute x5, waiting for transfers between devices, ahead(): lax.ppermute(block, AXES, [pair[::-1] for pair in route] if back else route)  2.01 us
    pallas_call x1, Pallas kernels, local(): pl.pallas_call(functools.partial(query_side_kernel, slots), out_shape=[sh...  1.57 us
    pallas_call x1, Pallas kernels, local(): pl.pallas_call(functools.partial(own_kernel, slots), out_shape=[pltpu.VME...  1.54 us
    pallas_call x1, Pallas kernels, local(): pl.pallas_call(functools.partial(late_kernel, slots), out_shape=stage(1)...  1.46 us
    ppermute x7, starting transfers between devices, swapped(): return lax.ppermute(block, AXES, [(i, i ^ 1) for i in range(devices)])  1.45 us
    pallas_call x2, Pallas kernels, next_stage(): pl.pallas_call(functools.partial(stage_kernel, first, len(group)), out_sh...  1.38 us
  transfers between devices with their start and end apart: 14, of which 5 were waited for; matrix products, arithmetic and copies ran while one was open for 0% of the time, Pallas kernels for 20%

profile of v6, /device:TPU:0, one launch (start us, length us, event | category | flops | bytes accessed | tf_op | source)
XLA Modules:
  0.0 27.1 jit_solution(854524561272306931)
XLA Ops:
  0.6 0.8 %pair_up.1.own_ref.refs_7_ = bf16[256,128]{1,0:T(8,128)(2,1)S(1)} custom-call(bf16[128,128]{1,0:T(8,128)(2,1)} %key_ref.1, bf16[128,128]{1,0:T(8,128)(2,1)} %value_ref.1), custom_call_target="tpu_custom_call" | custom-call | tf_op jit(solution)/shard_map/pair_up/pallas_call | solution.py:351
  1.4 3.0 %collective-permute-start.2 = (bf16[256,128]{1,0:T(8,128)(2,1)S(1)}, bf16[256,128]{1,0:T(8,128)(2,1)S(1)}, u32[]{:S(2)}, u32[]{:S(2)}) collective-permute-start(bf16[256,128]{1,0:T(8,128)(2,1)S(1)} %pair_up.1.own_ref.refs_7_), channel_id=1, source_target_pairs={{0,2},{1,3},{2,8},{3,9},{4,6},{5,7},{6,12},{7,13},{8,10},{9,11},{1... | collective-permute-start | bytes 196616 | tf_op jit(solution)/shard_map/ppermute | solution.py:336
  4.4 1.5 %collective-permute-start.3 = (bf16[256,128]{1,0:T(8,128)(2,1)S(1)}, bf16[256,128]{1,0:T(8,128)(2,1)S(1)}, u32[]{:S(2)}, u32[]{:S(2)}) collective-permute-start(bf16[256,128]{1,0:T(8,128)(2,1)S(1)} %pair_up.1.own_ref.refs_7_), channel_id=1, source_target_pairs={{0,4},{1,5},{2,6},{3,7},{4,8},{5,9},{6,10},{7,11},{8,12},{9,13},{1... | collective-permute-start | bytes 196616 | tf_op jit(solution)/shard_map/ppermute | solution.py:336
  5.9 2.5 %collective-permute-start.1 = (bf16[256,128]{1,0:T(8,128)(2,1)S(1)}, bf16[256,128]{1,0:T(8,128)(2,1)S(1)}, u32[]{:S(2)}, u32[]{:S(2)}) collective-permute-start(bf16[256,128]{1,0:T(8,128)(2,1)S(1)} %pair_up.1.own_ref.refs_7_), channel_id=1, source_target_pairs={{0,6},{1,7},{2,4},{3,5},{4,10},{5,11},{6,8},{7,9},{8,14},{9,15},{1... | collective-permute-start | bytes 196616 | tf_op jit(solution)/shard_map/ppermute | solution.py:336
  8.4 1.5 %own_scores.1 = (bf16[1024,128]{1,0:T(8,128)(2,1)S(1)}, bf16[1024,128]{1,0:T(8,128)(2,1)S(1)}, f32[8,1024]{1,0:T(8,128)S(1)}, f32[128,1024]{1,0:T(8,128)S(1)}, f...) custom-call(s32[32]{0:T(128)} %doc_hbm.1, bf16[128,1024]{1,0:T(8,128)(2,1)} %query_ref.1, bf16[128,1024]{1,0:T(8,128)(2,1)} %grad_ref.1, ...), custom_call_target="tpu_custom_call" | custom-call | flops 67108864 | bytes 524288 | tf_op jit(solution)/shard_map/own_scores/pallas_call | solution.py:370
  10.0 1.9 %collective-permute-done.3.refs_5_.refs_9_ = bf16[256,128]{1,0:T(8,128)(2,1)S(1)} collective-permute-done((bf16[256,128]{1,0:T(8,128)(2,1)S(1)}, bf16[256,128]{1,0:T(8,128)(2,1)S(1)}, u32[]{:S(2)}, u32[]{:S(2)}) %collective-permute-start.3) | collective-permute-done | bytes 65568 | tf_op jit(solution)/shard_map/ppermute | solution.py:336
  11.9 0.5 %collective-permute-start.4 = (bf16[256,128]{1,0:T(8,128)(2,1)S(1)}, bf16[256,128]{1,0:T(8,128)(2,1)S(1)}, u32[]{:S(2)}, u32[]{:S(2)}) collective-permute-start(bf16[256,128]{1,0:T(8,128)(2,1)S(1)} %collective-permute-done.2.refs_4_.refs_8_), channel_id=1, source_target_pairs={{0,1},{1,0},{2,3},{3,2},{4,5},{5,4},{6,7},{7,6},{8,9},{9,8},{10,11... | collective-permute-start | bytes 196616 | tf_op jit(solution)/shard_map/ppermute | solution.py:349
  12.4 0.6 %stage_scores.2 = (f32[256,1024]{1,0:T(8,128)S(1)}, f32[256,1024]{1,0:T(8,128)S(1)}, f32[8,1024]{1,0:T(8,128)S(1)}) custom-call(f32[8,1024]{1,0:T(8,128)S(1)} %get-tuple-element.38.refs_0_, bf16[1024,128]{1,0:T(8,128)(2,1)S(1)} %get-tuple-element.39.refs_1_.refs_0_, bf16[1024,128]{1,0:T(8,128)(2,1)S(1)} %get-tuple-element.40.refs_2_.refs_1_, ...), custom_call_target="tpu_custom_call" | custom-call | flops 134217728 | bytes 1048576 | tf_op jit(solution)/shard_map/stage_scores/pallas_call | solution.py:393
  13.0 0.6 %collective-permute-start.7 = (bf16[256,128]{1,0:T(8,128)(2,1)S(1)}, bf16[256,128]{1,0:T(8,128)(2,1)S(1)}, u32[]{:S(2)}, u32[]{:S(2)}) collective-permute-start(bf16[256,128]{1,0:T(8,128)(2,1)S(1)} %collective-permute-done), channel_id=1, source_target_pairs={{0,1},{1,0},{2,3},{3,2},{4,5},{5,4},{6,7},{7,6},{8,9},{9,8},{10,11... | collective-permute-start | bytes 196616 | tf_op jit(solution)/shard_map/ppermute | solution.py:349
  13.6 0.1 collective-permute-start.6
  13.7 0.8 %stage_scores.3 = (f32[384,1024]{1,0:T(8,128)S(1)}, f32[384,1024]{1,0:T(8,128)S(1)}, f32[8,1024]{1,0:T(8,128)S(1)}) custom-call(f32[8,1024]{1,0:T(8,128)S(1)} %get-tuple-element.38.refs_0_, bf16[1024,128]{1,0:T(8,128)(2,1)S(1)} %get-tuple-element.39.refs_1_.refs_0_, bf16[1024,128]{1,0:T(8,128)(2,1)S(1)} %get-tuple-element.40.refs_2_.refs_1_, ...), custom_call_target="tpu_custom_call" | custom-call | flops 201326592 | bytes 1572864 | tf_op jit(solution)/shard_map/stage_scores/pallas_call | solution.py:393
  14.5 0.3 %collective-permute-done.6.refs_6_.refs_10_ = bf16[256,128]{1,0:T(8,128)(2,1)S(1)} collective-permute-done((bf16[256,128]{1,0:T(8,128)(2,1)S(1)}, bf16[256,128]{1,0:T(8,128)(2,1)S(1)}, u32[]{:S(2)}, u32[]{:S(2)}) %collective-permute-start.6) | collective-permute-done | bytes 65568 | tf_op jit(solution)/shard_map/ppermute | solution.py:349
  14.9 1.5 %late_scores.1 = (f32[128,1024]{1,0:T(8,128)S(1)}, f32[128,1024]{1,0:T(8,128)S(1)}, f32[8,1024]{1,0:T(8,128)S(1)}, bf16[512,1024]{1,0:T(8,128)(2,1)S(1)}, bf16[5...) custom-call(f32[8,1024]{1,0:T(8,128)S(1)} %get-tuple-element.38.refs_0_, ...), custom_call_target="tpu_custom_call" | custom-call | flops 536870912 | bytes 4194304 | tf_op jit(solution)/shard_map/late_scores/pallas_call | solution.py:417
  16.3 0.2 collective-permute-start.9
  16.6 0.8 %other_grads.1 = (bf16[512,1024]{1,0:T(8,128)(2,1)S(1)}, bf16[512,1024]{1,0:T(8,128)(2,1)S(1)}, f32[4,256,128]{2,1,0:T(8,128)S(1)}) custom-call(bf16[1024,128]{1,0:T(8,128)(2,1)S(1)} %get-tuple-element.39.refs_1_.refs_0_, bf16[1024,128]{1,0:T(8,128)(2,1)S(1)} %get-tuple-element.40.refs_2_.refs_1_, f32[8,1024]{1,0:T(8,128)S(1)} %get-tuple-element.53.refs_2_, ...), custom_call_target="tpu_custom_call" | custom-call | flops 268435456 | bytes 2097152 | tf_op jit(solution)/shard_map/other_grads/pallas_call | solution.py:431
  17.3 0.6 %collective-permute-done.9.from_sib_ref = bf16[4,256,128]{2,1,0:T(8,128)(2,1)S(1)} collective-permute-done((bf16[4,256,128]{2,1,0:T(8,128)(2,1)S(1)}, bf16[4,256,128]{2,1,0:T(8,128)(2,1)S(1)}, u32[]{:S(2)}, u32[]{:S(2)}) %collective-permute-start.9) | collective-permute-done | bytes 262176 | tf_op jit(solution)/shard_map/ppermute | solution.py:349
  18.0 2.7 %collective-permute-start.10 = (bf16[512,128]{1,0:T(8,128)(2,1)S(1)}, bf16[512,128]{1,0:T(8,128)(2,1)S(1)}, u32[]{:S(2)}, u32[]{:S(2)}) collective-permute-start(bf16[512,128]{1,0:T(8,128)(2,1)S(1)} %get-tuple-element.67), channel_id=1, source_target_pairs={{6,0},{4,2},{10,4},{8,6},{14,8},{12,10},{18,12},{16,14},{22,16},{2... | collective-permute-start | bytes 393224 | tf_op jit(solution)/shard_map/ppermute | solution.py:341
  20.7 1.1 %collective-permute-start.12 = (bf16[256,128]{1,0:T(8,128)(2,1)S(1)}, bf16[256,128]{1,0:T(8,128)(2,1)S(1)}, u32[]{:S(2)}, u32[]{:S(2)}) collective-permute-start(bf16[256,128]{1,0:T(8,128)(2,1)S(1)} %get-tuple-element.68), channel_id=1, source_target_pairs={{4,0},{5,1},{6,2},{7,3},{8,4},{9,5},{10,6},{11,7},{12,8},{13,9},{1... | collective-permute-start | bytes 196616 | tf_op jit(solution)/shard_map/ppermute | solution.py:336
  21.9 1.7 %collective-permute-start.13 = (bf16[256,128]{1,0:T(8,128)(2,1)S(1)}, bf16[256,128]{1,0:T(8,128)(2,1)S(1)}, u32[]{:S(2)}, u32[]{:S(2)}) collective-permute-start(bf16[256,128]{1,0:T(8,128)(2,1)S(1)} %get-tuple-element.69), channel_id=1, source_target_pairs={{2,0},{3,1},{8,2},{9,3},{6,4},{7,5},{12,6},{13,7},{10,8},{11,9},{1... | collective-permute-start | bytes 196616 | tf_op jit(solution)/shard_map/ppermute | solution.py:336
  23.6 1.0 %collective-permute-done.10.far_ref = bf16[512,128]{1,0:T(8,128)(2,1)S(1)} collective-permute-done((bf16[512,128]{1,0:T(8,128)(2,1)S(1)}, bf16[512,128]{1,0:T(8,128)(2,1)S(1)}, u32[]{:S(2)}, u32[]{:S(2)}) %collective-permute-start.10) | collective-permute-done | bytes 131104 | tf_op jit(solution)/shard_map/ppermute | solution.py:341
  24.6 0.1 collective-permute-start.11
  24.7 1.6 %query_side.1 = (bf16[128,1024]{1,0:T(8,128)(2,1)}, bf16[128,1024]{1,0:T(8,128)(2,1)}) custom-call(bf16[512,1024]{1,0:T(8,128)(2,1)S(1)} %get-tuple-element.51.refs_0_, bf16[512,1024]{1,0:T(8,128)(2,1)S(1)} %get-tuple-element.52.refs_1_, bf16[512,1024]{1,0:T(8,128)(2,1)S(1)} %get-tuple-element.60.refs_2_, bf16[512,1024]{1,0:T(8,128)(2,1)S(1)} %get-tuple-element.61.refs_3_, ...), custom_call_target="tpu_custom_call" | custom-call | flops 536870912 | bytes 4194304 | tf_op jit(solution)/shard_map/query_side/pallas_call | solution.py:441
  26.3 0.1 collective-permute-done.13.refs_1_
  26.4 0.7 %total_grads.1 = (bf16[128,128]{1,0:T(8,128)(2,1)}, bf16[128,128]{1,0:T(8,128)(2,1)}) custom-call(f32[4,256,128]{2,1,0:T(8,128)S(1)} %get-tuple-element.64.mine_ref, bf16[512,128]{1,0:T(8,128)(2,1)S(1)} %collective-permute-done.10.far_ref, bf16[256,128]{1,0:T(8,128)(2,1)S(1)} %collective-permute-done.11.passed_ref, ...), custom_call_target="tpu_custom_call" | custom-call | tf_op jit(solution)/shard_map/total_grads/pallas_call | solution.py:483
  (14 shorter events, 0.1 us)
Async XLA Ops:
  1.4 8.6 %collective-permute-start.2 = (bf16[256,128]{1,0:T(8,128)(2,1)S(1)}, bf16[256,128]{1,0:T(8,128)(2,1)S(1)}, u32[]{:S(2)}, u32[]{:S(2)}) collective-permute-start(bf16[256,128]{1,0:T(8,128)(2,1)S(1)} %pair_up.1.own_ref.refs_7_), channel_id=1, source_target_pairs={{0,2},{1,3},{2,8},{3,9},{4,6},{5,7},{6,12},{7,13},{8,10},{9,11},{1... | collective-permute-start | bytes 196616 | tf_op jit(solution)/shard_map/ppermute | solution.py:336
  4.4 7.5 %collective-permute-start.3 = (bf16[256,128]{1,0:T(8,128)(2,1)S(1)}, bf16[256,128]{1,0:T(8,128)(2,1)S(1)}, u32[]{:S(2)}, u32[]{:S(2)}) collective-permute-start(bf16[256,128]{1,0:T(8,128)(2,1)S(1)} %pair_up.1.own_ref.refs_7_), channel_id=1, source_target_pairs={{0,4},{1,5},{2,6},{3,7},{4,8},{5,9},{6,10},{7,11},{8,12},{9,13},{1... | collective-permute-start | bytes 196616 | tf_op jit(solution)/shard_map/ppermute | solution.py:336
  5.9 7.1 %collective-permute-start.1 = (bf16[256,128]{1,0:T(8,128)(2,1)S(1)}, bf16[256,128]{1,0:T(8,128)(2,1)S(1)}, u32[]{:S(2)}, u32[]{:S(2)}) collective-permute-start(bf16[256,128]{1,0:T(8,128)(2,1)S(1)} %pair_up.1.own_ref.refs_7_), channel_id=1, source_target_pairs={{0,6},{1,7},{2,4},{3,5},{4,10},{5,11},{6,8},{7,9},{8,14},{9,15},{1... | collective-permute-start | bytes 196616 | tf_op jit(solution)/shard_map/ppermute | solution.py:336
  8.4 4.6 %collective-permute-start = (bf16[256,128]{1,0:T(8,128)(2,1)S(1)}, bf16[256,128]{1,0:T(8,128)(2,1)S(1)}, u32[]{:S(2)}, u32[]{:S(2)}) collective-permute-start(bf16[256,128]{1,0:T(8,128)(2,1)S(1)} %pair_up.1.own_ref.refs_7_), channel_id=1, source_target_pairs={{1,9},{3,11},{5,13},{7,15},{9,17},{11,19},{13,21},{15,23},{17,25},... | collective-permute-start | bytes 196616 | tf_op jit(solution)/shard_map/ppermute | solution.py:346
  11.9 1.8 %collective-permute-start.5 = (bf16[256,128]{1,0:T(8,128)(2,1)S(1)}, bf16[256,128]{1,0:T(8,128)(2,1)S(1)}, u32[]{:S(2)}, u32[]{:S(2)}) collective-permute-start(bf16[256,128]{1,0:T(8,128)(2,1)S(1)} %collective-permute-done.3.refs_5_.refs_9_), channel_id=1, source_target_pairs={{0,1},{1,0},{2,3},{3,2},{4,5},{5,4},{6,7},{7,6},{8,9},{9,8},{10,11... | collective-permute-start | bytes 196616 | tf_op jit(solution)/shard_map/ppermute | solution.py:349
  11.9 1.8 %collective-permute-start.4 = (bf16[256,128]{1,0:T(8,128)(2,1)S(1)}, bf16[256,128]{1,0:T(8,128)(2,1)S(1)}, u32[]{:S(2)}, u32[]{:S(2)}) collective-permute-start(bf16[256,128]{1,0:T(8,128)(2,1)S(1)} %collective-permute-done.2.refs_4_.refs_8_), channel_id=1, source_target_pairs={{0,1},{1,0},{2,3},{3,2},{4,5},{5,4},{6,7},{7,6},{8,9},{9,8},{10,11... | collective-permute-start | bytes 196616 | tf_op jit(solution)/shard_map/ppermute | solution.py:349
  12.4 2.1 %collective-permute-start.8 = (bf16[256,128]{1,0:T(8,128)(2,1)S(1)}, bf16[256,128]{1,0:T(8,128)(2,1)S(1)}, u32[]{:S(2)}, u32[]{:S(2)}) collective-permute-start(bf16[256,128]{1,0:T(8,128)(2,1)S(1)} %pair_up.1.own_ref.refs_7_), channel_id=1, source_target_pairs={{0,1},{1,0},{2,3},{3,2},{4,5},{5,4},{6,7},{7,6},{8,9},{9,8},{10,11... | collective-permute-start | bytes 196616 | tf_op jit(solution)/shard_map/ppermute | solution.py:349
  13.0 1.5 %collective-permute-start.7 = (bf16[256,128]{1,0:T(8,128)(2,1)S(1)}, bf16[256,128]{1,0:T(8,128)(2,1)S(1)}, u32[]{:S(2)}, u32[]{:S(2)}) collective-permute-start(bf16[256,128]{1,0:T(8,128)(2,1)S(1)} %collective-permute-done), channel_id=1, source_target_pairs={{0,1},{1,0},{2,3},{3,2},{4,5},{5,4},{6,7},{7,6},{8,9},{9,8},{10,11... | collective-permute-start | bytes 196616 | tf_op jit(solution)/shard_map/ppermute | solution.py:349
  13.6 1.3 %collective-permute-start.6 = (bf16[256,128]{1,0:T(8,128)(2,1)S(1)}, bf16[256,128]{1,0:T(8,128)(2,1)S(1)}, u32[]{:S(2)}, u32[]{:S(2)}) collective-permute-start(bf16[256,128]{1,0:T(8,128)(2,1)S(1)} %collective-permute-done.1.refs_6_), channel_id=1, source_target_pairs={{0,1},{1,0},{2,3},{3,2},{4,5},{5,4},{6,7},{7,6},{8,9},{9,8},{10,11... | collective-permute-start | bytes 196616 | tf_op jit(solution)/shard_map/ppermute | solution.py:349
  16.3 1.6 %collective-permute-start.9 = (bf16[4,256,128]{2,1,0:T(8,128)(2,1)S(1)}, bf16[4,256,128]{2,1,0:T(8,128)(2,1)S(1)}, u32[]{:S(2)}, u32[]{:S(2)}) collective-permute-start(bf16[4,256,128]{2,1,0:T(8,128)(2,1)S(1)} %get-tuple-element.66), channel_id=1, source_target_pairs={{0,1},{1,0},{2,3},{3,2},{4,5},{5,4},{6,7},{7,6},{8,9},{9,8},{10,11... | collective-permute-start | bytes 786440 | tf_op jit(solution)/shard_map/ppermute | solution.py:349
  18.0 6.6 %collective-permute-start.10 = (bf16[512,128]{1,0:T(8,128)(2,1)S(1)}, bf16[512,128]{1,0:T(8,128)(2,1)S(1)}, u32[]{:S(2)}, u32[]{:S(2)}) collective-permute-start(bf16[512,128]{1,0:T(8,128)(2,1)S(1)} %get-tuple-element.67), channel_id=1, source_target_pairs={{6,0},{4,2},{10,4},{8,6},{14,8},{12,10},{18,12},{16,14},{22,16},{2... | collective-permute-start | bytes 393224 | tf_op jit(solution)/shard_map/ppermute | solution.py:341
  20.7 5.6 %collective-permute-start.12 = (bf16[256,128]{1,0:T(8,128)(2,1)S(1)}, bf16[256,128]{1,0:T(8,128)(2,1)S(1)}, u32[]{:S(2)}, u32[]{:S(2)}) collective-permute-start(bf16[256,128]{1,0:T(8,128)(2,1)S(1)} %get-tuple-element.68), channel_id=1, source_target_pairs={{4,0},{5,1},{6,2},{7,3},{8,4},{9,5},{10,6},{11,7},{12,8},{13,9},{1... | collective-permute-start | bytes 196616 | tf_op jit(solution)/shard_map/ppermute | solution.py:336
  21.9 4.5 %collective-permute-start.13 = (bf16[256,128]{1,0:T(8,128)(2,1)S(1)}, bf16[256,128]{1,0:T(8,128)(2,1)S(1)}, u32[]{:S(2)}, u32[]{:S(2)}) collective-permute-start(bf16[256,128]{1,0:T(8,128)(2,1)S(1)} %get-tuple-element.69), channel_id=1, source_target_pairs={{2,0},{3,1},{8,2},{9,3},{6,4},{7,5},{12,6},{13,7},{10,8},{11,9},{1... | collective-permute-start | bytes 196616 | tf_op jit(solution)/shard_map/ppermute | solution.py:336
  24.6 1.8 %collective-permute-start.11 = (bf16[256,128]{1,0:T(8,128)(2,1)S(1)}, bf16[256,128]{1,0:T(8,128)(2,1)S(1)}, u32[]{:S(2)}, u32[]{:S(2)}) collective-permute-start(bf16[256,128]{1,0:T(8,128)(2,1)S(1)} %pass_on.1), channel_id=1, source_target_pairs={{0,1},{1,0},{2,3},{3,2},{4,5},{5,4},{6,7},{7,6},{8,9},{9,8},{10,11... | collective-permute-start | bytes 196616 | tf_op jit(solution)/shard_map/ppermute | solution.py:349

commit v7 on v6

--- a/solution.py
+++ b/solution.py
@@ -186,7 +186,7 @@
 def late_kernel(slots, *refs):
     bias_ref, query_rows, grad_rows, powers_ref, probs_ref, before_ref = refs[:6]
     sib_ref, far_ref, sib_own_ref = refs[6:9]
-    keep_powers, keep_probs, final_ref, weights_ref, score_grad_ref, swap_ref, lin_ref, last_ref = refs[9:]
+    keep_powers, keep_probs, final_ref, weights_ref, score_grad_ref, far_out, rest_out, lin_ref, last_ref = refs[9:]
     _, _, core = position()
     even = core == 0
     half = slots.half
@@ -220,8 +220,9 @@
     key_grad = dot(score_grad_ref[...], query_rows[...], 1, 0) * SCALE
     value_grad = dot(weights_ref[...], grad_rows[...], 1, 0)
     for k in range(half):
-        swap_ref[k, :BLOCK, :] = key_grad[rows_of(k), :].astype(jnp.bfloat16)
-        swap_ref[k, BLOCK:, :] = value_grad[rows_of(k), :].astype(jnp.bfloat16)
+        ref, at = (rest_out, k) if k < half - 2 else (far_out, k - (half - 2))
+        ref[at, :BLOCK, :] = key_grad[rows_of(k), :].astype(jnp.bfloat16)
+        ref[at, BLOCK:, :] = value_grad[rows_of(k), :].astype(jnp.bfloat16)
     lin_ref[:BLOCK, :] = key_grad[rows_of(half - 1), :]
     lin_ref[BLOCK:, :] = value_grad[rows_of(half - 1), :]
 
@@ -275,15 +276,17 @@
     query_grad_copy.wait()
 
 
-def merge_kernel(mine_ref, lin_ref, from_sib_ref, *sent_refs):
-    half = mine_ref.shape[0]
-    f32, bf16 = jnp.float32, jnp.bfloat16
-    for k, ref in enumerate(sent_refs[:-1]):
-        ref[...] = (mine_ref[k + 1] + from_sib_ref[k].astype(f32)).astype(bf16)
+def merge_far_kernel(mine_ref, lin_ref, from_sib_ref, sent_ref):
     _, _, core = position()
-    far = from_sib_ref[half - 2].astype(f32)
-    sent_refs[-1][: 2 * BLOCK, :] = (jnp.where(core == 0, lin_ref[...], 0.0) + far).astype(bf16)
-    sent_refs[-1][2 * BLOCK :, :] = (mine_ref[half - 1] + from_sib_ref[half - 1].astype(f32)).astype(bf16)
+    far = from_sib_ref[0].astype(jnp.float32) + jnp.where(core == 0, lin_ref[...], 0.0)
+    other = from_sib_ref[1].astype(jnp.float32) + mine_ref[mine_ref.shape[0] - 1]
+    sent_ref[: 2 * BLOCK, :] = far.astype(jnp.bfloat16)
+    sent_ref[2 * BLOCK :, :] = other.astype(jnp.bfloat16)
+
+
+def merge_rest_kernel(mine_ref, from_sib_ref, *sent_refs):
+    for k, ref in enumerate(sent_refs):
+        ref[...] = (mine_ref[k + 1] + from_sib_ref[k].astype(jnp.float32)).astype(jnp.bfloat16)
 
 
 def pass_kernel(mine_ref, far_ref, out_ref):
@@ -414,19 +417,20 @@
 
     sib, far, near = held[slots.late[0]], held["last"], sib_own
     weights = [pltpu.VMEM((half * BLOCK, FLAT), bf16)] * 2
-    *keep, final, swap_weights, swap_score_grad, swap_out, lin_out = pl.pallas_call(
+    *keep, final, swap_weights, swap_score_grad, far_out, rest_out, lin_out = pl.pallas_call(
         functools.partial(late_kernel, slots),
         out_shape=stage(1)
         + weights
-        + [pltpu.VMEM((half, 2 * BLOCK, HEAD_DIM), bf16), pltpu.VMEM((2 * BLOCK, HEAD_DIM), f32)],
+        + [pltpu.VMEM((blocks, 2 * BLOCK, HEAD_DIM), bf16) for blocks in (2, half - 2)]
+        + [pltpu.VMEM((2 * BLOCK, HEAD_DIM), f32)],
         in_specs=[VMEM] * 9,
-        out_specs=[VMEM] * 7,
+        out_specs=[VMEM] * 8,
         scratch_shapes=[pltpu.VMEM((2 * BLOCK, HEAD_DIM), bf16)],
         compiler_params=params,
         cost_estimate=cost(window, 2),
         name="late_scores",
     )(bias, query_rows, grad_rows, *closing_stage, sib, far, near)
-    from_sib = swapped(swap_out)
+    far_from_sib, rest_from_sib = swapped(far_out), swapped(rest_out)
 
     mine_weights, mine_score_grad, mine = pl.pallas_call(
         functools.partial(mine_kernel, slots),
@@ -460,14 +464,22 @@
     )
 
     block = pltpu.VMEM((2 * BLOCK, HEAD_DIM), bf16)
-    *sent, sent_far = pl.pallas_call(
-        merge_kernel,
-        out_shape=[block] * (half - 2) + [pltpu.VMEM((4 * BLOCK, HEAD_DIM), bf16)],
+    sent_far = pl.pallas_call(
+        merge_far_kernel,
+        out_shape=pltpu.VMEM((4 * BLOCK, HEAD_DIM), bf16),
         in_specs=[VMEM] * 3,
-        out_specs=[VMEM] * (half - 1),
+        out_specs=VMEM,
         compiler_params=small,
-        name="merge_siblings",
-    )(mine, lin_out, from_sib)
+        name="merge_far",
+    )(mine, lin_out, far_from_sib)
+    sent = pl.pallas_call(
+        merge_rest_kernel,
+        out_shape=[block] * (half - 2),
+        in_specs=[VMEM] * 2,
+        out_specs=[VMEM] * (half - 2),
+        compiler_params=small,
+        name="merge_rest",
+    )(mine, rest_from_sib)
     back_far = back_mixed(sent_far)
     passed = swapped(
         pl.pallas_call(

time: 27.3 us -> 27.1 us (level)
  waiting for transfers between devices: 4 us -> 3.37 us
  starting transfers between devices: 14.1 us -> 14.5 us
    ppermute x7 -> x8, waiting for transfers between devices: 0.95 us -> 0.41 us  [swapped(): return lax.ppermute(block, AXES, [(i, i ^ 1) for i in range(devices)])]
    ppermute x7 -> x8, starting transfers between devices: 1.45 us -> 1.81 us  [swapped(): return lax.ppermute(block, AXES, [(i, i ^ 1) for i in range(devices)])]
  transfers between devices with their start and end apart: 14 -> 15, of which waited for: 5 -> 4; matrix products, arithmetic and copies ran while one was open for 0% -> 0% of each run, Pallas kernels for 20% -> 20%
where the time goes in v7:
time: 27.1 us; the launch traced here: 26.9 us
  starting transfers between devices  14.5 us (54%)
  Pallas kernels  8.26 us (30%)
  waiting for transfers between devices  3.37 us (12%)
  between operations  0.76 us (3%)
    ppermute x5, starting transfers between devices, ahead(): lax.ppermute(block, AXES, [pair[::-1] for pair in route] if back else route)  9.91 us
    ppermute x1, starting transfers between devices, back_mixed(): return lax.ppermute(block, AXES, route)  2.74 us
    ppermute x5, waiting for transfers between devices, ahead(): lax.ppermute(block, AXES, [pair[::-1] for pair in route] if back else route)  2.01 us
    ppermute x8, starting transfers between devices, swapped(): return lax.ppermute(block, AXES, [(i, i ^ 1) for i in range(devices)])  1.81 us
    pallas_call x1, Pallas kernels, local(): pl.pallas_call(functools.partial(query_side_kernel, slots), out_shape=[sh...  1.57 us
    pallas_call x1, Pallas kernels, local(): pl.pallas_call(functools.partial(own_kernel, slots), out_shape=[pltpu.VME...  1.54 us
    pallas_call x1, Pallas kernels, local(): pl.pallas_call(functools.partial(late_kernel, slots), out_shape=stage(1)...  1.46 us
    pallas_call x2, Pallas kernels, next_stage(): pl.pallas_call(functools.partial(stage_kernel, first, len(group)), out_sh...  1.38 us
  transfers between devices with their start and end apart: 15, of which 4 were waited for; matrix products, arithmetic and copies ran while one was open for 0% of the time, Pallas kernels for 20%

profile of v7, /device:TPU:0, one launch (start us, length us, event | category | flops | bytes accessed | tf_op | source)
XLA Modules:
  0.0 26.9 jit_solution(16629101562987774393)
XLA Ops:
  0.6 0.8 %pair_up.1.own_ref.refs_7_ = bf16[256,128]{1,0:T(8,128)(2,1)S(1)} custom-call(bf16[128,128]{1,0:T(8,128)(2,1)} %key_ref.1, bf16[128,128]{1,0:T(8,128)(2,1)} %value_ref.1), custom_call_target="tpu_custom_call" | custom-call | tf_op jit(solution)/shard_map/pair_up/pallas_call | solution.py:354
  1.4 3.0 %collective-permute-start.2 = (bf16[256,128]{1,0:T(8,128)(2,1)S(1)}, bf16[256,128]{1,0:T(8,128)(2,1)S(1)}, u32[]{:S(2)}, u32[]{:S(2)}) collective-permute-start(bf16[256,128]{1,0:T(8,128)(2,1)S(1)} %pair_up.1.own_ref.refs_7_), channel_id=1, source_target_pairs={{0,2},{1,3},{2,8},{3,9},{4,6},{5,7},{6,12},{7,13},{8,10},{9,11},{1... | collective-permute-start | bytes 196616 | tf_op jit(solution)/shard_map/ppermute | solution.py:339
  4.4 1.5 %collective-permute-start.3 = (bf16[256,128]{1,0:T(8,128)(2,1)S(1)}, bf16[256,128]{1,0:T(8,128)(2,1)S(1)}, u32[]{:S(2)}, u32[]{:S(2)}) collective-permute-start(bf16[256,128]{1,0:T(8,128)(2,1)S(1)} %pair_up.1.own_ref.refs_7_), channel_id=1, source_target_pairs={{0,4},{1,5},{2,6},{3,7},{4,8},{5,9},{6,10},{7,11},{8,12},{9,13},{1... | collective-permute-start | bytes 196616 | tf_op jit(solution)/shard_map/ppermute | solution.py:339
  5.9 2.5 %collective-permute-start.1 = (bf16[256,128]{1,0:T(8,128)(2,1)S(1)}, bf16[256,128]{1,0:T(8,128)(2,1)S(1)}, u32[]{:S(2)}, u32[]{:S(2)}) collective-permute-start(bf16[256,128]{1,0:T(8,128)(2,1)S(1)} %pair_up.1.own_ref.refs_7_), channel_id=1, source_target_pairs={{0,6},{1,7},{2,4},{3,5},{4,10},{5,11},{6,8},{7,9},{8,14},{9,15},{1... | collective-permute-start | bytes 196616 | tf_op jit(solution)/shard_map/ppermute | solution.py:339
  8.4 1.5 %own_scores.1 = (bf16[1024,128]{1,0:T(8,128)(2,1)S(1)}, bf16[1024,128]{1,0:T(8,128)(2,1)S(1)}, f32[8,1024]{1,0:T(8,128)S(1)}, f32[128,1024]{1,0:T(8,128)S(1)}, f...) custom-call(s32[32]{0:T(128)} %doc_hbm.1, bf16[128,1024]{1,0:T(8,128)(2,1)} %query_ref.1, bf16[128,1024]{1,0:T(8,128)(2,1)} %grad_ref.1, ...), custom_call_target="tpu_custom_call" | custom-call | flops 67108864 | bytes 524288 | tf_op jit(solution)/shard_map/own_scores/pallas_call | solution.py:373
  10.0 1.9 %collective-permute-done.3.refs_5_.refs_9_ = bf16[256,128]{1,0:T(8,128)(2,1)S(1)} collective-permute-done((bf16[256,128]{1,0:T(8,128)(2,1)S(1)}, bf16[256,128]{1,0:T(8,128)(2,1)S(1)}, u32[]{:S(2)}, u32[]{:S(2)}) %collective-permute-start.3) | collective-permute-done | bytes 65568 | tf_op jit(solution)/shard_map/ppermute | solution.py:339
  11.9 0.5 %collective-permute-start.4 = (bf16[256,128]{1,0:T(8,128)(2,1)S(1)}, bf16[256,128]{1,0:T(8,128)(2,1)S(1)}, u32[]{:S(2)}, u32[]{:S(2)}) collective-permute-start(bf16[256,128]{1,0:T(8,128)(2,1)S(1)} %collective-permute-done.2.refs_4_.refs_8_), channel_id=1, source_target_pairs={{0,1},{1,0},{2,3},{3,2},{4,5},{5,4},{6,7},{7,6},{8,9},{9,8},{10,11... | collective-permute-start | bytes 196616 | tf_op jit(solution)/shard_map/ppermute | solution.py:352
  12.4 0.6 %stage_scores.2 = (f32[256,1024]{1,0:T(8,128)S(1)}, f32[256,1024]{1,0:T(8,128)S(1)}, f32[8,1024]{1,0:T(8,128)S(1)}) custom-call(f32[8,1024]{1,0:T(8,128)S(1)} %get-tuple-element.38.refs_0_, bf16[1024,128]{1,0:T(8,128)(2,1)S(1)} %get-tuple-element.39.refs_1_.refs_0_, bf16[1024,128]{1,0:T(8,128)(2,1)S(1)} %get-tuple-element.40.refs_2_.refs_1_, ...), custom_call_target="tpu_custom_call" | custom-call | flops 134217728 | bytes 1048576 | tf_op jit(solution)/shard_map/stage_scores/pallas_call | solution.py:396
  13.0 0.6 %collective-permute-start.7 = (bf16[256,128]{1,0:T(8,128)(2,1)S(1)}, bf16[256,128]{1,0:T(8,128)(2,1)S(1)}, u32[]{:S(2)}, u32[]{:S(2)}) collective-permute-start(bf16[256,128]{1,0:T(8,128)(2,1)S(1)} %collective-permute-done), channel_id=1, source_target_pairs={{0,1},{1,0},{2,3},{3,2},{4,5},{5,4},{6,7},{7,6},{8,9},{9,8},{10,11... | collective-permute-start | bytes 196616 | tf_op jit(solution)/shard_map/ppermute | solution.py:352
  13.6 0.1 collective-permute-start.6
  13.7 0.8 %stage_scores.3 = (f32[384,1024]{1,0:T(8,128)S(1)}, f32[384,1024]{1,0:T(8,128)S(1)}, f32[8,1024]{1,0:T(8,128)S(1)}) custom-call(f32[8,1024]{1,0:T(8,128)S(1)} %get-tuple-element.38.refs_0_, bf16[1024,128]{1,0:T(8,128)(2,1)S(1)} %get-tuple-element.39.refs_1_.refs_0_, bf16[1024,128]{1,0:T(8,128)(2,1)S(1)} %get-tuple-element.40.refs_2_.refs_1_, ...), custom_call_target="tpu_custom_call" | custom-call | flops 201326592 | bytes 1572864 | tf_op jit(solution)/shard_map/stage_scores/pallas_call | solution.py:396
  14.5 0.3 %collective-permute-done.6.refs_6_.refs_10_ = bf16[256,128]{1,0:T(8,128)(2,1)S(1)} collective-permute-done((bf16[256,128]{1,0:T(8,128)(2,1)S(1)}, bf16[256,128]{1,0:T(8,128)(2,1)S(1)}, u32[]{:S(2)}, u32[]{:S(2)}) %collective-permute-start.6) | collective-permute-done | bytes 65568 | tf_op jit(solution)/shard_map/ppermute | solution.py:352
  14.9 1.5 %late_scores.1 = (f32[128,1024]{1,0:T(8,128)S(1)}, f32[128,1024]{1,0:T(8,128)S(1)}, f32[8,1024]{1,0:T(8,128)S(1)}, bf16[512,1024]{1,0:T(8,128)(2,1)S(1)}, bf16[5...) custom-call(f32[8,1024]{1,0:T(8,128)S(1)} %get-tuple-element.38.refs, ...), custom_call_target="tpu_custom_call" | custom-call | flops 536870912 | bytes 4194304 | tf_op jit(solution)/shard_map/late_scores/pallas_call | solution.py:420
  16.3 0.2 collective-permute-start.9
  16.6 0.4 %collective-permute-start.12 = (bf16[2,256,128]{2,1,0:T(8,128)(2,1)S(1)}, bf16[2,256,128]{2,1,0:T(8,128)(2,1)S(1)}, u32[]{:S(2)}, u32[]{:S(2)}) collective-permute-start(bf16[2,256,128]{2,1,0:T(8,128)(2,1)S(1)} %get-tuple-element.67), channel_id=1, source_target_pairs={{0,1},{1,0},{2,3},{3,2},{4,5},{5,4},{6,7},{7,6},{8,9},{9,8},{10,11... | collective-permute-start | bytes 393224 | tf_op jit(solution)/shard_map/ppermute | solution.py:352
  16.9 0.8 %other_grads.1 = (bf16[512,1024]{1,0:T(8,128)(2,1)S(1)}, bf16[512,1024]{1,0:T(8,128)(2,1)S(1)}, f32[4,256,128]{2,1,0:T(8,128)S(1)}) custom-call(bf16[1024,128]{1,0:T(8,128)(2,1)S(1)} %get-tuple-element.39.refs_1_.refs_0_, bf16[1024,128]{1,0:T(8,128)(2,1)S(1)} %get-tuple-element.40.refs_2_.refs_1_, f32[8,1024]{1,0:T(8,128)S(1)} %get-tuple-element.53.refs_2_, ...), custom_call_target="tpu_custom_call" | custom-call | flops 268435456 | bytes 2097152 | tf_op jit(solution)/shard_map/other_grads/pallas_call | solution.py:435
  17.8 2.7 %collective-permute-start.10 = (bf16[512,128]{1,0:T(8,128)(2,1)S(1)}, bf16[512,128]{1,0:T(8,128)(2,1)S(1)}, u32[]{:S(2)}, u32[]{:S(2)}) collective-permute-start(bf16[512,128]{1,0:T(8,128)(2,1)S(1)} %merge_far.1), channel_id=1, source_target_pairs={{6,0},{4,2},{10,4},{8,6},{14,8},{12,10},{18,12},{16,14},{22,16},{2... | collective-permute-start | bytes 393224 | tf_op jit(solution)/shard_map/ppermute | solution.py:344
  20.5 1.2 %collective-permute-start.13 = (bf16[256,128]{1,0:T(8,128)(2,1)S(1)}, bf16[256,128]{1,0:T(8,128)(2,1)S(1)}, u32[]{:S(2)}, u32[]{:S(2)}) collective-permute-start(bf16[256,128]{1,0:T(8,128)(2,1)S(1)} %get-tuple-element.68), channel_id=1, source_target_pairs={{4,0},{5,1},{6,2},{7,3},{8,4},{9,5},{10,6},{11,7},{12,8},{13,9},{1... | collective-permute-start | bytes 196616 | tf_op jit(solution)/shard_map/ppermute | solution.py:339
  21.7 1.7 %collective-permute-start.14 = (bf16[256,128]{1,0:T(8,128)(2,1)S(1)}, bf16[256,128]{1,0:T(8,128)(2,1)S(1)}, u32[]{:S(2)}, u32[]{:S(2)}) collective-permute-start(bf16[256,128]{1,0:T(8,128)(2,1)S(1)} %get-tuple-element.69), channel_id=1, source_target_pairs={{2,0},{3,1},{8,2},{9,3},{6,4},{7,5},{12,6},{13,7},{10,8},{11,9},{1... | collective-permute-start | bytes 196616 | tf_op jit(solution)/shard_map/ppermute | solution.py:339
  23.4 1.0 %collective-permute-done.10.far_ref = bf16[512,128]{1,0:T(8,128)(2,1)S(1)} collective-permute-done((bf16[512,128]{1,0:T(8,128)(2,1)S(1)}, bf16[512,128]{1,0:T(8,128)(2,1)S(1)}, u32[]{:S(2)}, u32[]{:S(2)}) %collective-permute-start.10) | collective-permute-done | bytes 131104 | tf_op jit(solution)/shard_map/ppermute | solution.py:344
  24.4 0.1 collective-permute-start.11
  24.5 1.6 %query_side.1 = (bf16[128,1024]{1,0:T(8,128)(2,1)}, bf16[128,1024]{1,0:T(8,128)(2,1)}) custom-call(bf16[512,1024]{1,0:T(8,128)(2,1)S(1)} %get-tuple-element.51.refs_0_, bf16[512,1024]{1,0:T(8,128)(2,1)S(1)} %get-tuple-element.52.refs_1_, bf16[512,1024]{1,0:T(8,128)(2,1)S(1)} %get-tuple-element.60.refs_2_, bf16[512,1024]{1,0:T(8,128)(2,1)S(1)} %get-tuple-element.61.refs_3_, ...), custom_call_target="tpu_custom_call" | custom-call | flops 536870912 | bytes 4194304 | tf_op jit(solution)/shard_map/query_side/pallas_call | solution.py:445
  26.1 0.1 collective-permute-done.14.refs_1_
  26.2 0.7 %total_grads.1 = (bf16[128,128]{1,0:T(8,128)(2,1)}, bf16[128,128]{1,0:T(8,128)(2,1)}) custom-call(f32[4,256,128]{2,1,0:T(8,128)S(1)} %get-tuple-element.64.mine_ref, bf16[512,128]{1,0:T(8,128)(2,1)S(1)} %collective-permute-done.10.far_ref, bf16[256,128]{1,0:T(8,128)(2,1)S(1)} %collective-permute-done.11.passed_ref, ...), custom_call_target="tpu_custom_call" | custom-call | tf_op jit(solution)/shard_map/total_grads/pallas_call | solution.py:495
  (17 shorter events, 0.2 us)
Async XLA Ops:
  1.4 8.6 %collective-permute-start.2 = (bf16[256,128]{1,0:T(8,128)(2,1)S(1)}, bf16[256,128]{1,0:T(8,128)(2,1)S(1)}, u32[]{:S(2)}, u32[]{:S(2)}) collective-permute-start(bf16[256,128]{1,0:T(8,128)(2,1)S(1)} %pair_up.1.own_ref.refs_7_), channel_id=1, source_target_pairs={{0,2},{1,3},{2,8},{3,9},{4,6},{5,7},{6,12},{7,13},{8,10},{9,11},{1... | collective-permute-start | bytes 196616 | tf_op jit(solution)/shard_map/ppermute | solution.py:339
  4.4 7.5 %collective-permute-start.3 = (bf16[256,128]{1,0:T(8,128)(2,1)S(1)}, bf16[256,128]{1,0:T(8,128)(2,1)S(1)}, u32[]{:S(2)}, u32[]{:S(2)}) collective-permute-start(bf16[256,128]{1,0:T(8,128)(2,1)S(1)} %pair_up.1.own_ref.refs_7_), channel_id=1, source_target_pairs={{0,4},{1,5},{2,6},{3,7},{4,8},{5,9},{6,10},{7,11},{8,12},{9,13},{1... | collective-permute-start | bytes 196616 | tf_op jit(solution)/shard_map/ppermute | solution.py:339
  5.9 7.1 %collective-permute-start.1 = (bf16[256,128]{1,0:T(8,128)(2,1)S(1)}, bf16[256,128]{1,0:T(8,128)(2,1)S(1)}, u32[]{:S(2)}, u32[]{:S(2)}) collective-permute-start(bf16[256,128]{1,0:T(8,128)(2,1)S(1)} %pair_up.1.own_ref.refs_7_), channel_id=1, source_target_pairs={{0,6},{1,7},{2,4},{3,5},{4,10},{5,11},{6,8},{7,9},{8,14},{9,15},{1... | collective-permute-start | bytes 196616 | tf_op jit(solution)/shard_map/ppermute | solution.py:339
  8.4 4.6 %collective-permute-start = (bf16[256,128]{1,0:T(8,128)(2,1)S(1)}, bf16[256,128]{1,0:T(8,128)(2,1)S(1)}, u32[]{:S(2)}, u32[]{:S(2)}) collective-permute-start(bf16[256,128]{1,0:T(8,128)(2,1)S(1)} %pair_up.1.own_ref.refs_7_), channel_id=1, source_target_pairs={{1,9},{3,11},{5,13},{7,15},{9,17},{11,19},{13,21},{15,23},{17,25},... | collective-permute-start | bytes 196616 | tf_op jit(solution)/shard_map/ppermute | solution.py:349
  11.9 1.8 %collective-permute-start.5 = (bf16[256,128]{1,0:T(8,128)(2,1)S(1)}, bf16[256,128]{1,0:T(8,128)(2,1)S(1)}, u32[]{:S(2)}, u32[]{:S(2)}) collective-permute-start(bf16[256,128]{1,0:T(8,128)(2,1)S(1)} %collective-permute-done.3.refs_5_.refs_9_), channel_id=1, source_target_pairs={{0,1},{1,0},{2,3},{3,2},{4,5},{5,4},{6,7},{7,6},{8,9},{9,8},{10,11... | collective-permute-start | bytes 196616 | tf_op jit(solution)/shard_map/ppermute | solution.py:352
  11.9 1.8 %collective-permute-start.4 = (bf16[256,128]{1,0:T(8,128)(2,1)S(1)}, bf16[256,128]{1,0:T(8,128)(2,1)S(1)}, u32[]{:S(2)}, u32[]{:S(2)}) collective-permute-start(bf16[256,128]{1,0:T(8,128)(2,1)S(1)} %collective-permute-done.2.refs_4_.refs_8_), channel_id=1, source_target_pairs={{0,1},{1,0},{2,3},{3,2},{4,5},{5,4},{6,7},{7,6},{8,9},{9,8},{10,11... | collective-permute-start | bytes 196616 | tf_op jit(solution)/shard_map/ppermute | solution.py:352
  12.4 2.1 %collective-permute-start.8 = (bf16[256,128]{1,0:T(8,128)(2,1)S(1)}, bf16[256,128]{1,0:T(8,128)(2,1)S(1)}, u32[]{:S(2)}, u32[]{:S(2)}) collective-permute-start(bf16[256,128]{1,0:T(8,128)(2,1)S(1)} %pair_up.1.own_ref.refs_7_), channel_id=1, source_target_pairs={{0,1},{1,0},{2,3},{3,2},{4,5},{5,4},{6,7},{7,6},{8,9},{9,8},{10,11... | collective-permute-start | bytes 196616 | tf_op jit(solution)/shard_map/ppermute | solution.py:352
  13.0 1.5 %collective-permute-start.7 = (bf16[256,128]{1,0:T(8,128)(2,1)S(1)}, bf16[256,128]{1,0:T(8,128)(2,1)S(1)}, u32[]{:S(2)}, u32[]{:S(2)}) collective-permute-start(bf16[256,128]{1,0:T(8,128)(2,1)S(1)} %collective-permute-done), channel_id=1, source_target_pairs={{0,1},{1,0},{2,3},{3,2},{4,5},{5,4},{6,7},{7,6},{8,9},{9,8},{10,11... | collective-permute-start | bytes 196616 | tf_op jit(solution)/shard_map/ppermute | solution.py:352
  13.6 1.3 %collective-permute-start.6 = (bf16[256,128]{1,0:T(8,128)(2,1)S(1)}, bf16[256,128]{1,0:T(8,128)(2,1)S(1)}, u32[]{:S(2)}, u32[]{:S(2)}) collective-permute-start(bf16[256,128]{1,0:T(8,128)(2,1)S(1)} %collective-permute-done.1.refs_6_), channel_id=1, source_target_pairs={{0,1},{1,0},{2,3},{3,2},{4,5},{5,4},{6,7},{7,6},{8,9},{9,8},{10,11... | collective-permute-start | bytes 196616 | tf_op jit(solution)/shard_map/ppermute | solution.py:352
  16.3 1.4 %collective-permute-start.9 = (bf16[2,256,128]{2,1,0:T(8,128)(2,1)S(1)}, bf16[2,256,128]{2,1,0:T(8,128)(2,1)S(1)}, u32[]{:S(2)}, u32[]{:S(2)}) collective-permute-start(bf16[2,256,128]{2,1,0:T(8,128)(2,1)S(1)} %get-tuple-element.66), channel_id=1, source_target_pairs={{0,1},{1,0},{2,3},{3,2},{4,5},{5,4},{6,7},{7,6},{8,9},{9,8},{10,11... | collective-permute-start | bytes 393224 | tf_op jit(solution)/shard_map/ppermute | solution.py:352
  16.6 4.0 %collective-permute-start.12 = (bf16[2,256,128]{2,1,0:T(8,128)(2,1)S(1)}, bf16[2,256,128]{2,1,0:T(8,128)(2,1)S(1)}, u32[]{:S(2)}, u32[]{:S(2)}) collective-permute-start(bf16[2,256,128]{2,1,0:T(8,128)(2,1)S(1)} %get-tuple-element.67), channel_id=1, source_target_pairs={{0,1},{1,0},{2,3},{3,2},{4,5},{5,4},{6,7},{7,6},{8,9},{9,8},{10,11... | collective-permute-start | bytes 393224 | tf_op jit(solution)/shard_map/ppermute | solution.py:352
  17.8 6.6 %collective-permute-start.10 = (bf16[512,128]{1,0:T(8,128)(2,1)S(1)}, bf16[512,128]{1,0:T(8,128)(2,1)S(1)}, u32[]{:S(2)}, u32[]{:S(2)}) collective-permute-start(bf16[512,128]{1,0:T(8,128)(2,1)S(1)} %merge_far.1), channel_id=1, source_target_pairs={{6,0},{4,2},{10,4},{8,6},{14,8},{12,10},{18,12},{16,14},{22,16},{2... | collective-permute-start | bytes 393224 | tf_op jit(solution)/shard_map/ppermute | solution.py:344
  20.5 5.5 %collective-permute-start.13 = (bf16[256,128]{1,0:T(8,128)(2,1)S(1)}, bf16[256,128]{1,0:T(8,128)(2,1)S(1)}, u32[]{:S(2)}, u32[]{:S(2)}) collective-permute-start(bf16[256,128]{1,0:T(8,128)(2,1)S(1)} %get-tuple-element.68), channel_id=1, source_target_pairs={{4,0},{5,1},{6,2},{7,3},{8,4},{9,5},{10,6},{11,7},{12,8},{13,9},{1... | collective-permute-start | bytes 196616 | tf_op jit(solution)/shard_map/ppermute | solution.py:339
  21.7 4.4 %collective-permute-start.14 = (bf16[256,128]{1,0:T(8,128)(2,1)S(1)}, bf16[256,128]{1,0:T(8,128)(2,1)S(1)}, u32[]{:S(2)}, u32[]{:S(2)}) collective-permute-start(bf16[256,128]{1,0:T(8,128)(2,1)S(1)} %get-tuple-element.69), channel_id=1, source_target_pairs={{2,0},{3,1},{8,2},{9,3},{6,4},{7,5},{12,6},{13,7},{10,8},{11,9},{1... | collective-permute-start | bytes 196616 | tf_op jit(solution)/shard_map/ppermute | solution.py:339
  24.4 1.8 %collective-permute-start.11 = (bf16[256,128]{1,0:T(8,128)(2,1)S(1)}, bf16[256,128]{1,0:T(8,128)(2,1)S(1)}, u32[]{:S(2)}, u32[]{:S(2)}) collective-permute-start(bf16[256,128]{1,0:T(8,128)(2,1)S(1)} %pass_on.1), channel_id=1, source_target_pairs={{0,1},{1,0},{2,3},{3,2},{4,5},{5,4},{6,7},{7,6},{8,9},{9,8},{10,11... | collective-permute-start | bytes 196616 | tf_op jit(solution)/shard_map/ppermute | solution.py:352

commit v8 on v7

--- a/solution.py
+++ b/solution.py
@@ -207,12 +207,12 @@
         for row, value in enumerate((top, inverse, delta)):
             final_ref[row : row + 1, cols] = value
         sib_probs, last_probs = probs_grad[rows_of(0), :], probs_grad[rows_of(1), :]
-        keep_powers[:, cols] = jnp.where(even, powers[0], powers[1])
-        keep_probs[:, cols] = jnp.where(even, sib_probs, last_probs)
+        keep_powers[:, cols] = jnp.where(even, powers[1], powers[0])
+        keep_probs[:, cols] = jnp.where(even, last_probs, sib_probs)
         factor = jnp.exp2(start[0] - top) * inverse
         for s, slot in enumerate(slots.swapped):
             if slot == "swap":
-                piece = jnp.where(even, powers[1], powers[0]), inverse, jnp.where(even, last_probs, sib_probs)
+                piece = jnp.where(even, powers[0], powers[1]), inverse, jnp.where(even, sib_probs, last_probs)
             else:
                 _, rows = slots.place(slot)
                 piece = powers_ref[rows, cols], factor, probs_ref[rows, cols]
@@ -254,8 +254,8 @@
     sib_ref, far_ref, sib_own_ref, attended_out, query_grad_out = refs[2 + 2 * half : 7 + 2 * half]
     swap_ref, keep_ref, attended_ref, query_grad_ref, sems = refs[7 + 2 * half :]
     _, _, core = position()
-    put_either(core, far_ref, sib_ref, swap_ref)
-    put_either(core, sib_ref, sib_own_ref, keep_ref)
+    put_either(core, sib_ref, sib_own_ref, swap_ref)
+    put_either(core, far_ref, sib_ref, keep_ref)
     swapped.insert(half - 2, swap_ref)
     mine.append(keep_ref)
 
@@ -278,8 +278,9 @@
 
 def merge_far_kernel(mine_ref, lin_ref, from_sib_ref, sent_ref):
     _, _, core = position()
-    far = from_sib_ref[0].astype(jnp.float32) + jnp.where(core == 0, lin_ref[...], 0.0)
-    other = from_sib_ref[1].astype(jnp.float32) + mine_ref[mine_ref.shape[0] - 1]
+    keep = mine_ref[mine_ref.shape[0] - 1]
+    far = jnp.where(core == 1, from_sib_ref[0].astype(jnp.float32) + lin_ref[...], keep)
+    other = from_sib_ref[1].astype(jnp.float32) + keep
     sent_ref[: 2 * BLOCK, :] = far.astype(jnp.bfloat16)
     sent_ref[2 * BLOCK :, :] = other.astype(jnp.bfloat16)
 
@@ -289,15 +290,16 @@
         ref[...] = (mine_ref[k + 1] + from_sib_ref[k].astype(jnp.float32)).astype(jnp.bfloat16)
 
 
-def pass_kernel(mine_ref, far_ref, out_ref):
+def pass_kernel(far_ref, out_ref):
     _, _, core = position()
-    near = mine_ref[mine_ref.shape[0] - 1].astype(jnp.bfloat16)
-    out_ref[...] = jnp.where(core == 0, far_ref[2 * BLOCK :, :], near)
-
-
-def total_kernel(mine_ref, far_ref, passed_ref, *refs):
+    out_ref[...] = jnp.where(core == 1, far_ref[2 * BLOCK :, :], far_ref[: 2 * BLOCK, :])
+
+
+def total_kernel(mine_ref, from_sib_ref, far_ref, passed_ref, *refs):
     back, (key_ref, value_ref) = refs[:-2], refs[-2:]
-    total = mine_ref[0] + far_ref[: 2 * BLOCK, :].astype(jnp.float32) + passed_ref[...].astype(jnp.float32)
+    _, _, core = position()
+    total = mine_ref[0] + jnp.where(core == 0, from_sib_ref[0], far_ref[: 2 * BLOCK, :]).astype(jnp.float32)
+    total = total + passed_ref[...].astype(jnp.float32)
     for ref in back:
         total = total + ref[...].astype(jnp.float32)
     key_ref[...] = total[:BLOCK].astype(jnp.bfloat16)
@@ -339,8 +341,8 @@
         return lax.ppermute(block, AXES, [pair[::-1] for pair in route] if back else route)
 
     def back_mixed(block):
-        route = [(target(i, half - 1), i) for i in range(0, devices, 2)]
-        route += [((i + window) % devices, i) for i in range(1, devices, 2)]
+        route = [(target(i, half - 1), i) for i in range(1, devices, 2)]
+        route += [((i + window) % devices, i) for i in range(0, devices, 2)]
         return lax.ppermute(block, AXES, route)
 
     def ahead_odd(block):
@@ -385,7 +387,7 @@
         name="own_scores",
     )(in_hbm(doc_ids), in_hbm(queries), in_hbm(out_grad), own)
 
-    lins[0], own_stage[2] = lax.optimization_barrier((lins[0], own_stage[2]))
+    lins[0], lins[1], own_stage[2] = lax.optimization_barrier((lins[0], lins[1], own_stage[2]))
     sibs = [swapped(block) for block in lins[: half - 2]]
     held = {("lin", k): block for k, block in zip(slots.arrival[:-1], lins)}
 
@@ -485,21 +487,21 @@
         pl.pallas_call(
             pass_kernel,
             out_shape=block,
-            in_specs=[VMEM] * 2,
+            in_specs=[VMEM],
             out_specs=VMEM,
             compiler_params=small,
             name="pass_on",
-        )(mine, back_far)
+        )(back_far)
     )
     back = [ahead(sent[m - 1], m, back=True) for m in range(half - 2, 0, -1)]
     key_grad, value_grad = pl.pallas_call(
         total_kernel,
         out_shape=[shape((BLOCK, HEAD_DIM), bf16)] * 2,
-        in_specs=[VMEM] * (1 + half),
+        in_specs=[VMEM] * (2 + half),
         out_specs=[VMEM] * 2,
         compiler_params=small,
         name="total_grads",
-    )(mine, back_far, passed, *back)
+    )(mine, far_from_sib, back_far, passed, *back)
     return attended, query_grad, key_grad, value_grad
 
 

time: 27.1 us -> 26.8 us (0.989)
  starting transfers between devices: 14.5 us -> 13.8 us
  waiting for transfers between devices: 3.37 us -> 3.73 us
    ppermute x5, starting transfers between devices: 9.91 us -> 9.45 us  [ahead(): lax.ppermute(block, AXES, [pair[::-1] for pair in route] if back else route)]
    ppermute x1, waiting for transfers between devices: 0.96 us -> 1.34 us  [back_mixed(): return lax.ppermute(block, AXES, route)]
  transfers between devices with their start and end apart: 15 -> 15, of which waited for: 4 -> 5; matrix products, arithmetic and copies ran while one was open for 0% -> 0% of each run, Pallas kernels for 20% -> 20%
where the time goes in v8:
time: 26.8 us; the launch traced here: 26.6 us
  starting transfers between devices  13.8 us (51%)
  Pallas kernels  8.27 us (31%)
  waiting for transfers between devices  3.73 us (14%)
  between operations  0.74 us (3%)
    ppermute x5, starting transfers between devices, ahead(): lax.ppermute(block, AXES, [pair[::-1] for pair in route] if back else route)  9.45 us
    ppermute x1, starting transfers between devices, back_mixed(): return lax.ppermute(block, AXES, route)  2.7 us
    ppermute x5, waiting for transfers between devices, ahead(): lax.ppermute(block, AXES, [pair[::-1] for pair in route] if back else route)  2.11 us
    ppermute x8, starting transfers between devices, swapped(): return lax.ppermute(block, AXES, [(i, i ^ 1) for i in range(devices)])  1.67 us
    pallas_call x1, Pallas kernels, local(): pl.pallas_call(functools.partial(query_side_kernel, slots), out_shape=[sh...  1.57 us
    pallas_call x1, Pallas kernels, local(): pl.pallas_call(functools.partial(own_kernel, slots), out_shape=[pltpu.VME...  1.54 us
    pallas_call x1, Pallas kernels, local(): pl.pallas_call(functools.partial(late_kernel, slots), out_shape=stage(1)...  1.46 us
    pallas_call x2, Pallas kernels, next_stage(): pl.pallas_call(functools.partial(stage_kernel, first, len(group)), out_sh...  1.38 us
  transfers between devices with their start and end apart: 15, of which 5 were waited for; matrix products, arithmetic and copies ran while one was open for 0% of the time, Pallas kernels for 20%

profile of v8, /device:TPU:0, one launch (start us, length us, event | category | flops | bytes accessed | tf_op | source)
XLA Modules:
  0.0 26.6 jit_solution(9142488548914830481)
XLA Ops:
  0.6 0.8 %pair_up.1.own_ref.refs_7_ = bf16[256,128]{1,0:T(8,128)(2,1)S(1)} custom-call(bf16[128,128]{1,0:T(8,128)(2,1)} %key_ref.1, bf16[128,128]{1,0:T(8,128)(2,1)} %value_ref.1), custom_call_target="tpu_custom_call" | custom-call | tf_op jit(solution)/shard_map/pair_up/pallas_call | solution.py:356
  1.4 3.0 %collective-permute-start.3 = (bf16[256,128]{1,0:T(8,128)(2,1)S(1)}, bf16[256,128]{1,0:T(8,128)(2,1)S(1)}, u32[]{:S(2)}, u32[]{:S(2)}) collective-permute-start(bf16[256,128]{1,0:T(8,128)(2,1)S(1)} %pair_up.1.own_ref.refs_7_), channel_id=1, source_target_pairs={{0,4},{1,5},{2,6},{3,7},{4,8},{5,9},{6,10},{7,11},{8,12},{9,13},{1... | collective-permute-start | bytes 196616 | tf_op jit(solution)/shard_map/ppermute | solution.py:341
  4.5 1.5 %collective-permute-start.2 = (bf16[256,128]{1,0:T(8,128)(2,1)S(1)}, bf16[256,128]{1,0:T(8,128)(2,1)S(1)}, u32[]{:S(2)}, u32[]{:S(2)}) collective-permute-start(bf16[256,128]{1,0:T(8,128)(2,1)S(1)} %pair_up.1.own_ref.refs_7_), channel_id=1, source_target_pairs={{0,2},{1,3},{2,8},{3,9},{4,6},{5,7},{6,12},{7,13},{8,10},{9,11},{1... | collective-permute-start | bytes 196616 | tf_op jit(solution)/shard_map/ppermute | solution.py:341
  5.9 2.5 %collective-permute-start.1 = (bf16[256,128]{1,0:T(8,128)(2,1)S(1)}, bf16[256,128]{1,0:T(8,128)(2,1)S(1)}, u32[]{:S(2)}, u32[]{:S(2)}) collective-permute-start(bf16[256,128]{1,0:T(8,128)(2,1)S(1)} %pair_up.1.own_ref.refs_7_), channel_id=1, source_target_pairs={{0,6},{1,7},{2,4},{3,5},{4,10},{5,11},{6,8},{7,9},{8,14},{9,15},{1... | collective-permute-start | bytes 196616 | tf_op jit(solution)/shard_map/ppermute | solution.py:341
  8.4 1.5 %own_scores.1 = (bf16[1024,128]{1,0:T(8,128)(2,1)S(1)}, bf16[1024,128]{1,0:T(8,128)(2,1)S(1)}, f32[8,1024]{1,0:T(8,128)S(1)}, f32[128,1024]{1,0:T(8,128)S(1)}, f...) custom-call(s32[32]{0:T(128)} %doc_hbm.1, bf16[128,1024]{1,0:T(8,128)(2,1)} %query_ref.1, bf16[128,1024]{1,0:T(8,128)(2,1)} %grad_ref.1, ...), custom_call_target="tpu_custom_call" | custom-call | flops 67108864 | bytes 524288 | tf_op jit(solution)/shard_map/own_scores/pallas_call | solution.py:375
  10.0 1.5 %collective-permute-done.2.refs_4_.refs_8_ = bf16[256,128]{1,0:T(8,128)(2,1)S(1)} collective-permute-done((bf16[256,128]{1,0:T(8,128)(2,1)S(1)}, bf16[256,128]{1,0:T(8,128)(2,1)S(1)}, u32[]{:S(2)}, u32[]{:S(2)}) %collective-permute-start.2) | collective-permute-done | bytes 65568 | tf_op jit(solution)/shard_map/ppermute | solution.py:341
  11.5 0.5 %collective-permute-start.5 = (bf16[256,128]{1,0:T(8,128)(2,1)S(1)}, bf16[256,128]{1,0:T(8,128)(2,1)S(1)}, u32[]{:S(2)}, u32[]{:S(2)}) collective-permute-start(bf16[256,128]{1,0:T(8,128)(2,1)S(1)} %collective-permute-done.3.refs_5_.refs_9_), channel_id=1, source_target_pairs={{0,1},{1,0},{2,3},{3,2},{4,5},{5,4},{6,7},{7,6},{8,9},{9,8},{10,11... | collective-permute-start | bytes 196616 | tf_op jit(solution)/shard_map/ppermute | solution.py:354
  12.0 0.6 %stage_scores.2 = (f32[256,1024]{1,0:T(8,128)S(1)}, f32[256,1024]{1,0:T(8,128)S(1)}, f32[8,1024]{1,0:T(8,128)S(1)}) custom-call(f32[8,1024]{1,0:T(8,128)S(1)} %get-tuple-element.39.refs_0_, bf16[1024,128]{1,0:T(8,128)(2,1)S(1)} %get-tuple-element.40.refs_1_.refs_0_, bf16[1024,128]{1,0:T(8,128)(2,1)S(1)} %get-tuple-element.41.refs_2_.refs_1_, ...), custom_call_target="tpu_custom_call" | custom-call | flops 134217728 | bytes 1048576 | tf_op jit(solution)/shard_map/stage_scores/pallas_call | solution.py:398
  12.6 0.3 %collective-permute-done.1.refs_6_ = bf16[256,128]{1,0:T(8,128)(2,1)S(1)} collective-permute-done((bf16[256,128]{1,0:T(8,128)(2,1)S(1)}, bf16[256,128]{1,0:T(8,128)(2,1)S(1)}, u32[]{:S(2)}, u32[]{:S(2)}) %collective-permute-start.1) | collective-permute-done | bytes 65568 | tf_op jit(solution)/shard_map/ppermute | solution.py:341
  12.9 0.3 %collective-permute-start.7 = (bf16[256,128]{1,0:T(8,128)(2,1)S(1)}, bf16[256,128]{1,0:T(8,128)(2,1)S(1)}, u32[]{:S(2)}, u32[]{:S(2)}) collective-permute-start(bf16[256,128]{1,0:T(8,128)(2,1)S(1)} %collective-permute-done), channel_id=1, source_target_pairs={{0,1},{1,0},{2,3},{3,2},{4,5},{5,4},{6,7},{7,6},{8,9},{9,8},{10,11... | collective-permute-start | bytes 196616 | tf_op jit(solution)/shard_map/ppermute | solution.py:354
  13.2 0.2 collective-permute-start.6
  13.4 0.8 %stage_scores.3 = (f32[384,1024]{1,0:T(8,128)S(1)}, f32[384,1024]{1,0:T(8,128)S(1)}, f32[8,1024]{1,0:T(8,128)S(1)}) custom-call(f32[8,1024]{1,0:T(8,128)S(1)} %get-tuple-element.39.refs_0_, bf16[1024,128]{1,0:T(8,128)(2,1)S(1)} %get-tuple-element.40.refs_1_.refs_0_, bf16[1024,128]{1,0:T(8,128)(2,1)S(1)} %get-tuple-element.41.refs_2_.refs_1_, ...), custom_call_target="tpu_custom_call" | custom-call | flops 201326592 | bytes 1572864 | tf_op jit(solution)/shard_map/stage_scores/pallas_call | solution.py:398
  14.3 0.2 collective-permute-done.6.refs_6_.refs_10_
  14.5 1.5 %late_scores.1 = (f32[128,1024]{1,0:T(8,128)S(1)}, f32[128,1024]{1,0:T(8,128)S(1)}, f32[8,1024]{1,0:T(8,128)S(1)}, bf16[512,1024]{1,0:T(8,128)(2,1)S(1)}, bf16[5...) custom-call(f32[8,1024]{1,0:T(8,128)S(1)} %get-tuple-element.39.refs, ...), custom_call_target="tpu_custom_call" | custom-call | flops 536870912 | bytes 4194304 | tf_op jit(solution)/shard_map/late_scores/pallas_call | solution.py:422
  15.9 0.3 %collective-permute-start.9 = (bf16[2,256,128]{2,1,0:T(8,128)(2,1)S(1)}, bf16[2,256,128]{2,1,0:T(8,128)(2,1)S(1)}, u32[]{:S(2)}, u32[]{:S(2)}) collective-permute-start(bf16[2,256,128]{2,1,0:T(8,128)(2,1)S(1)} %get-tuple-element.67), channel_id=1, source_target_pairs={{0,1},{1,0},{2,3},{3,2},{4,5},{5,4},{6,7},{7,6},{8,9},{9,8},{10,11... | collective-permute-start | bytes 393224 | tf_op jit(solution)/shard_map/ppermute | solution.py:354
  16.2 0.3 %collective-permute-start.12 = (bf16[2,256,128]{2,1,0:T(8,128)(2,1)S(1)}, bf16[2,256,128]{2,1,0:T(8,128)(2,1)S(1)}, u32[]{:S(2)}, u32[]{:S(2)}) collective-permute-start(bf16[2,256,128]{2,1,0:T(8,128)(2,1)S(1)} %get-tuple-element.69), channel_id=1, source_target_pairs={{0,1},{1,0},{2,3},{3,2},{4,5},{5,4},{6,7},{7,6},{8,9},{9,8},{10,11... | collective-permute-start | bytes 393224 | tf_op jit(solution)/shard_map/ppermute | solution.py:354
  16.5 0.8 %other_grads.1 = (bf16[512,1024]{1,0:T(8,128)(2,1)S(1)}, bf16[512,1024]{1,0:T(8,128)(2,1)S(1)}, f32[4,256,128]{2,1,0:T(8,128)S(1)}) custom-call(bf16[1024,128]{1,0:T(8,128)(2,1)S(1)} %get-tuple-element.40.refs_1_.refs_0_, bf16[1024,128]{1,0:T(8,128)(2,1)S(1)} %get-tuple-element.41.refs_2_.refs_1_, f32[8,1024]{1,0:T(8,128)S(1)} %get-tuple-element.55.refs_2_, ...), custom_call_target="tpu_custom_call" | custom-call | flops 268435456 | bytes 2097152 | tf_op jit(solution)/shard_map/other_grads/pallas_call | solution.py:437
  17.4 2.7 %collective-permute-start.10 = (bf16[512,128]{1,0:T(8,128)(2,1)S(1)}, bf16[512,128]{1,0:T(8,128)(2,1)S(1)}, u32[]{:S(2)}, u32[]{:S(2)}) collective-permute-start(bf16[512,128]{1,0:T(8,128)(2,1)S(1)} %merge_far.1), channel_id=1, source_target_pairs={{7,1},{5,3},{11,5},{9,7},{15,9},{13,11},{19,13},{17,15},{23,17},{2... | collective-permute-start | bytes 393224 | tf_op jit(solution)/shard_map/ppermute | solution.py:346
  20.1 1.4 %collective-permute-start.13 = (bf16[256,128]{1,0:T(8,128)(2,1)S(1)}, bf16[256,128]{1,0:T(8,128)(2,1)S(1)}, u32[]{:S(2)}, u32[]{:S(2)}) collective-permute-start(bf16[256,128]{1,0:T(8,128)(2,1)S(1)} %get-tuple-element.70), channel_id=1, source_target_pairs={{4,0},{5,1},{6,2},{7,3},{8,4},{9,5},{10,6},{11,7},{12,8},{13,9},{1... | collective-permute-start | bytes 196616 | tf_op jit(solution)/shard_map/ppermute | solution.py:341
  21.6 1.0 %collective-permute-start.14 = (bf16[256,128]{1,0:T(8,128)(2,1)S(1)}, bf16[256,128]{1,0:T(8,128)(2,1)S(1)}, u32[]{:S(2)}, u32[]{:S(2)}) collective-permute-start(bf16[256,128]{1,0:T(8,128)(2,1)S(1)} %get-tuple-element.71), channel_id=1, source_target_pairs={{2,0},{3,1},{8,2},{9,3},{6,4},{7,5},{12,6},{13,7},{10,8},{11,9},{1... | collective-permute-start | bytes 196616 | tf_op jit(solution)/shard_map/ppermute | solution.py:341
  22.6 1.3 %collective-permute-done.10.far_ref = bf16[512,128]{1,0:T(8,128)(2,1)S(1)} collective-permute-done((bf16[512,128]{1,0:T(8,128)(2,1)S(1)}, bf16[512,128]{1,0:T(8,128)(2,1)S(1)}, u32[]{:S(2)}, u32[]{:S(2)}) %collective-permute-start.10) | collective-permute-done | bytes 131104 | tf_op jit(solution)/shard_map/ppermute | solution.py:346
  24.0 1.6 %query_side.1 = (bf16[128,1024]{1,0:T(8,128)(2,1)}, bf16[128,1024]{1,0:T(8,128)(2,1)}) custom-call(bf16[512,1024]{1,0:T(8,128)(2,1)S(1)} %get-tuple-element.53.refs_0_, bf16[512,1024]{1,0:T(8,128)(2,1)S(1)} %get-tuple-element.54.refs_1_, bf16[512,1024]{1,0:T(8,128)(2,1)S(1)} %get-tuple-element.62.refs_2_, bf16[512,1024]{1,0:T(8,128)(2,1)S(1)} %get-tuple-element.63.refs_3_, ...), custom_call_target="tpu_custom_call" | custom-call | flops 536870912 | bytes 4194304 | tf_op jit(solution)/shard_map/query_side/pallas_call | solution.py:447
  25.6 0.3 %collective-permute-done.14.refs_1_ = bf16[256,128]{1,0:T(8,128)(2,1)S(1)} collective-permute-done((bf16[256,128]{1,0:T(8,128)(2,1)S(1)}, bf16[256,128]{1,0:T(8,128)(2,1)S(1)}, u32[]{:S(2)}, u32[]{:S(2)}) %collective-permute-start.14) | collective-permute-done | bytes 65568 | tf_op jit(solution)/shard_map/ppermute | solution.py:341
  25.9 0.7 %total_grads.1 = (bf16[128,128]{1,0:T(8,128)(2,1)}, bf16[128,128]{1,0:T(8,128)(2,1)}) custom-call(f32[4,256,128]{2,1,0:T(8,128)S(1)} %get-tuple-element.66.mine_ref, bf16[2,256,128]{2,1,0:T(8,128)(2,1)S(1)} %collective-permute-done.9.from_sib_ref, bf16[512,128]{1,0:T(8,128)(2,1)S(1)} %collective-permute-done.10.far_ref, ...), custom_call_target="tpu_custom_call" | custom-call | tf_op jit(solution)/shard_map/total_grads/pallas_call | solution.py:497
  (17 shorter events, 0.2 us)
Async XLA Ops:
  1.4 8.6 %collective-permute-start.3 = (bf16[256,128]{1,0:T(8,128)(2,1)S(1)}, bf16[256,128]{1,0:T(8,128)(2,1)S(1)}, u32[]{:S(2)}, u32[]{:S(2)}) collective-permute-start(bf16[256,128]{1,0:T(8,128)(2,1)S(1)} %pair_up.1.own_ref.refs_7_), channel_id=1, source_target_pairs={{0,4},{1,5},{2,6},{3,7},{4,8},{5,9},{6,10},{7,11},{8,12},{9,13},{1... | collective-permute-start | bytes 196616 | tf_op jit(solution)/shard_map/ppermute | solution.py:341
  4.5 7.1 %collective-permute-start.2 = (bf16[256,128]{1,0:T(8,128)(2,1)S(1)}, bf16[256,128]{1,0:T(8,128)(2,1)S(1)}, u32[]{:S(2)}, u32[]{:S(2)}) collective-permute-start(bf16[256,128]{1,0:T(8,128)(2,1)S(1)} %pair_up.1.own_ref.refs_7_), channel_id=1, source_target_pairs={{0,2},{1,3},{2,8},{3,9},{4,6},{5,7},{6,12},{7,13},{8,10},{9,11},{1... | collective-permute-start | bytes 196616 | tf_op jit(solution)/shard_map/ppermute | solution.py:341
  5.9 7.0 %collective-permute-start.1 = (bf16[256,128]{1,0:T(8,128)(2,1)S(1)}, bf16[256,128]{1,0:T(8,128)(2,1)S(1)}, u32[]{:S(2)}, u32[]{:S(2)}) collective-permute-start(bf16[256,128]{1,0:T(8,128)(2,1)S(1)} %pair_up.1.own_ref.refs_7_), channel_id=1, source_target_pairs={{0,6},{1,7},{2,4},{3,5},{4,10},{5,11},{6,8},{7,9},{8,14},{9,15},{1... | collective-permute-start | bytes 196616 | tf_op jit(solution)/shard_map/ppermute | solution.py:341
  8.4 4.5 %collective-permute-start = (bf16[256,128]{1,0:T(8,128)(2,1)S(1)}, bf16[256,128]{1,0:T(8,128)(2,1)S(1)}, u32[]{:S(2)}, u32[]{:S(2)}) collective-permute-start(bf16[256,128]{1,0:T(8,128)(2,1)S(1)} %pair_up.1.own_ref.refs_7_), channel_id=1, source_target_pairs={{1,9},{3,11},{5,13},{7,15},{9,17},{11,19},{13,21},{15,23},{17,25},... | collective-permute-start | bytes 196616 | tf_op jit(solution)/shard_map/ppermute | solution.py:351
  11.5 1.9 %collective-permute-start.4 = (bf16[256,128]{1,0:T(8,128)(2,1)S(1)}, bf16[256,128]{1,0:T(8,128)(2,1)S(1)}, u32[]{:S(2)}, u32[]{:S(2)}) collective-permute-start(bf16[256,128]{1,0:T(8,128)(2,1)S(1)} %collective-permute-done.2.refs_4_.refs_8_), channel_id=1, source_target_pairs={{0,1},{1,0},{2,3},{3,2},{4,5},{5,4},{6,7},{7,6},{8,9},{9,8},{10,11... | collective-permute-start | bytes 196616 | tf_op jit(solution)/shard_map/ppermute | solution.py:354
  11.5 1.9 %collective-permute-start.5 = (bf16[256,128]{1,0:T(8,128)(2,1)S(1)}, bf16[256,128]{1,0:T(8,128)(2,1)S(1)}, u32[]{:S(2)}, u32[]{:S(2)}) collective-permute-start(bf16[256,128]{1,0:T(8,128)(2,1)S(1)} %collective-permute-done.3.refs_5_.refs_9_), channel_id=1, source_target_pairs={{0,1},{1,0},{2,3},{3,2},{4,5},{5,4},{6,7},{7,6},{8,9},{9,8},{10,11... | collective-permute-start | bytes 196616 | tf_op jit(solution)/shard_map/ppermute | solution.py:354
  12.0 2.2 %collective-permute-start.8 = (bf16[256,128]{1,0:T(8,128)(2,1)S(1)}, bf16[256,128]{1,0:T(8,128)(2,1)S(1)}, u32[]{:S(2)}, u32[]{:S(2)}) collective-permute-start(bf16[256,128]{1,0:T(8,128)(2,1)S(1)} %pair_up.1.own_ref.refs_7_), channel_id=1, source_target_pairs={{0,1},{1,0},{2,3},{3,2},{4,5},{5,4},{6,7},{7,6},{8,9},{9,8},{10,11... | collective-permute-start | bytes 196616 | tf_op jit(solution)/shard_map/ppermute | solution.py:354
  12.9 1.3 %collective-permute-start.7 = (bf16[256,128]{1,0:T(8,128)(2,1)S(1)}, bf16[256,128]{1,0:T(8,128)(2,1)S(1)}, u32[]{:S(2)}, u32[]{:S(2)}) collective-permute-start(bf16[256,128]{1,0:T(8,128)(2,1)S(1)} %collective-permute-done), channel_id=1, source_target_pairs={{0,1},{1,0},{2,3},{3,2},{4,5},{5,4},{6,7},{7,6},{8,9},{9,8},{10,11... | collective-permute-start | bytes 196616 | tf_op jit(solution)/shard_map/ppermute | solution.py:354
  13.2 1.3 %collective-permute-start.6 = (bf16[256,128]{1,0:T(8,128)(2,1)S(1)}, bf16[256,128]{1,0:T(8,128)(2,1)S(1)}, u32[]{:S(2)}, u32[]{:S(2)}) collective-permute-start(bf16[256,128]{1,0:T(8,128)(2,1)S(1)} %collective-permute-done.1.refs_6_), channel_id=1, source_target_pairs={{0,1},{1,0},{2,3},{3,2},{4,5},{5,4},{6,7},{7,6},{8,9},{9,8},{10,11... | collective-permute-start | bytes 196616 | tf_op jit(solution)/shard_map/ppermute | solution.py:354
  15.9 1.4 %collective-permute-start.9 = (bf16[2,256,128]{2,1,0:T(8,128)(2,1)S(1)}, bf16[2,256,128]{2,1,0:T(8,128)(2,1)S(1)}, u32[]{:S(2)}, u32[]{:S(2)}) collective-permute-start(bf16[2,256,128]{2,1,0:T(8,128)(2,1)S(1)} %get-tuple-element.67), channel_id=1, source_target_pairs={{0,1},{1,0},{2,3},{3,2},{4,5},{5,4},{6,7},{7,6},{8,9},{9,8},{10,11... | collective-permute-start | bytes 393224 | tf_op jit(solution)/shard_map/ppermute | solution.py:354
  16.2 3.9 %collective-permute-start.12 = (bf16[2,256,128]{2,1,0:T(8,128)(2,1)S(1)}, bf16[2,256,128]{2,1,0:T(8,128)(2,1)S(1)}, u32[]{:S(2)}, u32[]{:S(2)}) collective-permute-start(bf16[2,256,128]{2,1,0:T(8,128)(2,1)S(1)} %get-tuple-element.69), channel_id=1, source_target_pairs={{0,1},{1,0},{2,3},{3,2},{4,5},{5,4},{6,7},{7,6},{8,9},{9,8},{10,11... | collective-permute-start | bytes 393224 | tf_op jit(solution)/shard_map/ppermute | solution.py:354
  17.4 6.5 %collective-permute-start.10 = (bf16[512,128]{1,0:T(8,128)(2,1)S(1)}, bf16[512,128]{1,0:T(8,128)(2,1)S(1)}, u32[]{:S(2)}, u32[]{:S(2)}) collective-permute-start(bf16[512,128]{1,0:T(8,128)(2,1)S(1)} %merge_far.1), channel_id=1, source_target_pairs={{7,1},{5,3},{11,5},{9,7},{15,9},{13,11},{19,13},{17,15},{23,17},{2... | collective-permute-start | bytes 393224 | tf_op jit(solution)/shard_map/ppermute | solution.py:346
  20.1 5.5 %collective-permute-start.13 = (bf16[256,128]{1,0:T(8,128)(2,1)S(1)}, bf16[256,128]{1,0:T(8,128)(2,1)S(1)}, u32[]{:S(2)}, u32[]{:S(2)}) collective-permute-start(bf16[256,128]{1,0:T(8,128)(2,1)S(1)} %get-tuple-element.70), channel_id=1, source_target_pairs={{4,0},{5,1},{6,2},{7,3},{8,4},{9,5},{10,6},{11,7},{12,8},{13,9},{1... | collective-permute-start | bytes 196616 | tf_op jit(solution)/shard_map/ppermute | solution.py:341
  21.6 4.4 %collective-permute-start.14 = (bf16[256,128]{1,0:T(8,128)(2,1)S(1)}, bf16[256,128]{1,0:T(8,128)(2,1)S(1)}, u32[]{:S(2)}, u32[]{:S(2)}) collective-permute-start(bf16[256,128]{1,0:T(8,128)(2,1)S(1)} %get-tuple-element.71), channel_id=1, source_target_pairs={{2,0},{3,1},{8,2},{9,3},{6,4},{7,5},{12,6},{13,7},{10,8},{11,9},{1... | collective-permute-start | bytes 196616 | tf_op jit(solution)/shard_map/ppermute | solution.py:341
  23.9 2.0 %collective-permute-start.11 = (bf16[256,128]{1,0:T(8,128)(2,1)S(1)}, bf16[256,128]{1,0:T(8,128)(2,1)S(1)}, u32[]{:S(2)}, u32[]{:S(2)}) collective-permute-start(bf16[256,128]{1,0:T(8,128)(2,1)S(1)} %pass_on.1), channel_id=1, source_target_pairs={{0,1},{1,0},{2,3},{3,2},{4,5},{5,4},{6,7},{7,6},{8,9},{9,8},{10,11... | collective-permute-start | bytes 196616 | tf_op jit(solution)/shard_map/ppermute | solution.py:354

commit v9 on v8

--- a/solution.py
+++ b/solution.py
@@ -345,9 +345,9 @@
         route += [((i + window) % devices, i) for i in range(0, devices, 2)]
         return lax.ppermute(block, AXES, route)
 
-    def ahead_odd(block):
-        route = [(i, i + window if i + window < devices else i ^ 1) for i in range(1, devices, 2)]
-        route += [(i, i - window if i >= window else i ^ 1) for i in range(0, devices, 2)]
+    def ahead_even(block):
+        route = [(i, i + window if i + window < devices else i ^ 1) for i in range(0, devices, 2)]
+        route += [(i, i - window if i >= window else i ^ 1) for i in range(1, devices, 2)]
         return lax.ppermute(block, AXES, route)
 
     def swapped(block):
@@ -362,8 +362,8 @@
         compiler_params=small,
         name="pair_up",
     )(in_hbm(key_rows), in_hbm(value_rows))
-    lins = [ahead(own, k) for k in slots.arrival] + [ahead_odd(own)]
     sib_own = swapped(own)
+    lins = [ahead(own, k) for k in slots.arrival] + [ahead_even(sib_own)]
 
     def stage(blocks):
         return [
@@ -410,8 +410,8 @@
     lins[half - 1], lins[half - 2], middle_stage[2] = lax.optimization_barrier(
         (lins[half - 1], lins[half - 2], middle_stage[2])
     )
-    sibs += [swapped(block) for block in lins[half - 2 :]]
-    held |= {"own": own, "last": sibs[-1]}
+    sibs.append(swapped(lins[half - 2]))
+    held |= {"own": own, "last": lins[-1]}
     for k, block, swap in zip(slots.arrival, lins, sibs):
         held["lin", k] = block
         held["sib", k] = swap
@@ -493,7 +493,7 @@
             name="pass_on",
         )(back_far)
     )
-    back = [ahead(sent[m - 1], m, back=True) for m in range(half - 2, 0, -1)]
+    back = [ahead(sent[m - 1], m, back=True) for m in range(1, half - 1)]
     key_grad, value_grad = pl.pallas_call(
         total_kernel,
         out_shape=[shape((BLOCK, HEAD_DIM), bf16)] * 2,

time: 26.8 us -> 26.8 us (level)
  starting transfers between devices: 13.8 us -> 14.8 us
  waiting for transfers between devices: 3.73 us -> 2.79 us
    ppermute x1, starting transfers between devices: 0.01 us -> 1.58 us  [ahead_even(): return lax.ppermute(block, AXES, route)]
    ppermute x5, waiting for transfers between devices: 2.11 us -> 0.8 us  [ahead(): lax.ppermute(block, AXES, [pair[::-1] for pair in route] if back else route)]
    ppermute x1, starting transfers between devices: 2.7 us -> 2.22 us  [back_mixed(): return lax.ppermute(block, AXES, route)]
    ppermute x8 -> x7, starting transfers between devices: 1.67 us -> 1.73 us  [swapped(): return lax.ppermute(block, AXES, [(i, i ^ 1) for i in range(devices)])]
  transfers between devices with their start and end apart: 15 -> 14, of which waited for: 5 -> 4; matrix products, arithmetic and copies ran while one was open for 0% -> 0% of each run, Pallas kernels for 20% -> 20%
where the time goes in v9:
time: 26.8 us; the launch traced here: 26.6 us
  starting transfers between devices  14.8 us (55%)
  Pallas kernels  8.27 us (31%)
  waiting for transfers between devices  2.79 us (10%)
  between operations  0.75 us (3%)
    ppermute x5, starting transfers between devices, ahead(): lax.ppermute(block, AXES, [pair[::-1] for pair in route] if back else route)  9.23 us
    ppermute x1, starting transfers between devices, back_mixed(): return lax.ppermute(block, AXES, route)  2.22 us
    ppermute x7, starting transfers between devices, swapped(): return lax.ppermute(block, AXES, [(i, i ^ 1) for i in range(devices)])  1.73 us
    ppermute x1, starting transfers between devices, ahead_even(): return lax.ppermute(block, AXES, route)  1.58 us
    pallas_call x1, Pallas kernels, local(): pl.pallas_call(functools.partial(query_side_kernel, slots), out_shape=[sh...  1.57 us
    pallas_call x1, Pallas kernels, local(): pl.pallas_call(functools.partial(own_kernel, slots), out_shape=[pltpu.VME...  1.54 us
    ppermute x1, waiting for transfers between devices, back_mixed(): return lax.ppermute(block, AXES, route)  1.49 us
    pallas_call x1, Pallas kernels, local(): pl.pallas_call(functools.partial(late_kernel, slots), out_shape=stage(1)...  1.46 us
  transfers between devices with their start and end apart: 14, of which 4 were waited for; matrix products, arithmetic and copies ran while one was open for 0% of the time, Pallas kernels for 20%

profile of v9, /device:TPU:0, one launch (start us, length us, event | category | flops | bytes accessed | tf_op | source)
XLA Modules:
  0.0 26.6 jit_solution(8577344553927382037)
XLA Ops:
  0.6 0.8 %pair_up.1.own_ref.refs_7_ = bf16[256,128]{1,0:T(8,128)(2,1)S(1)} custom-call(bf16[128,128]{1,0:T(8,128)(2,1)} %key_ref.1, bf16[128,128]{1,0:T(8,128)(2,1)} %value_ref.1), custom_call_target="tpu_custom_call" | custom-call | tf_op jit(solution)/shard_map/pair_up/pallas_call | solution.py:356
  1.4 0.5 %collective-permute-start = (bf16[256,128]{1,0:T(8,128)(2,1)S(1)}, bf16[256,128]{1,0:T(8,128)(2,1)S(1)}, u32[]{:S(2)}, u32[]{:S(2)}) collective-permute-start(bf16[256,128]{1,0:T(8,128)(2,1)S(1)} %pair_up.1.own_ref.refs_7_), channel_id=1, source_target_pairs={{0,1},{1,0},{2,3},{3,2},{4,5},{5,4},{6,7},{7,6},{8,9},{9,8},{10,11... | collective-permute-start | bytes 196616 | tf_op jit(solution)/shard_map/ppermute | solution.py:354
  1.9 2.6 %collective-permute-start.4 = (bf16[256,128]{1,0:T(8,128)(2,1)S(1)}, bf16[256,128]{1,0:T(8,128)(2,1)S(1)}, u32[]{:S(2)}, u32[]{:S(2)}) collective-permute-start(bf16[256,128]{1,0:T(8,128)(2,1)S(1)} %pair_up.1.own_ref.refs_7_), channel_id=1, source_target_pairs={{0,4},{1,5},{2,6},{3,7},{4,8},{5,9},{6,10},{7,11},{8,12},{9,13},{1... | collective-permute-start | bytes 196616 | tf_op jit(solution)/shard_map/ppermute | solution.py:341
  4.5 1.5 %collective-permute-start.3 = (bf16[256,128]{1,0:T(8,128)(2,1)S(1)}, bf16[256,128]{1,0:T(8,128)(2,1)S(1)}, u32[]{:S(2)}, u32[]{:S(2)}) collective-permute-start(bf16[256,128]{1,0:T(8,128)(2,1)S(1)} %pair_up.1.own_ref.refs_7_), channel_id=1, source_target_pairs={{0,2},{1,3},{2,8},{3,9},{4,6},{5,7},{6,12},{7,13},{8,10},{9,11},{1... | collective-permute-start | bytes 196616 | tf_op jit(solution)/shard_map/ppermute | solution.py:341
  6.0 2.5 %collective-permute-start.2 = (bf16[256,128]{1,0:T(8,128)(2,1)S(1)}, bf16[256,128]{1,0:T(8,128)(2,1)S(1)}, u32[]{:S(2)}, u32[]{:S(2)}) collective-permute-start(bf16[256,128]{1,0:T(8,128)(2,1)S(1)} %pair_up.1.own_ref.refs_7_), channel_id=1, source_target_pairs={{0,6},{1,7},{2,4},{3,5},{4,10},{5,11},{6,8},{7,9},{8,14},{9,15},{1... | collective-permute-start | bytes 196616 | tf_op jit(solution)/shard_map/ppermute | solution.py:341
  8.5 1.6 %collective-permute-start.1 = (bf16[256,128]{1,0:T(8,128)(2,1)S(1)}, bf16[256,128]{1,0:T(8,128)(2,1)S(1)}, u32[]{:S(2)}, u32[]{:S(2)}) collective-permute-start(bf16[256,128]{1,0:T(8,128)(2,1)S(1)} %collective-permute-done.refs_8_.refs_12_), channel_id=1, source_target_pairs={{0,8},{2,10},{4,12},{6,14},{8,16},{10,18},{12,20},{14,22},{16,24},... | collective-permute-start | bytes 196616 | tf_op jit(solution)/shard_map/ppermute | solution.py:351
  10.1 1.5 %own_scores.1 = (bf16[1024,128]{1,0:T(8,128)(2,1)S(1)}, bf16[1024,128]{1,0:T(8,128)(2,1)S(1)}, f32[8,1024]{1,0:T(8,128)S(1)}, f32[128,1024]{1,0:T(8,128)S(1)}, f...) custom-call(s32[32]{0:T(128)} %doc_hbm.1, bf16[128,1024]{1,0:T(8,128)(2,1)} %query_ref.1, bf16[128,1024]{1,0:T(8,128)(2,1)} %grad_ref.1, ...), custom_call_target="tpu_custom_call" | custom-call | flops 67108864 | bytes 524288 | tf_op jit(solution)/shard_map/own_scores/pallas_call | solution.py:375
  11.8 0.5 %collective-permute-start.6 = (bf16[256,128]{1,0:T(8,128)(2,1)S(1)}, bf16[256,128]{1,0:T(8,128)(2,1)S(1)}, u32[]{:S(2)}, u32[]{:S(2)}) collective-permute-start(bf16[256,128]{1,0:T(8,128)(2,1)S(1)} %collective-permute-done.4.refs_5_.refs_9_), channel_id=1, source_target_pairs={{0,1},{1,0},{2,3},{3,2},{4,5},{5,4},{6,7},{7,6},{8,9},{9,8},{10,11... | collective-permute-start | bytes 196616 | tf_op jit(solution)/shard_map/ppermute | solution.py:354
  12.2 0.6 %stage_scores.2 = (f32[256,1024]{1,0:T(8,128)S(1)}, f32[256,1024]{1,0:T(8,128)S(1)}, f32[8,1024]{1,0:T(8,128)S(1)}) custom-call(f32[8,1024]{1,0:T(8,128)S(1)} %get-tuple-element.39.refs_0_, bf16[1024,128]{1,0:T(8,128)(2,1)S(1)} %get-tuple-element.40.refs_1_.refs_0_, bf16[1024,128]{1,0:T(8,128)(2,1)S(1)} %get-tuple-element.41.refs_2_.refs_1_, ...), custom_call_target="tpu_custom_call" | custom-call | flops 134217728 | bytes 1048576 | tf_op jit(solution)/shard_map/stage_scores/pallas_call | solution.py:398
  12.8 0.7 %collective-permute-done.2.refs_6_ = bf16[256,128]{1,0:T(8,128)(2,1)S(1)} collective-permute-done((bf16[256,128]{1,0:T(8,128)(2,1)S(1)}, bf16[256,128]{1,0:T(8,128)(2,1)S(1)}, u32[]{:S(2)}, u32[]{:S(2)}) %collective-permute-start.2) | collective-permute-done | bytes 65568 | tf_op jit(solution)/shard_map/ppermute | solution.py:341
  13.5 0.8 %stage_scores.3 = (f32[384,1024]{1,0:T(8,128)S(1)}, f32[384,1024]{1,0:T(8,128)S(1)}, f32[8,1024]{1,0:T(8,128)S(1)}) custom-call(f32[8,1024]{1,0:T(8,128)S(1)} %get-tuple-element.39.refs_0_, bf16[1024,128]{1,0:T(8,128)(2,1)S(1)} %get-tuple-element.40.refs_1_.refs_0_, bf16[1024,128]{1,0:T(8,128)(2,1)S(1)} %get-tuple-element.41.refs_2_.refs_1_, ...), custom_call_target="tpu_custom_call" | custom-call | flops 201326592 | bytes 1572864 | tf_op jit(solution)/shard_map/stage_scores/pallas_call | solution.py:398
  14.3 0.4 %collective-permute-done.7.refs_6_.refs_10_ = bf16[256,128]{1,0:T(8,128)(2,1)S(1)} collective-permute-done((bf16[256,128]{1,0:T(8,128)(2,1)S(1)}, bf16[256,128]{1,0:T(8,128)(2,1)S(1)}, u32[]{:S(2)}, u32[]{:S(2)}) %collective-permute-start.7) | collective-permute-done | bytes 65568 | tf_op jit(solution)/shard_map/ppermute | solution.py:354
  14.8 1.5 %late_scores.1 = (f32[128,1024]{1,0:T(8,128)S(1)}, f32[128,1024]{1,0:T(8,128)S(1)}, f32[8,1024]{1,0:T(8,128)S(1)}, bf16[512,1024]{1,0:T(8,128)(2,1)S(1)}, bf16[5...) custom-call(f32[8,1024]{1,0:T(8,128)S(1)} %get-tuple-element.39.refs, ...), custom_call_target="tpu_custom_call" | custom-call | flops 536870912 | bytes 4194304 | tf_op jit(solution)/shard_map/late_scores/pallas_call | solution.py:422
  16.2 0.2 collective-permute-start.8
  16.5 0.4 %collective-permute-start.11 = (bf16[2,256,128]{2,1,0:T(8,128)(2,1)S(1)}, bf16[2,256,128]{2,1,0:T(8,128)(2,1)S(1)}, u32[]{:S(2)}, u32[]{:S(2)}) collective-permute-start(bf16[2,256,128]{2,1,0:T(8,128)(2,1)S(1)} %get-tuple-element.69), channel_id=1, source_target_pairs={{0,1},{1,0},{2,3},{3,2},{4,5},{5,4},{6,7},{7,6},{8,9},{9,8},{10,11... | collective-permute-start | bytes 393224 | tf_op jit(solution)/shard_map/ppermute | solution.py:354
  16.8 0.8 %other_grads.1 = (bf16[512,1024]{1,0:T(8,128)(2,1)S(1)}, bf16[512,1024]{1,0:T(8,128)(2,1)S(1)}, f32[4,256,128]{2,1,0:T(8,128)S(1)}) custom-call(bf16[1024,128]{1,0:T(8,128)(2,1)S(1)} %get-tuple-element.40.refs_1_.refs_0_, bf16[1024,128]{1,0:T(8,128)(2,1)S(1)} %get-tuple-element.41.refs_2_.refs_1_, f32[8,1024]{1,0:T(8,128)S(1)} %get-tuple-element.55.refs_2_, ...), custom_call_target="tpu_custom_call" | custom-call | flops 268435456 | bytes 2097152 | tf_op jit(solution)/shard_map/other_grads/pallas_call | solution.py:437
  17.7 2.2 %collective-permute-start.9 = (bf16[512,128]{1,0:T(8,128)(2,1)S(1)}, bf16[512,128]{1,0:T(8,128)(2,1)S(1)}, u32[]{:S(2)}, u32[]{:S(2)}) collective-permute-start(bf16[512,128]{1,0:T(8,128)(2,1)S(1)} %merge_far.1), channel_id=1, source_target_pairs={{7,1},{5,3},{11,5},{9,7},{15,9},{13,11},{19,13},{17,15},{23,17},{2... | collective-permute-start | bytes 393224 | tf_op jit(solution)/shard_map/ppermute | solution.py:346
  20.0 1.5 %collective-permute-start.12 = (bf16[256,128]{1,0:T(8,128)(2,1)S(1)}, bf16[256,128]{1,0:T(8,128)(2,1)S(1)}, u32[]{:S(2)}, u32[]{:S(2)}) collective-permute-start(bf16[256,128]{1,0:T(8,128)(2,1)S(1)} %get-tuple-element.70), channel_id=1, source_target_pairs={{2,0},{3,1},{8,2},{9,3},{6,4},{7,5},{12,6},{13,7},{10,8},{11,9},{1... | collective-permute-start | bytes 196616 | tf_op jit(solution)/shard_map/ppermute | solution.py:341
  21.4 1.2 %collective-permute-start.13 = (bf16[256,128]{1,0:T(8,128)(2,1)S(1)}, bf16[256,128]{1,0:T(8,128)(2,1)S(1)}, u32[]{:S(2)}, u32[]{:S(2)}) collective-permute-start(bf16[256,128]{1,0:T(8,128)(2,1)S(1)} %get-tuple-element.71), channel_id=1, source_target_pairs={{4,0},{5,1},{6,2},{7,3},{8,4},{9,5},{10,6},{11,7},{12,8},{13,9},{1... | collective-permute-start | bytes 196616 | tf_op jit(solution)/shard_map/ppermute | solution.py:341
  22.6 1.5 %collective-permute-done.9.far_ref = bf16[512,128]{1,0:T(8,128)(2,1)S(1)} collective-permute-done((bf16[512,128]{1,0:T(8,128)(2,1)S(1)}, bf16[512,128]{1,0:T(8,128)(2,1)S(1)}, u32[]{:S(2)}, u32[]{:S(2)}) %collective-permute-start.9) | collective-permute-done | bytes 131104 | tf_op jit(solution)/shard_map/ppermute | solution.py:346
  24.1 0.1 collective-permute-start.10
  24.2 1.6 %query_side.1 = (bf16[128,1024]{1,0:T(8,128)(2,1)}, bf16[128,1024]{1,0:T(8,128)(2,1)}) custom-call(bf16[512,1024]{1,0:T(8,128)(2,1)S(1)} %get-tuple-element.53.refs_0_, bf16[512,1024]{1,0:T(8,128)(2,1)S(1)} %get-tuple-element.54.refs_1_, bf16[512,1024]{1,0:T(8,128)(2,1)S(1)} %get-tuple-element.62.refs_2_, bf16[512,1024]{1,0:T(8,128)(2,1)S(1)} %get-tuple-element.63.refs_3_, ...), custom_call_target="tpu_custom_call" | custom-call | flops 536870912 | bytes 4194304 | tf_op jit(solution)/shard_map/query_side/pallas_call | solution.py:447
  25.8 0.1 collective-permute-done.13.refs_1_
  25.9 0.7 %total_grads.1 = (bf16[128,128]{1,0:T(8,128)(2,1)}, bf16[128,128]{1,0:T(8,128)(2,1)}) custom-call(f32[4,256,128]{2,1,0:T(8,128)S(1)} %get-tuple-element.66.mine_ref, bf16[2,256,128]{2,1,0:T(8,128)(2,1)S(1)} %collective-permute-done.8.from_sib_ref, bf16[512,128]{1,0:T(8,128)(2,1)S(1)} %collective-permute-done.9.far_ref, ...), custom_call_target="tpu_custom_call" | custom-call | tf_op jit(solution)/shard_map/total_grads/pallas_call | solution.py:497
  (15 shorter events, 0.2 us)
Async XLA Ops:
  1.4 7.1 %collective-permute-start = (bf16[256,128]{1,0:T(8,128)(2,1)S(1)}, bf16[256,128]{1,0:T(8,128)(2,1)S(1)}, u32[]{:S(2)}, u32[]{:S(2)}) collective-permute-start(bf16[256,128]{1,0:T(8,128)(2,1)S(1)} %pair_up.1.own_ref.refs_7_), channel_id=1, source_target_pairs={{0,1},{1,0},{2,3},{3,2},{4,5},{5,4},{6,7},{7,6},{8,9},{9,8},{10,11... | collective-permute-start | bytes 196616 | tf_op jit(solution)/shard_map/ppermute | solution.py:354
  1.9 9.7 %collective-permute-start.4 = (bf16[256,128]{1,0:T(8,128)(2,1)S(1)}, bf16[256,128]{1,0:T(8,128)(2,1)S(1)}, u32[]{:S(2)}, u32[]{:S(2)}) collective-permute-start(bf16[256,128]{1,0:T(8,128)(2,1)S(1)} %pair_up.1.own_ref.refs_7_), channel_id=1, source_target_pairs={{0,4},{1,5},{2,6},{3,7},{4,8},{5,9},{6,10},{7,11},{8,12},{9,13},{1... | collective-permute-start | bytes 196616 | tf_op jit(solution)/shard_map/ppermute | solution.py:341
  4.5 7.1 %collective-permute-start.3 = (bf16[256,128]{1,0:T(8,128)(2,1)S(1)}, bf16[256,128]{1,0:T(8,128)(2,1)S(1)}, u32[]{:S(2)}, u32[]{:S(2)}) collective-permute-start(bf16[256,128]{1,0:T(8,128)(2,1)S(1)} %pair_up.1.own_ref.refs_7_), channel_id=1, source_target_pairs={{0,2},{1,3},{2,8},{3,9},{4,6},{5,7},{6,12},{7,13},{8,10},{9,11},{1... | collective-permute-start | bytes 196616 | tf_op jit(solution)/shard_map/ppermute | solution.py:341
  6.0 7.5 %collective-permute-start.2 = (bf16[256,128]{1,0:T(8,128)(2,1)S(1)}, bf16[256,128]{1,0:T(8,128)(2,1)S(1)}, u32[]{:S(2)}, u32[]{:S(2)}) collective-permute-start(bf16[256,128]{1,0:T(8,128)(2,1)S(1)} %pair_up.1.own_ref.refs_7_), channel_id=1, source_target_pairs={{0,6},{1,7},{2,4},{3,5},{4,10},{5,11},{6,8},{7,9},{8,14},{9,15},{1... | collective-permute-start | bytes 196616 | tf_op jit(solution)/shard_map/ppermute | solution.py:341
  8.5 5.0 %collective-permute-start.1 = (bf16[256,128]{1,0:T(8,128)(2,1)S(1)}, bf16[256,128]{1,0:T(8,128)(2,1)S(1)}, u32[]{:S(2)}, u32[]{:S(2)}) collective-permute-start(bf16[256,128]{1,0:T(8,128)(2,1)S(1)} %collective-permute-done.refs_8_.refs_12_), channel_id=1, source_target_pairs={{0,8},{2,10},{4,12},{6,14},{8,16},{10,18},{12,20},{14,22},{16,24},... | collective-permute-start | bytes 196616 | tf_op jit(solution)/shard_map/ppermute | solution.py:351
  11.7 1.9 %collective-permute-start.5 = (bf16[256,128]{1,0:T(8,128)(2,1)S(1)}, bf16[256,128]{1,0:T(8,128)(2,1)S(1)}, u32[]{:S(2)}, u32[]{:S(2)}) collective-permute-start(bf16[256,128]{1,0:T(8,128)(2,1)S(1)} %collective-permute-done.3.refs_4_.refs_8_), channel_id=1, source_target_pairs={{0,1},{1,0},{2,3},{3,2},{4,5},{5,4},{6,7},{7,6},{8,9},{9,8},{10,11... | collective-permute-start | bytes 196616 | tf_op jit(solution)/shard_map/ppermute | solution.py:354
  11.8 1.8 %collective-permute-start.6 = (bf16[256,128]{1,0:T(8,128)(2,1)S(1)}, bf16[256,128]{1,0:T(8,128)(2,1)S(1)}, u32[]{:S(2)}, u32[]{:S(2)}) collective-permute-start(bf16[256,128]{1,0:T(8,128)(2,1)S(1)} %collective-permute-done.4.refs_5_.refs_9_), channel_id=1, source_target_pairs={{0,1},{1,0},{2,3},{3,2},{4,5},{5,4},{6,7},{7,6},{8,9},{9,8},{10,11... | collective-permute-start | bytes 196616 | tf_op jit(solution)/shard_map/ppermute | solution.py:354
  13.5 1.3 %collective-permute-start.7 = (bf16[256,128]{1,0:T(8,128)(2,1)S(1)}, bf16[256,128]{1,0:T(8,128)(2,1)S(1)}, u32[]{:S(2)}, u32[]{:S(2)}) collective-permute-start(bf16[256,128]{1,0:T(8,128)(2,1)S(1)} %collective-permute-done.2.refs_6_), channel_id=1, source_target_pairs={{0,1},{1,0},{2,3},{3,2},{4,5},{5,4},{6,7},{7,6},{8,9},{9,8},{10,11... | collective-permute-start | bytes 196616 | tf_op jit(solution)/shard_map/ppermute | solution.py:354
  16.2 1.4 %collective-permute-start.8 = (bf16[2,256,128]{2,1,0:T(8,128)(2,1)S(1)}, bf16[2,256,128]{2,1,0:T(8,128)(2,1)S(1)}, u32[]{:S(2)}, u32[]{:S(2)}) collective-permute-start(bf16[2,256,128]{2,1,0:T(8,128)(2,1)S(1)} %get-tuple-element.67), channel_id=1, source_target_pairs={{0,1},{1,0},{2,3},{3,2},{4,5},{5,4},{6,7},{7,6},{8,9},{9,8},{10,11... | collective-permute-start | bytes 393224 | tf_op jit(solution)/shard_map/ppermute | solution.py:354
  16.5 3.4 %collective-permute-start.11 = (bf16[2,256,128]{2,1,0:T(8,128)(2,1)S(1)}, bf16[2,256,128]{2,1,0:T(8,128)(2,1)S(1)}, u32[]{:S(2)}, u32[]{:S(2)}) collective-permute-start(bf16[2,256,128]{2,1,0:T(8,128)(2,1)S(1)} %get-tuple-element.69), channel_id=1, source_target_pairs={{0,1},{1,0},{2,3},{3,2},{4,5},{5,4},{6,7},{7,6},{8,9},{9,8},{10,11... | collective-permute-start | bytes 393224 | tf_op jit(solution)/shard_map/ppermute | solution.py:354
  17.7 6.4 %collective-permute-start.9 = (bf16[512,128]{1,0:T(8,128)(2,1)S(1)}, bf16[512,128]{1,0:T(8,128)(2,1)S(1)}, u32[]{:S(2)}, u32[]{:S(2)}) collective-permute-start(bf16[512,128]{1,0:T(8,128)(2,1)S(1)} %merge_far.1), channel_id=1, source_target_pairs={{7,1},{5,3},{11,5},{9,7},{15,9},{13,11},{19,13},{17,15},{23,17},{2... | collective-permute-start | bytes 393224 | tf_op jit(solution)/shard_map/ppermute | solution.py:346
  20.0 5.8 %collective-permute-start.12 = (bf16[256,128]{1,0:T(8,128)(2,1)S(1)}, bf16[256,128]{1,0:T(8,128)(2,1)S(1)}, u32[]{:S(2)}, u32[]{:S(2)}) collective-permute-start(bf16[256,128]{1,0:T(8,128)(2,1)S(1)} %get-tuple-element.70), channel_id=1, source_target_pairs={{2,0},{3,1},{8,2},{9,3},{6,4},{7,5},{12,6},{13,7},{10,8},{11,9},{1... | collective-permute-start | bytes 196616 | tf_op jit(solution)/shard_map/ppermute | solution.py:341
  21.4 4.5 %collective-permute-start.13 = (bf16[256,128]{1,0:T(8,128)(2,1)S(1)}, bf16[256,128]{1,0:T(8,128)(2,1)S(1)}, u32[]{:S(2)}, u32[]{:S(2)}) collective-permute-start(bf16[256,128]{1,0:T(8,128)(2,1)S(1)} %get-tuple-element.71), channel_id=1, source_target_pairs={{4,0},{5,1},{6,2},{7,3},{8,4},{9,5},{10,6},{11,7},{12,8},{13,9},{1... | collective-permute-start | bytes 196616 | tf_op jit(solution)/shard_map/ppermute | solution.py:341
  24.1 1.8 %collective-permute-start.10 = (bf16[256,128]{1,0:T(8,128)(2,1)S(1)}, bf16[256,128]{1,0:T(8,128)(2,1)S(1)}, u32[]{:S(2)}, u32[]{:S(2)}) collective-permute-start(bf16[256,128]{1,0:T(8,128)(2,1)S(1)} %pass_on.1), channel_id=1, source_target_pairs={{0,1},{1,0},{2,3},{3,2},{4,5},{5,4},{6,7},{7,6},{8,9},{9,8},{10,11... | collective-permute-start | bytes 196616 | tf_op jit(solution)/shard_map/ppermute | solution.py:354

commit v10 on v8

--- a/solution.py
+++ b/solution.py
@@ -295,8 +295,8 @@
     out_ref[...] = jnp.where(core == 1, far_ref[2 * BLOCK :, :], far_ref[: 2 * BLOCK, :])
 
 
-def total_kernel(mine_ref, from_sib_ref, far_ref, passed_ref, *refs):
-    back, (key_ref, value_ref) = refs[:-2], refs[-2:]
+def total_kernel(mine_ref, from_sib_ref, far_ref, *refs):
+    back, passed_ref, (key_ref, value_ref) = refs[:-3], refs[-3], refs[-2:]
     _, _, core = position()
     total = mine_ref[0] + jnp.where(core == 0, from_sib_ref[0], far_ref[: 2 * BLOCK, :]).astype(jnp.float32)
     total = total + passed_ref[...].astype(jnp.float32)
@@ -501,7 +501,7 @@
         out_specs=[VMEM] * 2,
         compiler_params=small,
         name="total_grads",
-    )(mine, far_from_sib, back_far, passed, *back)
+    )(mine, far_from_sib, back_far, *back, passed)
     return attended, query_grad, key_grad, value_grad
 
 

time: 26.8 us -> 26.8 us (level)
  no operation moved by 1% of the time
where the time goes in v10:
time: 26.8 us; the launch traced here: 26.6 us
  starting transfers between devices  13.8 us (51%)
  Pallas kernels  8.27 us (31%)
  waiting for transfers between devices  3.73 us (14%)
  between operations  0.74 us (3%)
    ppermute x5, starting transfers between devices, ahead(): lax.ppermute(block, AXES, [pair[::-1] for pair in route] if back else route)  9.45 us
    ppermute x1, starting transfers between devices, back_mixed(): return lax.ppermute(block, AXES, route)  2.7 us
    ppermute x5, waiting for transfers between devices, ahead(): lax.ppermute(block, AXES, [pair[::-1] for pair in route] if back else route)  2.11 us
    ppermute x8, starting transfers between devices, swapped(): return lax.ppermute(block, AXES, [(i, i ^ 1) for i in range(devices)])  1.67 us
    pallas_call x1, Pallas kernels, local(): pl.pallas_call(functools.partial(query_side_kernel, slots), out_shape=[sh...  1.57 us
    pallas_call x1, Pallas kernels, local(): pl.pallas_call(functools.partial(own_kernel, slots), out_shape=[pltpu.VME...  1.54 us
    pallas_call x1, Pallas kernels, local(): pl.pallas_call(functools.partial(late_kernel, slots), out_shape=stage(1)...  1.46 us
    pallas_call x2, Pallas kernels, next_stage(): pl.pallas_call(functools.partial(stage_kernel, first, len(group)), out_sh...  1.38 us
  transfers between devices with their start and end apart: 15, of which 5 were waited for; matrix products, arithmetic and copies ran while one was open for 0% of the time, Pallas kernels for 20%

profile of v10, /device:TPU:0, one launch (start us, length us, event | category | flops | bytes accessed | tf_op | source)
XLA Modules:
  0.0 26.6 jit_solution(11279467861110773287)
XLA Ops:
  0.6 0.8 %pair_up.1.own_ref.refs_7_ = bf16[256,128]{1,0:T(8,128)(2,1)S(1)} custom-call(bf16[128,128]{1,0:T(8,128)(2,1)} %key_ref.1, bf16[128,128]{1,0:T(8,128)(2,1)} %value_ref.1), custom_call_target="tpu_custom_call" | custom-call | tf_op jit(solution)/shard_map/pair_up/pallas_call | solution.py:356
  1.4 3.0 %collective-permute-start.3 = (bf16[256,128]{1,0:T(8,128)(2,1)S(1)}, bf16[256,128]{1,0:T(8,128)(2,1)S(1)}, u32[]{:S(2)}, u32[]{:S(2)}) collective-permute-start(bf16[256,128]{1,0:T(8,128)(2,1)S(1)} %pair_up.1.own_ref.refs_7_), channel_id=1, source_target_pairs={{0,4},{1,5},{2,6},{3,7},{4,8},{5,9},{6,10},{7,11},{8,12},{9,13},{1... | collective-permute-start | bytes 196616 | tf_op jit(solution)/shard_map/ppermute | solution.py:341
  4.5 1.5 %collective-permute-start.2 = (bf16[256,128]{1,0:T(8,128)(2,1)S(1)}, bf16[256,128]{1,0:T(8,128)(2,1)S(1)}, u32[]{:S(2)}, u32[]{:S(2)}) collective-permute-start(bf16[256,128]{1,0:T(8,128)(2,1)S(1)} %pair_up.1.own_ref.refs_7_), channel_id=1, source_target_pairs={{0,2},{1,3},{2,8},{3,9},{4,6},{5,7},{6,12},{7,13},{8,10},{9,11},{1... | collective-permute-start | bytes 196616 | tf_op jit(solution)/shard_map/ppermute | solution.py:341
  5.9 2.5 %collective-permute-start.1 = (bf16[256,128]{1,0:T(8,128)(2,1)S(1)}, bf16[256,128]{1,0:T(8,128)(2,1)S(1)}, u32[]{:S(2)}, u32[]{:S(2)}) collective-permute-start(bf16[256,128]{1,0:T(8,128)(2,1)S(1)} %pair_up.1.own_ref.refs_7_), channel_id=1, source_target_pairs={{0,6},{1,7},{2,4},{3,5},{4,10},{5,11},{6,8},{7,9},{8,14},{9,15},{1... | collective-permute-start | bytes 196616 | tf_op jit(solution)/shard_map/ppermute | solution.py:341
  8.4 1.5 %own_scores.1 = (bf16[1024,128]{1,0:T(8,128)(2,1)S(1)}, bf16[1024,128]{1,0:T(8,128)(2,1)S(1)}, f32[8,1024]{1,0:T(8,128)S(1)}, f32[128,1024]{1,0:T(8,128)S(1)}, f...) custom-call(s32[32]{0:T(128)} %doc_hbm.1, bf16[128,1024]{1,0:T(8,128)(2,1)} %query_ref.1, bf16[128,1024]{1,0:T(8,128)(2,1)} %grad_ref.1, ...), custom_call_target="tpu_custom_call" | custom-call | flops 67108864 | bytes 524288 | tf_op jit(solution)/shard_map/own_scores/pallas_call | solution.py:375
  10.0 1.5 %collective-permute-done.2.refs_4_.refs_8_ = bf16[256,128]{1,0:T(8,128)(2,1)S(1)} collective-permute-done((bf16[256,128]{1,0:T(8,128)(2,1)S(1)}, bf16[256,128]{1,0:T(8,128)(2,1)S(1)}, u32[]{:S(2)}, u32[]{:S(2)}) %collective-permute-start.2) | collective-permute-done | bytes 65568 | tf_op jit(solution)/shard_map/ppermute | solution.py:341
  11.5 0.5 %collective-permute-start.5 = (bf16[256,128]{1,0:T(8,128)(2,1)S(1)}, bf16[256,128]{1,0:T(8,128)(2,1)S(1)}, u32[]{:S(2)}, u32[]{:S(2)}) collective-permute-start(bf16[256,128]{1,0:T(8,128)(2,1)S(1)} %collective-permute-done.3.refs_5_.refs_9_), channel_id=1, source_target_pairs={{0,1},{1,0},{2,3},{3,2},{4,5},{5,4},{6,7},{7,6},{8,9},{9,8},{10,11... | collective-permute-start | bytes 196616 | tf_op jit(solution)/shard_map/ppermute | solution.py:354
  12.0 0.6 %stage_scores.2 = (f32[256,1024]{1,0:T(8,128)S(1)}, f32[256,1024]{1,0:T(8,128)S(1)}, f32[8,1024]{1,0:T(8,128)S(1)}) custom-call(f32[8,1024]{1,0:T(8,128)S(1)} %get-tuple-element.39.refs_0_, bf16[1024,128]{1,0:T(8,128)(2,1)S(1)} %get-tuple-element.40.refs_1_.refs_0_, bf16[1024,128]{1,0:T(8,128)(2,1)S(1)} %get-tuple-element.41.refs_2_.refs_1_, ...), custom_call_target="tpu_custom_call" | custom-call | flops 134217728 | bytes 1048576 | tf_op jit(solution)/shard_map/stage_scores/pallas_call | solution.py:398
  12.6 0.3 %collective-permute-done.1.refs_6_ = bf16[256,128]{1,0:T(8,128)(2,1)S(1)} collective-permute-done((bf16[256,128]{1,0:T(8,128)(2,1)S(1)}, bf16[256,128]{1,0:T(8,128)(2,1)S(1)}, u32[]{:S(2)}, u32[]{:S(2)}) %collective-permute-start.1) | collective-permute-done | bytes 65568 | tf_op jit(solution)/shard_map/ppermute | solution.py:341
  12.9 0.3 %collective-permute-start.7 = (bf16[256,128]{1,0:T(8,128)(2,1)S(1)}, bf16[256,128]{1,0:T(8,128)(2,1)S(1)}, u32[]{:S(2)}, u32[]{:S(2)}) collective-permute-start(bf16[256,128]{1,0:T(8,128)(2,1)S(1)} %collective-permute-done), channel_id=1, source_target_pairs={{0,1},{1,0},{2,3},{3,2},{4,5},{5,4},{6,7},{7,6},{8,9},{9,8},{10,11... | collective-permute-start | bytes 196616 | tf_op jit(solution)/shard_map/ppermute | solution.py:354
  13.2 0.2 collective-permute-start.6
  13.4 0.8 %stage_scores.3 = (f32[384,1024]{1,0:T(8,128)S(1)}, f32[384,1024]{1,0:T(8,128)S(1)}, f32[8,1024]{1,0:T(8,128)S(1)}) custom-call(f32[8,1024]{1,0:T(8,128)S(1)} %get-tuple-element.39.refs_0_, bf16[1024,128]{1,0:T(8,128)(2,1)S(1)} %get-tuple-element.40.refs_1_.refs_0_, bf16[1024,128]{1,0:T(8,128)(2,1)S(1)} %get-tuple-element.41.refs_2_.refs_1_, ...), custom_call_target="tpu_custom_call" | custom-call | flops 201326592 | bytes 1572864 | tf_op jit(solution)/shard_map/stage_scores/pallas_call | solution.py:398
  14.3 0.2 collective-permute-done.6.refs_6_.refs_10_
  14.5 1.5 %late_scores.1 = (f32[128,1024]{1,0:T(8,128)S(1)}, f32[128,1024]{1,0:T(8,128)S(1)}, f32[8,1024]{1,0:T(8,128)S(1)}, bf16[512,1024]{1,0:T(8,128)(2,1)S(1)}, bf16[5...) custom-call(f32[8,1024]{1,0:T(8,128)S(1)} %get-tuple-element.39.refs, ...), custom_call_target="tpu_custom_call" | custom-call | flops 536870912 | bytes 4194304 | tf_op jit(solution)/shard_map/late_scores/pallas_call | solution.py:422
  15.9 0.3 %collective-permute-start.9 = (bf16[2,256,128]{2,1,0:T(8,128)(2,1)S(1)}, bf16[2,256,128]{2,1,0:T(8,128)(2,1)S(1)}, u32[]{:S(2)}, u32[]{:S(2)}) collective-permute-start(bf16[2,256,128]{2,1,0:T(8,128)(2,1)S(1)} %get-tuple-element.67), channel_id=1, source_target_pairs={{0,1},{1,0},{2,3},{3,2},{4,5},{5,4},{6,7},{7,6},{8,9},{9,8},{10,11... | collective-permute-start | bytes 393224 | tf_op jit(solution)/shard_map/ppermute | solution.py:354
  16.2 0.3 %collective-permute-start.11 = (bf16[2,256,128]{2,1,0:T(8,128)(2,1)S(1)}, bf16[2,256,128]{2,1,0:T(8,128)(2,1)S(1)}, u32[]{:S(2)}, u32[]{:S(2)}) collective-permute-start(bf16[2,256,128]{2,1,0:T(8,128)(2,1)S(1)} %get-tuple-element.69), channel_id=1, source_target_pairs={{0,1},{1,0},{2,3},{3,2},{4,5},{5,4},{6,7},{7,6},{8,9},{9,8},{10,11... | collective-permute-start | bytes 393224 | tf_op jit(solution)/shard_map/ppermute | solution.py:354
  16.5 0.8 %other_grads.1 = (bf16[512,1024]{1,0:T(8,128)(2,1)S(1)}, bf16[512,1024]{1,0:T(8,128)(2,1)S(1)}, f32[4,256,128]{2,1,0:T(8,128)S(1)}) custom-call(bf16[1024,128]{1,0:T(8,128)(2,1)S(1)} %get-tuple-element.40.refs_1_.refs_0_, bf16[1024,128]{1,0:T(8,128)(2,1)S(1)} %get-tuple-element.41.refs_2_.refs_1_, f32[8,1024]{1,0:T(8,128)S(1)} %get-tuple-element.55.refs_2_, ...), custom_call_target="tpu_custom_call" | custom-call | flops 268435456 | bytes 2097152 | tf_op jit(solution)/shard_map/other_grads/pallas_call | solution.py:437
  17.4 2.7 %collective-permute-start.10 = (bf16[512,128]{1,0:T(8,128)(2,1)S(1)}, bf16[512,128]{1,0:T(8,128)(2,1)S(1)}, u32[]{:S(2)}, u32[]{:S(2)}) collective-permute-start(bf16[512,128]{1,0:T(8,128)(2,1)S(1)} %merge_far.1), channel_id=1, source_target_pairs={{7,1},{5,3},{11,5},{9,7},{15,9},{13,11},{19,13},{17,15},{23,17},{2... | collective-permute-start | bytes 393224 | tf_op jit(solution)/shard_map/ppermute | solution.py:346
  20.1 1.4 %collective-permute-start.12 = (bf16[256,128]{1,0:T(8,128)(2,1)S(1)}, bf16[256,128]{1,0:T(8,128)(2,1)S(1)}, u32[]{:S(2)}, u32[]{:S(2)}) collective-permute-start(bf16[256,128]{1,0:T(8,128)(2,1)S(1)} %get-tuple-element.70), channel_id=1, source_target_pairs={{4,0},{5,1},{6,2},{7,3},{8,4},{9,5},{10,6},{11,7},{12,8},{13,9},{1... | collective-permute-start | bytes 196616 | tf_op jit(solution)/shard_map/ppermute | solution.py:341
  21.6 1.0 %collective-permute-start.13 = (bf16[256,128]{1,0:T(8,128)(2,1)S(1)}, bf16[256,128]{1,0:T(8,128)(2,1)S(1)}, u32[]{:S(2)}, u32[]{:S(2)}) collective-permute-start(bf16[256,128]{1,0:T(8,128)(2,1)S(1)} %get-tuple-element.71), channel_id=1, source_target_pairs={{2,0},{3,1},{8,2},{9,3},{6,4},{7,5},{12,6},{13,7},{10,8},{11,9},{1... | collective-permute-start | bytes 196616 | tf_op jit(solution)/shard_map/ppermute | solution.py:341
  22.6 1.3 %collective-permute-done.10.far_ref = bf16[512,128]{1,0:T(8,128)(2,1)S(1)} collective-permute-done((bf16[512,128]{1,0:T(8,128)(2,1)S(1)}, bf16[512,128]{1,0:T(8,128)(2,1)S(1)}, u32[]{:S(2)}, u32[]{:S(2)}) %collective-permute-start.10) | collective-permute-done | bytes 131104 | tf_op jit(solution)/shard_map/ppermute | solution.py:346
  24.0 1.6 %query_side.1 = (bf16[128,1024]{1,0:T(8,128)(2,1)}, bf16[128,1024]{1,0:T(8,128)(2,1)}) custom-call(bf16[512,1024]{1,0:T(8,128)(2,1)S(1)} %get-tuple-element.53.refs_0_, bf16[512,1024]{1,0:T(8,128)(2,1)S(1)} %get-tuple-element.54.refs_1_, bf16[512,1024]{1,0:T(8,128)(2,1)S(1)} %get-tuple-element.62.refs_2_, bf16[512,1024]{1,0:T(8,128)(2,1)S(1)} %get-tuple-element.63.refs_3_, ...), custom_call_target="tpu_custom_call" | custom-call | flops 536870912 | bytes 4194304 | tf_op jit(solution)/shard_map/query_side/pallas_call | solution.py:447
  25.6 0.3 %collective-permute-done.13.refs_1_ = bf16[256,128]{1,0:T(8,128)(2,1)S(1)} collective-permute-done((bf16[256,128]{1,0:T(8,128)(2,1)S(1)}, bf16[256,128]{1,0:T(8,128)(2,1)S(1)}, u32[]{:S(2)}, u32[]{:S(2)}) %collective-permute-start.13) | collective-permute-done | bytes 65568 | tf_op jit(solution)/shard_map/ppermute | solution.py:341
  25.9 0.7 %total_grads.1 = (bf16[128,128]{1,0:T(8,128)(2,1)}, bf16[128,128]{1,0:T(8,128)(2,1)}) custom-call(f32[4,256,128]{2,1,0:T(8,128)S(1)} %get-tuple-element.66.mine_ref, bf16[2,256,128]{2,1,0:T(8,128)(2,1)S(1)} %collective-permute-done.9.from_sib_ref, bf16[512,128]{1,0:T(8,128)(2,1)S(1)} %collective-permute-done.10.far_ref, ...), custom_call_target="tpu_custom_call" | custom-call | tf_op jit(solution)/shard_map/total_grads/pallas_call | solution.py:497
  (17 shorter events, 0.2 us)
Async XLA Ops:
  1.4 8.6 %collective-permute-start.3 = (bf16[256,128]{1,0:T(8,128)(2,1)S(1)}, bf16[256,128]{1,0:T(8,128)(2,1)S(1)}, u32[]{:S(2)}, u32[]{:S(2)}) collective-permute-start(bf16[256,128]{1,0:T(8,128)(2,1)S(1)} %pair_up.1.own_ref.refs_7_), channel_id=1, source_target_pairs={{0,4},{1,5},{2,6},{3,7},{4,8},{5,9},{6,10},{7,11},{8,12},{9,13},{1... | collective-permute-start | bytes 196616 | tf_op jit(solution)/shard_map/ppermute | solution.py:341
  4.5 7.1 %collective-permute-start.2 = (bf16[256,128]{1,0:T(8,128)(2,1)S(1)}, bf16[256,128]{1,0:T(8,128)(2,1)S(1)}, u32[]{:S(2)}, u32[]{:S(2)}) collective-permute-start(bf16[256,128]{1,0:T(8,128)(2,1)S(1)} %pair_up.1.own_ref.refs_7_), channel_id=1, source_target_pairs={{0,2},{1,3},{2,8},{3,9},{4,6},{5,7},{6,12},{7,13},{8,10},{9,11},{1... | collective-permute-start | bytes 196616 | tf_op jit(solution)/shard_map/ppermute | solution.py:341
  5.9 7.0 %collective-permute-start.1 = (bf16[256,128]{1,0:T(8,128)(2,1)S(1)}, bf16[256,128]{1,0:T(8,128)(2,1)S(1)}, u32[]{:S(2)}, u32[]{:S(2)}) collective-permute-start(bf16[256,128]{1,0:T(8,128)(2,1)S(1)} %pair_up.1.own_ref.refs_7_), channel_id=1, source_target_pairs={{0,6},{1,7},{2,4},{3,5},{4,10},{5,11},{6,8},{7,9},{8,14},{9,15},{1... | collective-permute-start | bytes 196616 | tf_op jit(solution)/shard_map/ppermute | solution.py:341
  8.4 4.5 %collective-permute-start = (bf16[256,128]{1,0:T(8,128)(2,1)S(1)}, bf16[256,128]{1,0:T(8,128)(2,1)S(1)}, u32[]{:S(2)}, u32[]{:S(2)}) collective-permute-start(bf16[256,128]{1,0:T(8,128)(2,1)S(1)} %pair_up.1.own_ref.refs_7_), channel_id=1, source_target_pairs={{1,9},{3,11},{5,13},{7,15},{9,17},{11,19},{13,21},{15,23},{17,25},... | collective-permute-start | bytes 196616 | tf_op jit(solution)/shard_map/ppermute | solution.py:351
  11.5 1.9 %collective-permute-start.4 = (bf16[256,128]{1,0:T(8,128)(2,1)S(1)}, bf16[256,128]{1,0:T(8,128)(2,1)S(1)}, u32[]{:S(2)}, u32[]{:S(2)}) collective-permute-start(bf16[256,128]{1,0:T(8,128)(2,1)S(1)} %collective-permute-done.2.refs_4_.refs_8_), channel_id=1, source_target_pairs={{0,1},{1,0},{2,3},{3,2},{4,5},{5,4},{6,7},{7,6},{8,9},{9,8},{10,11... | collective-permute-start | bytes 196616 | tf_op jit(solution)/shard_map/ppermute | solution.py:354
  11.5 1.9 %collective-permute-start.5 = (bf16[256,128]{1,0:T(8,128)(2,1)S(1)}, bf16[256,128]{1,0:T(8,128)(2,1)S(1)}, u32[]{:S(2)}, u32[]{:S(2)}) collective-permute-start(bf16[256,128]{1,0:T(8,128)(2,1)S(1)} %collective-permute-done.3.refs_5_.refs_9_), channel_id=1, source_target_pairs={{0,1},{1,0},{2,3},{3,2},{4,5},{5,4},{6,7},{7,6},{8,9},{9,8},{10,11... | collective-permute-start | bytes 196616 | tf_op jit(solution)/shard_map/ppermute | solution.py:354
  12.0 2.2 %collective-permute-start.8 = (bf16[256,128]{1,0:T(8,128)(2,1)S(1)}, bf16[256,128]{1,0:T(8,128)(2,1)S(1)}, u32[]{:S(2)}, u32[]{:S(2)}) collective-permute-start(bf16[256,128]{1,0:T(8,128)(2,1)S(1)} %pair_up.1.own_ref.refs_7_), channel_id=1, source_target_pairs={{0,1},{1,0},{2,3},{3,2},{4,5},{5,4},{6,7},{7,6},{8,9},{9,8},{10,11... | collective-permute-start | bytes 196616 | tf_op jit(solution)/shard_map/ppermute | solution.py:354
  12.9 1.3 %collective-permute-start.7 = (bf16[256,128]{1,0:T(8,128)(2,1)S(1)}, bf16[256,128]{1,0:T(8,128)(2,1)S(1)}, u32[]{:S(2)}, u32[]{:S(2)}) collective-permute-start(bf16[256,128]{1,0:T(8,128)(2,1)S(1)} %collective-permute-done), channel_id=1, source_target_pairs={{0,1},{1,0},{2,3},{3,2},{4,5},{5,4},{6,7},{7,6},{8,9},{9,8},{10,11... | collective-permute-start | bytes 196616 | tf_op jit(solution)/shard_map/ppermute | solution.py:354
  13.2 1.3 %collective-permute-start.6 = (bf16[256,128]{1,0:T(8,128)(2,1)S(1)}, bf16[256,128]{1,0:T(8,128)(2,1)S(1)}, u32[]{:S(2)}, u32[]{:S(2)}) collective-permute-start(bf16[256,128]{1,0:T(8,128)(2,1)S(1)} %collective-permute-done.1.refs_6_), channel_id=1, source_target_pairs={{0,1},{1,0},{2,3},{3,2},{4,5},{5,4},{6,7},{7,6},{8,9},{9,8},{10,11... | collective-permute-start | bytes 196616 | tf_op jit(solution)/shard_map/ppermute | solution.py:354
  15.9 1.4 %collective-permute-start.9 = (bf16[2,256,128]{2,1,0:T(8,128)(2,1)S(1)}, bf16[2,256,128]{2,1,0:T(8,128)(2,1)S(1)}, u32[]{:S(2)}, u32[]{:S(2)}) collective-permute-start(bf16[2,256,128]{2,1,0:T(8,128)(2,1)S(1)} %get-tuple-element.67), channel_id=1, source_target_pairs={{0,1},{1,0},{2,3},{3,2},{4,5},{5,4},{6,7},{7,6},{8,9},{9,8},{10,11... | collective-permute-start | bytes 393224 | tf_op jit(solution)/shard_map/ppermute | solution.py:354
  16.2 3.9 %collective-permute-start.11 = (bf16[2,256,128]{2,1,0:T(8,128)(2,1)S(1)}, bf16[2,256,128]{2,1,0:T(8,128)(2,1)S(1)}, u32[]{:S(2)}, u32[]{:S(2)}) collective-permute-start(bf16[2,256,128]{2,1,0:T(8,128)(2,1)S(1)} %get-tuple-element.69), channel_id=1, source_target_pairs={{0,1},{1,0},{2,3},{3,2},{4,5},{5,4},{6,7},{7,6},{8,9},{9,8},{10,11... | collective-permute-start | bytes 393224 | tf_op jit(solution)/shard_map/ppermute | solution.py:354
  17.4 6.5 %collective-permute-start.10 = (bf16[512,128]{1,0:T(8,128)(2,1)S(1)}, bf16[512,128]{1,0:T(8,128)(2,1)S(1)}, u32[]{:S(2)}, u32[]{:S(2)}) collective-permute-start(bf16[512,128]{1,0:T(8,128)(2,1)S(1)} %merge_far.1), channel_id=1, source_target_pairs={{7,1},{5,3},{11,5},{9,7},{15,9},{13,11},{19,13},{17,15},{23,17},{2... | collective-permute-start | bytes 393224 | tf_op jit(solution)/shard_map/ppermute | solution.py:346
  20.1 5.5 %collective-permute-start.12 = (bf16[256,128]{1,0:T(8,128)(2,1)S(1)}, bf16[256,128]{1,0:T(8,128)(2,1)S(1)}, u32[]{:S(2)}, u32[]{:S(2)}) collective-permute-start(bf16[256,128]{1,0:T(8,128)(2,1)S(1)} %get-tuple-element.70), channel_id=1, source_target_pairs={{4,0},{5,1},{6,2},{7,3},{8,4},{9,5},{10,6},{11,7},{12,8},{13,9},{1... | collective-permute-start | bytes 196616 | tf_op jit(solution)/shard_map/ppermute | solution.py:341
  21.6 4.4 %collective-permute-start.13 = (bf16[256,128]{1,0:T(8,128)(2,1)S(1)}, bf16[256,128]{1,0:T(8,128)(2,1)S(1)}, u32[]{:S(2)}, u32[]{:S(2)}) collective-permute-start(bf16[256,128]{1,0:T(8,128)(2,1)S(1)} %get-tuple-element.71), channel_id=1, source_target_pairs={{2,0},{3,1},{8,2},{9,3},{6,4},{7,5},{12,6},{13,7},{10,8},{11,9},{1... | collective-permute-start | bytes 196616 | tf_op jit(solution)/shard_map/ppermute | solution.py:341
  23.9 2.0 %collective-permute-start.14 = (bf16[256,128]{1,0:T(8,128)(2,1)S(1)}, bf16[256,128]{1,0:T(8,128)(2,1)S(1)}, u32[]{:S(2)}, u32[]{:S(2)}) collective-permute-start(bf16[256,128]{1,0:T(8,128)(2,1)S(1)} %pass_on.1), channel_id=1, source_target_pairs={{0,1},{1,0},{2,3},{3,2},{4,5},{5,4},{6,7},{7,6},{8,9},{9,8},{10,11... | collective-permute-start | bytes 196616 | tf_op jit(solution)/shard_map/ppermute | solution.py:354
